TPU v7x, 512 devices: a whole 4x8x8 slice. The times are simulated.
512 devices in a mesh: row: 16 (over y, x_hi), col: 32 (over x_lo, z, core).
Axes of the slice: x: 4 (x_hi: 2, x_lo: 2; x = x_hi * 2 + x_lo), y: 8, z: 8, core: 2. Of those that a mesh axis runs over, the one named last changes fastest.
Arguments:
- tokens: bfloat16 [2048, 4096], P('row', 'col'), may hold values from -6 to 6
- mixer_out: bfloat16 [2048, 8192], P('row', 'col'), may hold values from -6 to 6
- gate_weight: bfloat16 [4096, 8192], P('row', 'col'), may hold values from -0.09375 to 0.09375
- out_weight: bfloat16 [8192, 4096], P('row', 'col'), may hold values from -0.125 to 0.125
- out_grad: bfloat16 [2048, 4096], P('row', 'col'), may hold values from -6 to 6
Outputs:
- layer_out: bfloat16 [2048, 4096], P('row', 'col')
- mixer_grad: bfloat16 [2048, 8192], P('row', 'col')
- gate_weight_grad: bfloat16 [4096, 8192], P('row', 'col')
- out_weight_grad: bfloat16 [8192, 4096], P('row', 'col')
All inputs are finite; a program needn't handle non-finite values.
Results may differ from a plain program's by a relative error of at most 0.0049.
Values may be sent and summed in bfloat16 or wider, within the bound.
No kernel may reach another device: no remote copies, remote signals or barrier semaphores. Data moves between devices by JAX's collectives and lax.ppermute only.
A program may use at most 64 MiB of HBM per device.

v0:
```python
import jax
import jax.numpy as jnp
from jax import lax
from jax.sharding import PartitionSpec as P


def local(tokens, mixer_out, gate_weight, out_weight, out_grad):
    act_rows = lax.all_gather(tokens, "col", axis=1, tiled=True)
    gate_pre = jnp.dot(
        act_rows,
        lax.all_gather(gate_weight, "row", axis=0, tiled=True),
        preferred_element_type=jnp.float32,
    )
    out_full = lax.all_gather(out_weight, "row", axis=0, tiled=True)
    gate_sig = jax.nn.sigmoid(gate_pre)
    gate_silu = gate_pre * gate_sig
    mixer_vals = mixer_out.astype(jnp.float32)
    gated = (mixer_vals * gate_silu).astype(jnp.bfloat16)
    gated_full = lax.all_gather(gated, "col", axis=1, tiled=True)
    layer_out = jnp.dot(gated_full, out_full, preferred_element_type=jnp.float32).astype(
        jnp.bfloat16
    )
    partial_value = lax.dot_general(
        out_grad, out_full, (((1,), (1,)), ((), ())), preferred_element_type=jnp.float32
    )
    hidden_grad = lax.psum_scatter(partial_value, "col", scatter_dimension=1, tiled=True)
    mixer_grad = (hidden_grad * gate_silu).astype(jnp.bfloat16)
    pre_grad = (hidden_grad * mixer_vals * gate_sig * (1.0 + gate_pre * (1.0 - gate_sig))).astype(
        jnp.bfloat16
    )
    act_cols, gated_cols = (
        lax.all_to_all(act_rows, "row", split_axis=1, concat_axis=0, tiled=True),
        lax.all_to_all(gated_full, "row", split_axis=1, concat_axis=0, tiled=True),
    )
    pre_all, cot_all = (
        lax.all_gather(pre_grad, "row", axis=0, tiled=True),
        lax.all_gather(out_grad, "row", axis=0, tiled=True),
    )
    gate_weight_grad = lax.dot_general(
        act_cols, pre_all, (((0,), (0,)), ((), ())), preferred_element_type=jnp.float32
    ).astype(jnp.bfloat16)
    out_weight_grad = lax.dot_general(
        gated_cols, cot_all, (((0,), (0,)), ((), ())), preferred_element_type=jnp.float32
    ).astype(jnp.bfloat16)
    return (layer_out, mixer_grad, gate_weight_grad, out_weight_grad)


def solution(mesh):
    in_specs = (P("row", "col"), P("row", "col"), P("row", "col"), P("row", "col"), P("row", "col"))
    out_specs = (P("row", "col"), P("row", "col"), P("row", "col"), P("row", "col"))
    return jax.shard_map(local, mesh=mesh, in_specs=in_specs, out_specs=out_specs, check_vma=False)
```

profile of v0, /device:TPU:16, one launch (start us, length us, event | category | flops | bytes accessed | tf_op | source)
XLA Modules:
  0.0 592.6 jit_solution(14906419829611233574)
XLA Ops:
  7.2 0.0 all-gather.12.cloned.1.call-start
  7.2 0.7 all-gather.12.cloned.1.call-update
  7.9 0.0 all-gather.6.cloned.1.call-start
  7.9 1.5 copy.12
  9.4 0.0 all-gather.6.cloned.1.call-update
  9.4 0.0 all-gather.8.cloned.1.call-start
  9.5 0.7 all-gather.8.cloned.1.call-update
  10.2 0.0 reduce-scatter.2.cloned.1.call-start
  10.2 94.7 %all-gather.12.cloned.1.call-done = bf16[8192,128]{1,0:T(8,128)(2,1)} async-done(((bf16[512,128]{1,0:T(8,128)(2,1)}), bf16[8192,128]{1,0:T(8,128)(2,1)}) %all-gather.12.cloned.1.call-update) | async-done | bytes 2097168 | tf_op jit(solution)/shard_map/all_gather | solution.py:14
  105.0 4.3 fusion.6
  109.2 0.0 copy-start.3
  109.2 0.0 reduce-scatter.2.cloned.1.call-update
  109.3 0.0 all-gather.10.cloned.1.call-start
  109.3 63.6 %all-gather.6.cloned.1.call-done = bf16[128,4096]{0,1:T(8,128)(2,1)} async-done(((bf16[128,128]{0,1:T(8,128)(2,1)}), bf16[128,4096]{0,1:T(8,128)(2,1)}) %all-gather.6.cloned.1.call-update) | async-done | bytes 1048592 | tf_op jit(solution)/shard_map/all_gather | solution.py:8
  172.9 91.9 %all-gather.8.cloned.1.call-done = bf16[4096,256]{1,0:T(8,128)(2,1)} async-done(((bf16[256,256]{1,0:T(8,128)(2,1)}), bf16[4096,256]{1,0:T(8,128)(2,1)}) %all-gather.8.cloned.1.call-update) | async-done | bytes 2097168 | tf_op jit(solution)/shard_map/all_gather | solution.py:11
  264.8 126.8 %reduce-scatter.2.cloned.1.call-done = f32[128,256]{1,0:T(8,128)} async-done(((f32[128,8192]{1,0:T(8,128)}), f32[128,256]{1,0:T(8,128)}) %reduce-scatter.2.cloned.1.call-update) | async-done | bytes 131088 | tf_op jit(solution)/shard_map/reduce_scatter | solution.py:26
  391.7 0.0 copy-done.3
  391.7 3.2 fusion.4
  394.8 0.0 all-gather.10.cloned.1.call-update
  394.8 9.4 %all-to-all-start = ((bf16[128,16,256]{0,2,1:T(8,128)(2,1)}), bf16[128,16,256]{0,2,1:T(8,128)(2,1)S(1)}, u32[]{:S(2)}, u32[]{:S(2)}) async-start(bf16[128,16,256]{0,2,1:T(8,128)(2,1)} %bitcast), calls=%async_computation.1 | async-start | bytes 2097152 | tf_op jit(solution)/shard_map/all_to_all | solution.py:32
  404.2 56.4 %all-gather.10.cloned.1.call-done = bf16[128,8192]{1,0:T(8,128)(2,1)} async-done(((bf16[128,256]{1,0:T(8,128)(2,1)}), bf16[128,8192]{1,0:T(8,128)(2,1)}) %all-gather.10.cloned.1.call-update) | async-done | bytes 2097168 | tf_op jit(solution)/shard_map/all_gather | solution.py:19
  460.6 3.2 copy.18
  463.8 0.0 all-to-all-done
  463.8 0.0 copy-start.2
  463.8 14.6 %all-to-all-start.1 = ((bf16[128,16,512]{2,0,1:T(8,128)(2,1)}), bf16[128,16,512]{2,0,1:T(8,128)(2,1)}, u32[]{:S(2)}, u32[]{:S(2)}) async-start(bf16[128,16,512]{2,0,1:T(8,128)(2,1)} %bitcast.21), calls=%async_computation.2 | async-start | bytes 4194304 | tf_op jit(solution)/shard_map/all_to_all | solution.py:33
  478.4 0.0 all-gather.14.cloned.1.call-start
  478.5 0.5 all-gather.14.cloned.1.call-update
  479.0 0.0 copy-done.2
  479.0 85.3 %all_gather.23 = bf16[2048,128]{1,0:T(8,128)(2,1)} all-gather(bf16[128,128]{1,0:T(8,128)(2,1)S(1)} %copy-done.2), channel_id=1, replica_groups=mesh['row'=16,'col'=32] {'row'}, dimensions={0}, use_global_device_ids=true | all-gather | bytes 557056 | tf_op jit(solution)/shard_map/all_gather | solution.py:37
  564.3 0.0 copy-start
  564.3 1.3 copy.13
  565.7 11.3 %all-gather.14.cloned.1.call-done = bf16[2048,256]{1,0:T(8,128)(2,1)} async-done(((bf16[128,256]{1,0:T(8,128)(2,1)}), bf16[2048,256]{1,0:T(8,128)(2,1)}) %all-gather.14.cloned.1.call-update) | async-done | bytes 1048592 | tf_op jit(solution)/shard_map/all_gather | solution.py:36
  577.0 2.0 fusion
  579.0 0.8 copy.15
  579.7 0.0 copy-done
  579.7 0.0 copy-start.1
  579.7 3.0 convolution_convert_fusion.2
  582.7 0.0 all-to-all-done.1
  582.7 0.0 copy-done.1
  582.7 3.0 convolution_convert_fusion
Async XLA Ops:
  7.2 97.8 %all-gather.12.cloned.1.call-start = ((), (), s32[]{:S(2)}) async-start(), calls=%async_computation.6 | async-start | bytes 2228224 | tf_op jit(solution)/shard_map/all_gather | solution.py:14
  7.9 165.0 %all-gather.6.cloned.1.call-start = ((), (), s32[]{:S(2)}) async-start(), calls=%async_computation.3 | async-start | bytes 1081344 | tf_op jit(solution)/shard_map/all_gather | solution.py:8
  9.4 255.4 %all-gather.8.cloned.1.call-start = ((), (), s32[]{:S(2)}) async-start(), calls=%async_computation.4 | async-start | bytes 2228224 | tf_op jit(solution)/shard_map/all_gather | solution.py:11
  10.2 381.5 %reduce-scatter.2.cloned.1.call-start = ((), (), s32[]{:S(2)}) async-start(), calls=%async_computation.7 | async-start | bytes 4325376 | tf_op jit(solution)/shard_map/reduce_scatter | solution.py:26
  109.2 282.4 %copy-start.3 = (bf16[128,256]{1,0:T(8,128)(2,1)S(1)}, bf16[128,256]{1,0:T(8,128)(2,1)}, u32[]{:S(2)}) copy-start(bf16[128,256]{1,0:T(8,128)(2,1)} %param.6) | copy-start | bytes 196612
  109.3 351.3 %all-gather.10.cloned.1.call-start = ((), (), s32[]{:S(2)}) async-start(), calls=%async_computation.5 | async-start | bytes 2162688 | tf_op jit(solution)/shard_map/all_gather | solution.py:19
  394.8 68.9 %all-to-all-start = ((bf16[128,16,256]{0,2,1:T(8,128)(2,1)}), bf16[128,16,256]{0,2,1:T(8,128)(2,1)S(1)}, u32[]{:S(2)}, u32[]{:S(2)}) async-start(bf16[128,16,256]{0,2,1:T(8,128)(2,1)} %bitcast), calls=%async_computation.1 | async-start | bytes 2097152 | tf_op jit(solution)/shard_map/all_to_all | solution.py:32
  463.8 15.2 %copy-start.2 = (bf16[128,128]{1,0:T(8,128)(2,1)S(1)}, bf16[128,128]{1,0:T(8,128)(2,1)}, u32[]{:S(2)}) copy-start(bf16[128,128]{1,0:T(8,128)(2,1)} %param.9) | copy-start | bytes 98308
  463.8 118.9 %all-to-all-start.1 = ((bf16[128,16,512]{2,0,1:T(8,128)(2,1)}), bf16[128,16,512]{2,0,1:T(8,128)(2,1)}, u32[]{:S(2)}, u32[]{:S(2)}) async-start(bf16[128,16,512]{2,0,1:T(8,128)(2,1)} %bitcast.21), calls=%async_computation.2 | async-start | bytes 4194304 | tf_op jit(solution)/shard_map/all_to_all | solution.py:33
  478.4 98.5 %all-gather.14.cloned.1.call-start = ((), (), s32[]{:S(2)}) async-start(), calls=%async_computation.8 | async-start | bytes 1114112 | tf_op jit(solution)/shard_map/all_gather | solution.py:36
  564.3 15.4 %copy-start = (bf16[8192,128]{1,0:T(8,128)(2,1)S(1)}, bf16[8192,128]{1,0:T(8,128)(2,1)}, u32[]{:S(2)}) copy-start(bf16[8192,128]{1,0:T(8,128)(2,1)} %all-gather.12.cloned.1.call-done) | copy-start | bytes 6291460
  579.7 3.0 copy-start.1
Sparse Core Ops, SparseCore 0:
  11.2 93.7 all-gather.11
  107.7 65.1 all-gather.5
  176.1 88.6 all-gather.7
  267.5 124.1 reduce-scatter.1
  395.0 65.5 all-gather.9
  482.7 94.2 all-gather.13
where the time goes:
time: 593 us
  waiting for transfers between devices  447 us (75%)
  blocking collectives  85.3 us (14%)
  starting transfers between devices  24.3 us (4%)
  matrix products  15.4 us (3%)
  between operations  14.1 us (2%)
  local copies, waits for them, and re-layouts  6.77 us (1%)
    reduce_scatter x1, waiting for transfers between devices, local(): lax.psum_scatter(partial_value, 'col', scatter_dimension=1, tiled=True)  127 us
    all_gather x1, waiting for transfers between devices, local(): out_full = lax.all_gather(out_weight, 'row', axis=0, tiled=True)  94.7 us
    all_gather x1, waiting for transfers between devices, local(): lax.all_gather(gate_weight, 'row', axis=0, tiled=True)  91.9 us
    all_gather x1, blocking collectives, local(): lax.all_gather(out_grad, 'row', axis=0, tiled=True)  85.3 us
    all_gather x1, waiting for transfers between devices, local(): act_rows = lax.all_gather(tokens, 'col', axis=1, tiled=True)  63.6 us
    all_gather x1, waiting for transfers between devices, local(): gated_full = lax.all_gather(gated, 'col', axis=1, tiled=True)  56.4 us
    all_to_all x1, starting transfers between devices, local(): lax.all_to_all(gated_full, 'row', split_axis=1, concat_axis=0, tiled=True)  14.6 us
  transfers between devices with their start and end apart: 8, of which 6 were waited for; matrix products, arithmetic and copies ran while one was open for 3% of the time, Pallas kernels for 0%

commit v1 on v0

v1 whole, which is shorter than its diff:
```python
import jax
import jax.numpy as jnp
from jax import lax
from jax.sharding import Mesh, PartitionSpec as P

ROWS, COLS = ("y", "xh"), ("xl", "z", "c")
ALL = ROWS + COLS
N = 16


def device(r, j, core):
    return (r * N + j) * 2 + core


ALONG_J = [[[device(r, j, core) for j in range(N)] for r in range(N)] for core in (0, 1)]
ALONG_R = [[[device(r, j, core) for r in range(N)] for j in range(N)] for core in (0, 1)]
GROUPS_A = ALONG_J[0] + ALONG_R[1]
GROUPS_B = ALONG_R[0] + ALONG_J[1]
CHIPS = [(r, j) for r in range(N) for j in range(N)]
SWAP = [(d, d ^ 1) for d in range(2 * N * N)]
TURN_OWN = [p for r, j in CHIPS for p in ((device(r, j, 0), device(j, r, 0)), (device(r, j, 1), device(r, j, 1)))]
TURN_OTHER = [p for r, j in CHIPS for p in ((device(r, j, 1), device(j, r, 0)), (device(r, j, 0), device(r, j, 1)))]
CROSS = [p for r, j in CHIPS for p in ((device(r, j, 0), device(j, r, 1)), (device(r, j, 1), device(j, r, 0)))]


def trade(blocks, groups):
    return lax.all_to_all(blocks, ALL, split_axis=0, concat_axis=0, axis_index_groups=groups, tiled=True)


def gather(block, groups):
    out = trade(jnp.broadcast_to(block, (N,) + block.shape), groups)
    return out.reshape(N * block.shape[0], block.shape[1])


def reduce(partial, groups):
    blocks = partial.astype(jnp.bfloat16).reshape(N, partial.shape[0] // N, partial.shape[1])
    return jnp.sum(trade(blocks, groups).astype(jnp.float32), axis=0)


def fold(wide):
    half = wide.shape[1] // 2
    return jnp.concatenate([wide[:, :half], wide[:, half:]], axis=0)


def unfold(tall):
    half = tall.shape[0] // 2
    return jnp.concatenate([tall[:half], tall[half:]], axis=1)


def local(tokens, mixer_out, gate_weight, out_weight, out_grad):
    f32, bf16 = jnp.float32, jnp.bfloat16
    first = lax.axis_index("c") == 0
    own = lax.ppermute(jnp.where(first, tokens, out_grad), ALL, TURN_OWN)
    other = lax.ppermute(jnp.where(first, out_grad, tokens), ALL, TURN_OTHER)
    acts = jnp.concatenate([own, other], axis=1)
    out_t = out_weight.T
    weight_in = lax.ppermute(jnp.where(first, fold(out_t), gate_weight), ALL, SWAP)
    weight = jnp.where(
        first,
        jnp.concatenate([gate_weight, weight_in], axis=1),
        jnp.concatenate([out_t, unfold(weight_in)], axis=0),
    )
    mixer_in = lax.ppermute(mixer_out, ALL, SWAP)
    mixer_vals = jnp.concatenate([mixer_out, mixer_in], axis=1).astype(f32)

    acts_all = gather(acts, GROUPS_A)
    total = reduce(jnp.dot(acts_all, weight, preferred_element_type=f32), GROUPS_B)

    gate_pre = total
    gate_sig = jax.nn.sigmoid(gate_pre)
    gate_silu = gate_pre * gate_sig
    gated = (mixer_vals * gate_silu).astype(bf16)
    crossed = lax.ppermute(jnp.where(first, gated.astype(f32), total), ALL, CROSS)
    hidden_grad = crossed
    mixer_grad = (hidden_grad * gate_silu).astype(bf16)
    pre_grad = (hidden_grad * mixer_vals * gate_sig * (1.0 + gate_pre * (1.0 - gate_sig))).astype(bf16)
    units_all = gather(jnp.where(first, pre_grad, crossed.astype(bf16)), GROUPS_B)

    layer_pair = reduce(
        lax.dot_general(units_all, weight, (((1,), (1,)), ((), ())), preferred_element_type=f32), GROUPS_A
    ).astype(bf16)
    grads = lax.dot_general(
        acts_all, units_all, (((0,), (0,)), ((), ())), preferred_element_type=f32
    ).astype(bf16)

    inner, width = gate_weight.shape[1], out_grad.shape[1]
    mixer_grad_in = lax.ppermute(mixer_grad[:, inner:], ALL, SWAP)
    grads_in = lax.ppermute(jnp.where(first, grads[:, inner:], fold(grads[width:])), ALL, SWAP)
    layer_in = lax.ppermute(layer_pair[:, width:], ALL, SWAP)
    return (
        jnp.where(first, layer_in, layer_pair[:, :width]),
        jnp.where(first, mixer_grad[:, :inner], mixer_grad_in),
        jnp.where(first, grads[:, :inner], grads_in),
        jnp.where(first, unfold(grads_in), grads[:width]).T,
    )


def solution(mesh):
    fine = Mesh(mesh.devices.reshape(8, 2, 2, 8, 2), ALL)
    spec = P(ROWS, COLS)
    return jax.shard_map(local, mesh=fine, in_specs=(spec,) * 5, out_specs=(spec,) * 4, check_vma=False)
```

time: 593 us -> 214 us (0.36)
  the two profiles are of different devices: /device:TPU:16 before, /device:TPU:1 now
where the time goes in v1:
time: 214 us; the launch traced here: 213 us
  blocking collectives  78.1 us (36%)
  starting transfers between devices  74 us (35%)
  waiting for transfers between devices  44.2 us (21%)
  matrix products  6.08 us (3%)
  other arithmetic  5.34 us (2%)
  local copies, waits for them, and re-layouts  4.34 us (2%)
    all_to_all x1, blocking collectives, trade(): lax.all_to_all(blocks, ALL, split_axis=0, concat_axis=0, axis_index_group...  78.1 us
    all_to_all x3, waiting for transfers between devices, trade(): lax.all_to_all(blocks, ALL, split_axis=0, concat_axis=0, axis_index_group...  40.5 us
    all_to_all x3, starting transfers between devices, trade(): lax.all_to_all(blocks, ALL, split_axis=0, concat_axis=0, axis_index_group...  31.4 us
    ppermute x1, starting transfers between devices, local(): other = lax.ppermute(jnp.where(first, out_grad, tokens), ALL, TURN_OTHER)  8.79 us
    ppermute x1, starting transfers between devices, local(): lax.ppermute(jnp.where(first, fold(out_t), gate_weight), ALL, SWAP)  7.38 us
    ppermute x1, starting transfers between devices, local(): mixer_grad_in = lax.ppermute(mixer_grad[:, inner:], ALL, SWAP)  7.12 us
    ppermute x1, starting transfers between devices, local(): lax.ppermute(jnp.where(first, gated.astype(f32), total), ALL, CROSS)  6.77 us
    ppermute x1, starting transfers between devices, local(): mixer_in = lax.ppermute(mixer_out, ALL, SWAP)  5.44 us
  transfers between devices with their start and end apart: 11, of which 7 were waited for; matrix products, arithmetic and copies ran while one was open for 2% of the time, Pallas kernels for 0%

profile of v1, /device:TPU:1, one launch (start us, length us, event | category | flops | bytes accessed | tf_op | source)
XLA Modules:
  0.0 213.0 jit_solution(8553407251485421659)
XLA Ops:
  0.6 0.0 copy-start.9
  0.6 0.0 copy-start.1
  0.7 0.8 broadcast_select_fusion.1
  1.5 0.7 collective-permute-start.1
  2.1 8.8 %collective-permute-start.2 = (bf16[128,128]{1,0:T(8,128)(2,1)S(1)}, bf16[128,128]{1,0:T(8,128)(2,1)S(1)}, u32[]{:S(2)}, u32[]{:S(2)}) collective-permute-start(bf16[128,128]{1,0:T(8,128)(2,1)S(1)} %get-tuple-element.21), channel_id=1, source_target_pairs={{1,0},{0,1},{3,32},{2,3},{5,64},{4,5},{7,96},{6,7},{9,128},{8,9},{... | collective-permute-start | bytes 98312 | tf_op jit(solution)/shard_map/ppermute | solution.py:54
  10.9 0.0 collective-permute-done.1
  11.0 0.8 collective-permute-done.2
  11.8 0.1 copy.12
  11.9 1.2 broadcast_in_dim.6
  13.1 12.9 %all-to-all-start = ((bf16[16,128,256]{1,2,0:T(8,128)(2,1)}), bf16[16,128,256]{1,2,0:T(8,128)(2,1)S(1)}, u32[]{:S(2)}, u32[]{:S(2)}) async-start(bf16[16,128,256]{1,2,0:T(8,128)(2,1)} %broadcast_in_dim.6), calls=%async_computation | async-start | bytes 2097152 | tf_op jit(solution)/shard_map/all_to_all | solution.py:27
  26.1 0.0 copy-done.9
  26.1 0.1 copy.14
  26.2 0.0 copy-done.1
  26.3 7.4 %collective-permute-start.3 = (bf16[256,256]{1,0:T(8,128)(2,1)S(1)}, bf16[256,256]{1,0:T(8,128)(2,1)S(1)}, u32[]{:S(2)}, u32[]{:S(2)}) collective-permute-start(bf16[256,256]{1,0:T(8,128)(2,1)S(1)} %maximum_select_fusion.1), channel_id=1, source_target_pairs={{0,1},{1,0},{2,3},{3,2},{4,5},{5,4},{6,7},{7,6},{8,9},{9,8},{10,11... | collective-permute-start | bytes 393224 | tf_op jit(solution)/shard_map/ppermute | solution.py:57
  33.7 1.0 collective-permute-done.3
  34.6 0.0 copy-start.3
  34.6 0.0 copy-start.5
  34.6 0.0 copy-start.7
  34.7 11.0 %all-to-all-done = bf16[16,128,256]{1,2,0:T(8,128)(2,1)S(1)} async-done(((bf16[16,128,256]{1,2,0:T(8,128)(2,1)}), bf16[16,128,256]{1,2,0:T(8,128)(2,1)S(1)}, u32[]{:S(2)}, u32[]{:S(2)}) %all-to-all-start) | async-done | bytes 1048608 | tf_op jit(solution)/shard_map/all_to_all | solution.py:27
  45.7 0.5 copy.13
  46.2 2.1 convolution_convert_fusion
  48.3 0.0 copy-done.3
  48.3 0.0 copy-done.5
  48.3 0.0 copy-done.7
  48.3 11.4 %all-to-all-start.1 = ((bf16[16,128,512]{2,1,0:T(8,128)(2,1)}), bf16[16,128,512]{2,1,0:T(8,128)(2,1)S(1)}, u32[]{:S(2)}, u32[]{:S(2)}) async-start(bf16[16,128,512]{2,1,0:T(8,128)(2,1)} %bitcast.2), calls=%async_computation.1 | async-start | bytes 4194304 | tf_op jit(solution)/shard_map/all_to_all | solution.py:27
  59.7 5.4 %collective-permute-start = (bf16[128,256]{1,0:T(8,128)(2,1)}, bf16[128,256]{1,0:T(8,128)(2,1)}, u32[]{:S(2)}, u32[]{:S(2)}) collective-permute-start(bf16[128,256]{1,0:T(8,128)(2,1)} %param.6), channel_id=1, source_target_pairs={{0,1},{1,0},{2,3},{3,2},{4,5},{5,4},{6,7},{7,6},{8,9},{9,8},{10,11... | collective-permute-start | bytes 196616 | tf_op jit(solution)/shard_map/ppermute | solution.py:63
  65.1 23.6 %all-to-all-done.1 = bf16[16,128,512]{2,1,0:T(8,128)(2,1)S(1)} async-done(((bf16[16,128,512]{2,1,0:T(8,128)(2,1)}), bf16[16,128,512]{2,1,0:T(8,128)(2,1)S(1)}, u32[]{:S(2)}, u32[]{:S(2)}) %all-to-all-start.1) | async-done | bytes 2097184 | tf_op jit(solution)/shard_map/all_to_all | solution.py:27
  88.7 0.3 convert_reduce_fusion
  89.0 0.0 collective-permute-done
  89.0 1.0 convert_select_fusion
  89.9 6.8 %collective-permute-start.4 = (f32[128,512]{1,0:T(8,128)S(1)}, f32[128,512]{1,0:T(8,128)S(1)}, u32[]{:S(2)}, u32[]{:S(2)}) collective-permute-start(f32[128,512]{1,0:T(8,128)S(1)} %convert_select_fusion), channel_id=1, source_target_pairs={{0,1},{1,0},{2,33},{3,32},{4,65},{5,64},{6,97},{7,96},{8,129},{9,1... | collective-permute-start | bytes 786440 | tf_op jit(solution)/shard_map/ppermute | solution.py:73
  96.7 1.1 collective-permute-done.4
  97.8 1.0 convert_select_fusion.1
  98.8 0.2 broadcast_in_dim.7
  99.0 0.0 copy-start.2
  99.1 0.0 copy-start.4
  99.1 0.0 copy-start.6
  99.1 0.0 copy-start.8
  99.1 78.1 %all_to_all.20 = bf16[16,128,512]{2,1,0:T(8,128)(2,1)S(1)} all-to-all(bf16[16,128,512]{2,1,0:T(8,128)(2,1)S(1)} %broadcast_in_dim.7), channel_id=1, replica_groups={{0,32,64,96,128,160,192,224,256,288,320,352,384,416,448,480},{2,34,66,9..., dimensions={0} | all-to-all | bytes 4194304 | tf_op jit(solution)/shard_map/all_to_all | solution.py:27
  177.2 0.0 copy-start
  177.2 1.3 copy-done
  178.5 0.0 copy-done.2
  178.5 0.0 copy-done.4
  178.5 0.0 copy-done.6
  178.5 0.0 copy-done.8
  178.5 1.7 convolution_convert_fusion.1
  180.2 7.1 %all-to-all-start.3 = ((bf16[16,128,256]{2,1,0:T(8,128)(2,1)}), bf16[16,128,256]{2,1,0:T(8,128)(2,1)S(1)}, u32[]{:S(2)}, u32[]{:S(2)}) async-start(bf16[16,128,256]{2,1,0:T(8,128)(2,1)} %bitcast.4), calls=%async_computation.3 | async-start | bytes 2097152 | tf_op jit(solution)/shard_map/all_to_all | solution.py:27
  187.3 0.1 multiply_convert_fusion
  187.4 7.1 %collective-permute-start.6 = (bf16[128,256]{1,0:T(8,128)(2,1)S(1)}, bf16[128,256]{1,0:T(8,128)(2,1)S(1)}, u32[]{:S(2)}, u32[]{:S(2)}) collective-permute-start(bf16[128,256]{1,0:T(8,128)(2,1)S(1)} %slice.70), channel_id=1, source_target_pairs={{0,1},{1,0},{2,3},{3,2},{4,5},{5,4},{6,7},{7,6},{8,9},{9,8},{10,11... | collective-permute-start | bytes 196616 | tf_op jit(solution)/shard_map/ppermute | solution.py:87
  194.6 2.3 %fusion = bf16[256,512]{1,0:T(8,128)(2,1)S(1)} fusion(bf16[16,128,256]{1,2,0:T(8,128)(2,1)S(1)} %all-to-all-done, bf16[16,128,512]{2,1,0:T(8,128)(2,1)} %copy-done), kind=kOutput, calls=%fused_computation.4 | convolution fusion | flops 537001984 | bytes 3407872 | tf_op jit(solution)/shard_map/dot_general | solution.py:82
  196.9 1.9 collective-permute-start.7
  198.9 0.0 collective-permute-done.6
  198.9 0.6 slice_select_fusion.3
  199.5 0.7 collective-permute-done.7
  200.2 0.7 slice_select_fusion.2
  200.9 6.0 %all-to-all-done.3 = bf16[16,128,256]{2,1,0:T(8,128)(2,1)S(1)} async-done(((bf16[16,128,256]{2,1,0:T(8,128)(2,1)}), bf16[16,128,256]{2,1,0:T(8,128)(2,1)S(1)}, u32[]{:S(2)}, u32[]{:S(2)}) %all-to-all-start.3) | async-done | bytes 1048608 | tf_op jit(solution)/shard_map/all_to_all | solution.py:27
  206.8 0.1 reduce_sum.22
  207.0 4.5 %collective-permute-start.5 = (bf16[128,128]{1,0:T(8,128)(2,1)S(1)}, bf16[128,128]{1,0:T(8,128)(2,1)S(1)}, u32[]{:S(2)}, u32[]{:S(2)}) collective-permute-start(bf16[128,128]{1,0:T(8,128)(2,1)S(1)} %slice.67), channel_id=1, source_target_pairs={{0,1},{1,0},{2,3},{3,2},{4,5},{5,4},{6,7},{7,6},{8,9},{9,8},{10,11... | collective-permute-start | bytes 98312 | tf_op jit(solution)/shard_map/ppermute | solution.py:89
  211.6 0.8 copy.15
  212.3 0.0 collective-permute-done.5
  212.4 0.6 slice_select_fusion.4
  (10 shorter events, 0.2 us)
Async XLA Ops:
  0.6 25.4 %copy-start.9 = (bf16[512,128]{1,0:T(8,128)(2,1)S(1)}, bf16[512,128]{1,0:T(8,128)(2,1)}, u32[]{:S(2)}) copy-start(bf16[512,128]{1,0:T(8,128)(2,1)} %param.8) | copy-start | bytes 393220
  0.6 25.6 %copy-start.1 = (bf16[256,256]{1,0:T(8,128)(2,1)S(1)}, bf16[256,256]{1,0:T(8,128)(2,1)}, u32[]{:S(2)}) copy-start(bf16[256,256]{1,0:T(8,128)(2,1)} %param.7) | copy-start | bytes 393220
  1.5 9.5 %collective-permute-start.1 = (bf16[128,128]{1,0:T(8,128)(2,1)S(1)}, bf16[128,128]{1,0:T(8,128)(2,1)S(1)}, u32[]{:S(2)}, u32[]{:S(2)}) collective-permute-start(bf16[128,128]{1,0:T(8,128)(2,1)S(1)} %get-tuple-element.20), channel_id=1, source_target_pairs={{0,0},{1,1},{2,32},{3,3},{4,64},{5,5},{6,96},{7,7},{8,128},{9,9},{... | collective-permute-start | bytes 98312 | tf_op jit(solution)/shard_map/ppermute | solution.py:53
  2.1 9.6 %collective-permute-start.2 = (bf16[128,128]{1,0:T(8,128)(2,1)S(1)}, bf16[128,128]{1,0:T(8,128)(2,1)S(1)}, u32[]{:S(2)}, u32[]{:S(2)}) collective-permute-start(bf16[128,128]{1,0:T(8,128)(2,1)S(1)} %get-tuple-element.21), channel_id=1, source_target_pairs={{1,0},{0,1},{3,32},{2,3},{5,64},{4,5},{7,96},{6,7},{9,128},{8,9},{... | collective-permute-start | bytes 98312 | tf_op jit(solution)/shard_map/ppermute | solution.py:54
  13.1 32.6 %all-to-all-start = ((bf16[16,128,256]{1,2,0:T(8,128)(2,1)}), bf16[16,128,256]{1,2,0:T(8,128)(2,1)S(1)}, u32[]{:S(2)}, u32[]{:S(2)}) async-start(bf16[16,128,256]{1,2,0:T(8,128)(2,1)} %broadcast_in_dim.6), calls=%async_computation | async-start | bytes 2097152 | tf_op jit(solution)/shard_map/all_to_all | solution.py:27
  26.3 8.4 %collective-permute-start.3 = (bf16[256,256]{1,0:T(8,128)(2,1)S(1)}, bf16[256,256]{1,0:T(8,128)(2,1)S(1)}, u32[]{:S(2)}, u32[]{:S(2)}) collective-permute-start(bf16[256,256]{1,0:T(8,128)(2,1)S(1)} %maximum_select_fusion.1), channel_id=1, source_target_pairs={{0,1},{1,0},{2,3},{3,2},{4,5},{5,4},{6,7},{7,6},{8,9},{9,8},{10,11... | collective-permute-start | bytes 393224 | tf_op jit(solution)/shard_map/ppermute | solution.py:57
  34.6 13.6 %copy-start.3 = (bf16[256,256]{1,0:T(8,128)(2,1)}, bf16[256,256]{1,0:T(8,128)(2,1)S(1)}, u32[]{:S(2)}) copy-start(bf16[256,256]{1,0:T(8,128)(2,1)S(1)} %collective-permute-done.3) | copy-start | bytes 393220
  34.6 13.6 %copy-start.5 = (bf16[128,256]{1,0:T(8,128)(2,1)}, bf16[128,256]{1,0:T(8,128)(2,1)S(1)}, u32[]{:S(2)}) copy-start(bf16[128,256]{1,0:T(8,128)(2,1)S(1)} %get-tuple-element.16) | copy-start | bytes 196612
  34.6 13.6 %copy-start.7 = (bf16[128,256]{1,0:T(8,128)(2,1)}, bf16[128,256]{1,0:T(8,128)(2,1)S(1)}, u32[]{:S(2)}) copy-start(bf16[128,256]{1,0:T(8,128)(2,1)S(1)} %get-tuple-element.17) | copy-start | bytes 196612
  48.3 40.4 %all-to-all-start.1 = ((bf16[16,128,512]{2,1,0:T(8,128)(2,1)}), bf16[16,128,512]{2,1,0:T(8,128)(2,1)S(1)}, u32[]{:S(2)}, u32[]{:S(2)}) async-start(bf16[16,128,512]{2,1,0:T(8,128)(2,1)} %bitcast.2), calls=%async_computation.1 | async-start | bytes 4194304 | tf_op jit(solution)/shard_map/all_to_all | solution.py:27
  59.7 29.3 %collective-permute-start = (bf16[128,256]{1,0:T(8,128)(2,1)}, bf16[128,256]{1,0:T(8,128)(2,1)}, u32[]{:S(2)}, u32[]{:S(2)}) collective-permute-start(bf16[128,256]{1,0:T(8,128)(2,1)} %param.6), channel_id=1, source_target_pairs={{0,1},{1,0},{2,3},{3,2},{4,5},{5,4},{6,7},{7,6},{8,9},{9,8},{10,11... | collective-permute-start | bytes 196616 | tf_op jit(solution)/shard_map/ppermute | solution.py:63
  89.9 7.9 %collective-permute-start.4 = (f32[128,512]{1,0:T(8,128)S(1)}, f32[128,512]{1,0:T(8,128)S(1)}, u32[]{:S(2)}, u32[]{:S(2)}) collective-permute-start(f32[128,512]{1,0:T(8,128)S(1)} %convert_select_fusion), channel_id=1, source_target_pairs={{0,1},{1,0},{2,33},{3,32},{4,65},{5,64},{6,97},{7,96},{8,129},{9,1... | collective-permute-start | bytes 786440 | tf_op jit(solution)/shard_map/ppermute | solution.py:73
  99.0 79.5 %copy-start.2 = (bf16[256,256]{1,0:T(8,128)(2,1)S(1)}, bf16[256,256]{1,0:T(8,128)(2,1)}, u32[]{:S(2)}) copy-start(bf16[256,256]{1,0:T(8,128)(2,1)} %param.7) | copy-start | bytes 393220
  99.1 79.4 %copy-start.4 = (bf16[256,256]{1,0:T(8,128)(2,1)S(1)}, bf16[256,256]{1,0:T(8,128)(2,1)}, u32[]{:S(2)}) copy-start(bf16[256,256]{1,0:T(8,128)(2,1)} %copy-done.3) | copy-start | bytes 393220
  99.1 79.4 %copy-start.6 = (bf16[128,256]{1,0:T(8,128)(2,1)S(1)}, bf16[128,256]{1,0:T(8,128)(2,1)}, u32[]{:S(2)}) copy-start(bf16[128,256]{1,0:T(8,128)(2,1)} %copy-done.5) | copy-start | bytes 196612
  99.1 79.4 %copy-start.8 = (bf16[128,256]{1,0:T(8,128)(2,1)S(1)}, bf16[128,256]{1,0:T(8,128)(2,1)}, u32[]{:S(2)}) copy-start(bf16[128,256]{1,0:T(8,128)(2,1)} %copy-done.7) | copy-start | bytes 196612
  177.2 1.3 copy-start
  180.2 26.6 %all-to-all-start.3 = ((bf16[16,128,256]{2,1,0:T(8,128)(2,1)}), bf16[16,128,256]{2,1,0:T(8,128)(2,1)S(1)}, u32[]{:S(2)}, u32[]{:S(2)}) async-start(bf16[16,128,256]{2,1,0:T(8,128)(2,1)} %bitcast.4), calls=%async_computation.3 | async-start | bytes 2097152 | tf_op jit(solution)/shard_map/all_to_all | solution.py:27
  187.4 11.4 %collective-permute-start.6 = (bf16[128,256]{1,0:T(8,128)(2,1)S(1)}, bf16[128,256]{1,0:T(8,128)(2,1)S(1)}, u32[]{:S(2)}, u32[]{:S(2)}) collective-permute-start(bf16[128,256]{1,0:T(8,128)(2,1)S(1)} %slice.70), channel_id=1, source_target_pairs={{0,1},{1,0},{2,3},{3,2},{4,5},{5,4},{6,7},{7,6},{8,9},{9,8},{10,11... | collective-permute-start | bytes 196616 | tf_op jit(solution)/shard_map/ppermute | solution.py:87
  196.9 3.2 %collective-permute-start.7 = (bf16[256,256]{1,0:T(8,128)(2,1)S(1)}, bf16[256,256]{1,0:T(8,128)(2,1)S(1)}, u32[]{:S(2)}, u32[]{:S(2)}) collective-permute-start(bf16[256,256]{1,0:T(8,128)(2,1)S(1)} %slice_select_fusion.1), channel_id=1, source_target_pairs={{0,1},{1,0},{2,3},{3,2},{4,5},{5,4},{6,7},{7,6},{8,9},{9,8},{10,11... | collective-permute-start | bytes 393224 | tf_op jit(solution)/shard_map/ppermute | solution.py:88
  207.0 5.4 %collective-permute-start.5 = (bf16[128,128]{1,0:T(8,128)(2,1)S(1)}, bf16[128,128]{1,0:T(8,128)(2,1)S(1)}, u32[]{:S(2)}, u32[]{:S(2)}) collective-permute-start(bf16[128,128]{1,0:T(8,128)(2,1)S(1)} %slice.67), channel_id=1, source_target_pairs={{0,1},{1,0},{2,3},{3,2},{4,5},{5,4},{6,7},{7,6},{8,9},{9,8},{10,11... | collective-permute-start | bytes 98312 | tf_op jit(solution)/shard_map/ppermute | solution.py:89

commit v2 on v1

v2 whole, which is shorter than its diff:
```python
import jax
import jax.numpy as jnp
from jax import lax
from jax.sharding import Mesh, PartitionSpec as P

ROWS, COLS = ("y", "xh"), ("xl", "z", "c")
ALL = ROWS + COLS
N = 8


def device(y, xh, xl, z, core):
    return (((y * 2 + xh) * 2 + xl) * N + z) * 2 + core


CHIPS = [(y, xh, xl, z) for y in range(N) for xh in (0, 1) for xl in (0, 1) for z in range(N)]


def column_of(y, xh):
    return y // 4, (y % 4) * 2 + xh


def hidden_z(y, xh, token_y):
    return (column_of(y, xh)[1] + token_y - y) % N


def token_place(y, parity, token_y):
    return parity, (column_of(y, parity)[1] + token_y - y) % N


WIDE = [
    [device(y, xh, *token_place(y, xh ^ rel, a), 0) for rel in (0, 1) for a in range(N)]
    for y in range(N)
    for xh in (0, 1)
] + [
    [device(a, xl ^ rel, xl, z, 1) for rel in (0, 1) for a in range(N)] for xl in (0, 1) for z in range(N)
]
NARROW = [[device(a, xh, xl, z, 0) for a in range(N)] for xh in (0, 1) for xl in (0, 1) for z in range(N)] + [
    [device(y, xh, xl, hidden_z(y, xh, a), 1) for a in range(N)] for y in range(N) for xh in (0, 1) for xl in (0, 1)
]

SWAP = [(d, d ^ 1) for d in range(4 * N * N * 2)]
PARTNER = [(device(y, xh, xl, z, 0), device(y, 1 - xh, xl, z, 0)) for y, xh, xl, z in CHIPS] + [
    (device(y, xh, xl, z, 1), device(y, xh, 1 - xl, z, 1)) for y, xh, xl, z in CHIPS
]


def spread(core):
    moves = []
    for y, xh, xl, z in CHIPS:
        column = xl * N + z
        row = column // 2
        moves.append((device(y, xh, xl, z, core), device(row, xh, *token_place(row, column % 2, y), 0)))
        moves.append((device(y, xh, xl, z, 1 - core), device(y, xl, xh, z, 1)))
    return moves


SPREAD_OWN, SPREAD_OTHER = spread(0), spread(1)
CROSS = [
    move
    for y, xh, xl, z in CHIPS
    for a in [(z - column_of(y, xh)[1] + y) % N]
    for here, there in [(device(y, xh, xl, z, 1), device(a, xl, *column_of(y, xh), 0))]
    for move in ((here, there), (there, here))
]
BACK_OWN = [(device(y, xh, xl, z, core), device(y, xl, xh, z, core)) for y, xh, xl, z in CHIPS for core in (0, 1)]
BACK_OTHER = [(device(y, xh, xl, z, core), device(y, xl, xh, z, 1 - core)) for y, xh, xl, z in CHIPS for core in (0, 1)]


def trade(blocks, groups):
    return lax.all_to_all(blocks, ALL, split_axis=0, concat_axis=0, axis_index_groups=groups, tiled=True)


def gather(block, groups):
    return trade(jnp.broadcast_to(block, (len(groups[0]),) + block.shape), groups)


def reduce(partial, groups):
    return jnp.sum(trade(partial.astype(jnp.bfloat16), groups).astype(jnp.float32), axis=0)


def fold(wide):
    half = wide.shape[1] // 2
    return jnp.concatenate([wide[:, :half], wide[:, half:]], axis=0)


def unfold(tall):
    half = tall.shape[0] // 2
    return jnp.concatenate([tall[:half], tall[half:]], axis=1)


def local(tokens, mixer_out, gate_weight, out_weight, out_grad):
    f32, bf16 = jnp.float32, jnp.bfloat16
    first = lax.axis_index("c") == 0
    inner, width = gate_weight.shape[1], out_grad.shape[1]
    own = lax.ppermute(jnp.where(first, tokens, out_grad), ALL, SPREAD_OWN)
    other = lax.ppermute(jnp.where(first, out_grad, tokens), ALL, SPREAD_OTHER)
    acts = gather(jnp.concatenate([own, other], axis=1), WIDE)
    acts = acts.reshape(2, N * acts.shape[1], acts.shape[2])

    out_t = out_weight.T
    weight_in = lax.ppermute(jnp.where(first, fold(out_t), gate_weight), ALL, SWAP)
    weight = jnp.where(
        first,
        jnp.concatenate([gate_weight, weight_in], axis=1),
        jnp.concatenate([out_t, unfold(weight_in)], axis=0),
    )
    weight = jnp.stack([weight, lax.ppermute(weight, ALL, PARTNER)])
    mixer_in = lax.ppermute(mixer_out, ALL, SWAP)
    mixer_vals = jnp.concatenate([mixer_out, mixer_in], axis=1).astype(f32)

    partial = jnp.einsum("kad,kdn->an", acts, weight, preferred_element_type=f32)
    total = reduce(partial.reshape(N, -1, partial.shape[1]), NARROW)

    gate_pre = total
    gate_sig = jax.nn.sigmoid(gate_pre)
    gate_silu = gate_pre * gate_sig
    gated = (mixer_vals * gate_silu).astype(bf16)
    crossed = lax.ppermute(jnp.where(first, gated.astype(f32), total), ALL, CROSS)
    hidden_grad = crossed
    mixer_grad = (hidden_grad * gate_silu).astype(bf16)
    pre_grad = (hidden_grad * mixer_vals * gate_sig * (1.0 + gate_pre * (1.0 - gate_sig))).astype(bf16)
    units = gather(jnp.where(first, pre_grad, crossed.astype(bf16)), NARROW)
    units = units.reshape(-1, units.shape[2])

    layer_part = jnp.einsum("an,kdn->kad", units, weight, preferred_element_type=f32)
    layer_pair = reduce(layer_part.reshape(2 * N, -1, layer_part.shape[2]), WIDE).astype(bf16)
    layer_own = lax.ppermute(layer_pair[:, :width], ALL, BACK_OWN)
    layer_other = lax.ppermute(layer_pair[:, width:], ALL, BACK_OTHER)

    grads = jnp.einsum("kad,an->kdn", acts, units, preferred_element_type=f32)
    grads_in = lax.ppermute(grads[1].astype(bf16), ALL, PARTNER)
    grads = (grads[0] + grads_in.astype(f32)).astype(bf16)

    mixer_grad_in = lax.ppermute(mixer_grad[:, inner:], ALL, SWAP)
    grads_in = lax.ppermute(jnp.where(first, grads[:, inner:], fold(grads[width:])), ALL, SWAP)
    return (
        jnp.where(first, layer_other, layer_own),
        jnp.where(first, mixer_grad[:, :inner], mixer_grad_in),
        jnp.where(first, grads[:, :inner], grads_in),
        jnp.where(first, unfold(grads_in), grads[:width]).T,
    )


def solution(mesh):
    fine = Mesh(mesh.devices.reshape(N, 2, 2, N, 2), ALL)
    spec = P(ROWS, COLS)
    return jax.shard_map(local, mesh=fine, in_specs=(spec,) * 5, out_specs=(spec,) * 4, check_vma=False)
```

time: 214 us -> 169 us (0.79)
  the two profiles are of different devices: /device:TPU:1 before, /device:TPU:11 now
where the time goes in v2:
time: 169 us; the launch traced here: 168 us
  starting transfers between devices  77.2 us (46%)
  waiting for transfers between devices  49.5 us (29%)
  blocking collectives  29.1 us (17%)
  local copies, waits for them, and re-layouts  4.24 us (3%)
  other arithmetic  3.66 us (2%)
  matrix products  3.21 us (2%)
    all_to_all x1, blocking collectives, trade(): lax.all_to_all(blocks, ALL, split_axis=0, concat_axis=0, axis_index_group...  29.1 us
    all_to_all x3, starting transfers between devices, trade(): lax.all_to_all(blocks, ALL, split_axis=0, concat_axis=0, axis_index_group...  21.7 us
    ppermute x1, starting transfers between devices, local(): other = lax.ppermute(jnp.where(first, out_grad, tokens), ALL, SPREAD_OTHER)  17.3 us
    ppermute x1, waiting for transfers between devices, local(): lax.ppermute(jnp.where(first, gated.astype(f32), total), ALL, CROSS)  14.3 us
    all_to_all x3, waiting for transfers between devices, trade(): lax.all_to_all(blocks, ALL, split_axis=0, concat_axis=0, axis_index_group...  12.6 us
    ppermute x1, waiting for transfers between devices, local(): weight = jnp.stack([weight, lax.ppermute(weight, ALL, PARTNER)])  9.61 us
    ppermute x1, starting transfers between devices, local(): mixer_grad_in = lax.ppermute(mixer_grad[:, inner:], ALL, SWAP)  7.76 us
    ppermute x1, waiting for transfers between devices, local(): grads_in = lax.ppermute(grads[1].astype(bf16), ALL, PARTNER)  7.71 us
  transfers between devices with their start and end apart: 14, of which 8 were waited for; matrix products, arithmetic and copies ran while one was open for 2% of the time, Pallas kernels for 0%

profile of v2, /device:TPU:11, one launch (start us, length us, event | category | flops | bytes accessed | tf_op | source)
XLA Modules:
  0.0 167.9 jit_solution(2563523190789643991)
XLA Ops:
  0.6 0.8 broadcast_select_fusion.2
  1.4 3.1 %collective-permute-start.3 = (bf16[128,128]{1,0:T(8,128)(2,1)S(1)}, bf16[128,128]{1,0:T(8,128)(2,1)S(1)}, u32[]{:S(2)}, u32[]{:S(2)}) collective-permute-start(bf16[128,128]{1,0:T(8,128)(2,1)S(1)} %get-tuple-element.22), channel_id=1, source_target_pairs={{0,0},{1,1},{2,18},{3,3},{4,66},{5,5},{6,84},{7,7},{8,132},{9,9},{... | collective-permute-start | bytes 98312 | tf_op jit(solution)/shard_map/ppermute | solution.py:95
  4.5 17.3 %collective-permute-start.4 = (bf16[128,128]{1,0:T(8,128)(2,1)S(1)}, bf16[128,128]{1,0:T(8,128)(2,1)S(1)}, u32[]{:S(2)}, u32[]{:S(2)}) collective-permute-start(bf16[128,128]{1,0:T(8,128)(2,1)S(1)} %get-tuple-element.23), channel_id=1, source_target_pairs={{1,0},{0,1},{3,18},{2,3},{5,66},{4,5},{7,84},{6,7},{9,132},{8,9},{... | collective-permute-start | bytes 98312 | tf_op jit(solution)/shard_map/ppermute | solution.py:96
  21.8 0.0 collective-permute-done.3
  21.9 1.1 collective-permute-done.4
  23.0 1.1 broadcast_in_dim.6
  24.1 0.0 copy-start
  24.1 5.6 %all-to-all-start = ((bf16[16,128,256]{2,1,0:T(8,128)(2,1)}), bf16[16,128,256]{2,1,0:T(8,128)(2,1)S(1)}, u32[]{:S(2)}, u32[]{:S(2)}) async-start(bf16[16,128,256]{2,1,0:T(8,128)(2,1)} %broadcast_in_dim.6), calls=%async_computation | async-start | bytes 2097152 | tf_op jit(solution)/shard_map/all_to_all | solution.py:70
  29.7 0.0 copy-done.6
  29.7 0.1 copy.11
  29.9 0.0 copy-done
  29.9 6.8 %collective-permute-start = (bf16[256,256]{1,0:T(8,128)(2,1)S(1)}, bf16[256,256]{1,0:T(8,128)(2,1)S(1)}, u32[]{:S(2)}, u32[]{:S(2)}) collective-permute-start(bf16[256,256]{1,0:T(8,128)(2,1)S(1)} %maximum_select_fusion.2), channel_id=1, source_target_pairs={{0,1},{1,0},{2,3},{3,2},{4,5},{5,4},{6,7},{7,6},{8,9},{9,8},{10,11... | collective-permute-start | bytes 393224 | tf_op jit(solution)/shard_map/ppermute | solution.py:101
  36.7 1.0 collective-permute-done
  37.7 0.1 maximum_select_fusion.1
  37.7 2.2 %collective-permute-start.1 = (bf16[256,512]{1,0:T(8,128)(2,1)S(1)}, bf16[256,512]{1,0:T(8,128)(2,1)S(1)}, u32[]{:S(2)}, u32[]{:S(2)}) collective-permute-start(bf16[256,512]{1,0:T(8,128)(2,1)S(1)} %maximum_select_fusion.1), channel_id=1, source_target_pairs={{0,32},{2,34},{4,36},{6,38},{8,40},{10,42},{12,44},{14,46},{16,48}... | collective-permute-start | bytes 786440 | tf_op jit(solution)/shard_map/ppermute | solution.py:107
  39.9 0.1 maximum_select_fusion
  40.0 0.0 copy-start.3
  40.0 9.6 %collective-permute-done.1 = bf16[256,512]{1,0:T(8,128)(2,1)S(1)} collective-permute-done((bf16[256,512]{1,0:T(8,128)(2,1)S(1)}, bf16[256,512]{1,0:T(8,128)(2,1)S(1)}, u32[]{:S(2)}, u32[]{:S(2)}) %collective-permute-start.1) | collective-permute-done | bytes 262176 | tf_op jit(solution)/shard_map/ppermute | solution.py:107
  49.6 0.0 copy-start.7
  49.6 0.0 all-to-all-done
  49.6 1.7 %bitcast_convert_fusion = bf16[8,128,512]{2,1,0:T(8,128)(2,1)} fusion(bf16[8,128,256,2]{2,1,0,3:T(8,128)(2,1)S(1)} %bitcast.45, bf16[1,256,512]{2,1,0:T(8,128)(2,1)S(1)} %bitcast.49, bf16[1,256,512]{2,1,0:T(8,128)(2,1)S(1)} %maximum_select_fusion), kind=kOutput, calls=%fused_computation | convolution fusion | flops 537657344 | bytes 2621440 | tf_op jit(solution)/shard_map/kad,kdn->an/dot_general | solution.py:111
  51.4 0.0 copy-done.3
  51.4 0.0 copy-done.7
  51.4 0.0 copy-start.5
  51.4 8.1 %all-to-all-start.1 = ((bf16[8,128,512]{2,1,0:T(8,128)(2,1)}), bf16[8,128,512]{2,1,0:T(8,128)(2,1)S(1)}, u32[]{:S(2)}, u32[]{:S(2)}) async-start(bf16[8,128,512]{2,1,0:T(8,128)(2,1)} %bitcast_convert_fusion), calls=%async_computation.1 | async-start | bytes 2097152 | tf_op jit(solution)/shard_map/all_to_all | solution.py:70
  59.5 0.0 copy-done.5
  59.5 4.3 %collective-permute-start.2 = (bf16[128,256]{1,0:T(8,128)(2,1)S(1)}, bf16[128,256]{1,0:T(8,128)(2,1)S(1)}, u32[]{:S(2)}, u32[]{:S(2)}) collective-permute-start(bf16[128,256]{1,0:T(8,128)(2,1)S(1)} %copy-done.5), channel_id=1, source_target_pairs={{0,1},{1,0},{2,3},{3,2},{4,5},{5,4},{6,7},{7,6},{8,9},{9,8},{10,11... | collective-permute-start | bytes 196616 | tf_op jit(solution)/shard_map/ppermute | solution.py:108
  63.8 12.6 %all-to-all-done.1 = bf16[8,128,512]{2,1,0:T(8,128)(2,1)S(1)} async-done(((bf16[8,128,512]{2,1,0:T(8,128)(2,1)}), bf16[8,128,512]{2,1,0:T(8,128)(2,1)S(1)}, u32[]{:S(2)}, u32[]{:S(2)}) %all-to-all-start.1) | async-done | bytes 1048608 | tf_op jit(solution)/shard_map/all_to_all | solution.py:70
  76.4 0.1 convert_reduce_fusion
  76.6 0.0 collective-permute-done.2
  76.6 0.1 convert_select_fusion
  76.7 2.8 %collective-permute-start.5 = (f32[128,512]{1,0:T(8,128)S(1)}, f32[128,512]{1,0:T(8,128)S(1)}, u32[]{:S(2)}, u32[]{:S(2)}) collective-permute-start(f32[128,512]{1,0:T(8,128)S(1)} %convert_select_fusion), channel_id=1, source_target_pairs={{1,0},{0,1},{3,64},{64,3},{5,128},{128,5},{7,192},{192,7},{9,256},... | collective-permute-start | bytes 786440 | tf_op jit(solution)/shard_map/ppermute | solution.py:118
  79.5 14.3 %collective-permute-done.5 = f32[128,512]{1,0:T(8,128)S(1)} collective-permute-done((f32[128,512]{1,0:T(8,128)S(1)}, f32[128,512]{1,0:T(8,128)S(1)}, u32[]{:S(2)}, u32[]{:S(2)}) %collective-permute-start.5) | collective-permute-done | bytes 262176 | tf_op jit(solution)/shard_map/ppermute | solution.py:118
  93.9 0.7 copy-done.1
  94.6 0.1 convert_select_fusion.1
  94.7 0.1 broadcast_in_dim.7
  94.8 0.0 copy-start.4
  94.8 0.0 copy-start.8
  94.8 29.1 %all_to_all.20 = bf16[8,128,512]{2,1,0:T(8,128)(2,1)S(1)} all-to-all(bf16[8,128,512]{2,1,0:T(8,128)(2,1)S(1)} %broadcast_in_dim.7), channel_id=1, replica_groups={{0,64,128,192,256,320,384,448},{2,66,130,194,258,322,386,450},{4,68,132..., dimensions={0} | all-to-all | bytes 2097152 | tf_op jit(solution)/shard_map/all_to_all | solution.py:70
  123.9 0.0 copy-done.4
  123.9 0.0 copy-done.8
  123.9 0.7 fusion
  124.7 1.3 copy.13
  126.0 7.9 %all-to-all-start.3 = ((bf16[16,128,256]{2,1,0:T(8,128)(2,1)}), bf16[16,128,256]{2,1,0:T(8,128)(2,1)S(1)}, u32[]{:S(2)}, u32[]{:S(2)}) async-start(bf16[16,128,256]{2,1,0:T(8,128)(2,1)} %bitcast.15), calls=%async_computation.3 | async-start | bytes 2097152 | tf_op jit(solution)/shard_map/all_to_all | solution.py:70
  134.0 0.7 fusion.18
  134.7 1.9 %collective-permute-start.9 = (bf16[256,512]{1,0:T(8,128)(2,1)S(1)}, bf16[256,512]{1,0:T(8,128)(2,1)S(1)}, u32[]{:S(2)}, u32[]{:S(2)}) collective-permute-start(bf16[256,512]{1,0:T(8,128)(2,1)S(1)} %fusion.8), channel_id=1, source_target_pairs={{0,32},{2,34},{4,36},{6,38},{8,40},{10,42},{12,44},{14,46},{16,48}... | collective-permute-start | bytes 786440 | tf_op jit(solution)/shard_map/ppermute | solution.py:131
  136.7 0.0 copy-done.2
  136.7 0.1 multiply_convert_fusion
  136.8 7.8 %collective-permute-start.8 = (bf16[128,256]{1,0:T(8,128)(2,1)S(1)}, bf16[128,256]{1,0:T(8,128)(2,1)S(1)}, u32[]{:S(2)}, u32[]{:S(2)}) collective-permute-start(bf16[128,256]{1,0:T(8,128)(2,1)S(1)} %slice.79), channel_id=1, source_target_pairs={{0,1},{1,0},{2,3},{3,2},{4,5},{5,4},{6,7},{7,6},{8,9},{9,8},{10,11... | collective-permute-start | bytes 196616 | tf_op jit(solution)/shard_map/ppermute | solution.py:134
  144.5 7.7 %collective-permute-done.9 = bf16[256,512]{1,0:T(8,128)(2,1)S(1)} collective-permute-done((bf16[256,512]{1,0:T(8,128)(2,1)S(1)}, bf16[256,512]{1,0:T(8,128)(2,1)S(1)}, u32[]{:S(2)}, u32[]{:S(2)}) %collective-permute-start.9) | collective-permute-done | bytes 262176 | tf_op jit(solution)/shard_map/ppermute | solution.py:131
  152.2 0.1 fusion.2
  152.4 3.1 %collective-permute-start.10 = (bf16[256,256]{1,0:T(8,128)(2,1)S(1)}, bf16[256,256]{1,0:T(8,128)(2,1)S(1)}, u32[]{:S(2)}, u32[]{:S(2)}) collective-permute-start(bf16[256,256]{1,0:T(8,128)(2,1)S(1)} %slice_select_fusion.1), channel_id=1, source_target_pairs={{0,1},{1,0},{2,3},{3,2},{4,5},{5,4},{6,7},{7,6},{8,9},{9,8},{10,11... | collective-permute-start | bytes 393224 | tf_op jit(solution)/shard_map/ppermute | solution.py:135
  155.5 0.0 collective-permute-done.8
  155.5 0.6 slice_select_fusion.3
  156.2 0.3 collective-permute-done.10
  156.5 0.7 slice_select_fusion.2
  157.2 0.0 all-to-all-done.3
  157.2 0.1 reduce_sum.22
  157.3 4.1 %collective-permute-start.7 = (bf16[128,128]{1,0:T(8,128)(2,1)S(1)}, bf16[128,128]{1,0:T(8,128)(2,1)S(1)}, u32[]{:S(2)}, u32[]{:S(2)}) collective-permute-start(bf16[128,128]{1,0:T(8,128)(2,1)S(1)} %get-tuple-element.20), channel_id=1, source_target_pairs={{0,0},{1,1},{2,2},{3,3},{4,4},{5,5},{6,6},{7,7},{8,8},{9,9},{10,10... | collective-permute-start | bytes 98312 | tf_op jit(solution)/shard_map/ppermute | solution.py:127
  161.4 2.2 %collective-permute-start.6 = (bf16[128,128]{1,0:T(8,128)(2,1)S(1)}, bf16[128,128]{1,0:T(8,128)(2,1)S(1)}, u32[]{:S(2)}, u32[]{:S(2)}) collective-permute-start(bf16[128,128]{1,0:T(8,128)(2,1)S(1)} %get-tuple-element.21), channel_id=1, source_target_pairs={{0,1},{1,0},{2,3},{3,2},{4,5},{5,4},{6,7},{7,6},{8,9},{9,8},{10,11... | collective-permute-start | bytes 98312 | tf_op jit(solution)/shard_map/ppermute | solution.py:128
  163.7 0.8 copy.15
  164.4 0.0 collective-permute-done.7
  164.4 2.8 %collective-permute-done.6 = bf16[128,128]{1,0:T(8,128)(2,1)S(1)} collective-permute-done((bf16[128,128]{1,0:T(8,128)(2,1)S(1)}, bf16[128,128]{1,0:T(8,128)(2,1)S(1)}, u32[]{:S(2)}, u32[]{:S(2)}) %collective-permute-start.6) | collective-permute-done | bytes 32800 | tf_op jit(solution)/shard_map/ppermute | solution.py:128
  167.2 0.6 broadcast_select_fusion
  (15 shorter events, 0.2 us)
Async XLA Ops:
  1.4 20.4 %collective-permute-start.3 = (bf16[128,128]{1,0:T(8,128)(2,1)S(1)}, bf16[128,128]{1,0:T(8,128)(2,1)S(1)}, u32[]{:S(2)}, u32[]{:S(2)}) collective-permute-start(bf16[128,128]{1,0:T(8,128)(2,1)S(1)} %get-tuple-element.22), channel_id=1, source_target_pairs={{0,0},{1,1},{2,18},{3,3},{4,66},{5,5},{6,84},{7,7},{8,132},{9,9},{... | collective-permute-start | bytes 98312 | tf_op jit(solution)/shard_map/ppermute | solution.py:95
  4.5 18.5 %collective-permute-start.4 = (bf16[128,128]{1,0:T(8,128)(2,1)S(1)}, bf16[128,128]{1,0:T(8,128)(2,1)S(1)}, u32[]{:S(2)}, u32[]{:S(2)}) collective-permute-start(bf16[128,128]{1,0:T(8,128)(2,1)S(1)} %get-tuple-element.23), channel_id=1, source_target_pairs={{1,0},{0,1},{3,18},{2,3},{5,66},{4,5},{7,84},{6,7},{9,132},{8,9},{... | collective-permute-start | bytes 98312 | tf_op jit(solution)/shard_map/ppermute | solution.py:96
  24.1 5.6 %copy-start.6 = (bf16[512,128]{1,0:T(8,128)(2,1)S(1)}, bf16[512,128]{1,0:T(8,128)(2,1)}, u32[]{:S(2)}) copy-start(bf16[512,128]{1,0:T(8,128)(2,1)} %param.8) | copy-start | bytes 393220
  24.1 5.7 %copy-start = (bf16[256,256]{1,0:T(8,128)(2,1)S(1)}, bf16[256,256]{1,0:T(8,128)(2,1)}, u32[]{:S(2)}) copy-start(bf16[256,256]{1,0:T(8,128)(2,1)} %param.7) | copy-start | bytes 393220
  24.1 25.5 %all-to-all-start = ((bf16[16,128,256]{2,1,0:T(8,128)(2,1)}), bf16[16,128,256]{2,1,0:T(8,128)(2,1)S(1)}, u32[]{:S(2)}, u32[]{:S(2)}) async-start(bf16[16,128,256]{2,1,0:T(8,128)(2,1)} %broadcast_in_dim.6), calls=%async_computation | async-start | bytes 2097152 | tf_op jit(solution)/shard_map/all_to_all | solution.py:70
  29.9 7.7 %collective-permute-start = (bf16[256,256]{1,0:T(8,128)(2,1)S(1)}, bf16[256,256]{1,0:T(8,128)(2,1)S(1)}, u32[]{:S(2)}, u32[]{:S(2)}) collective-permute-start(bf16[256,256]{1,0:T(8,128)(2,1)S(1)} %maximum_select_fusion.2), channel_id=1, source_target_pairs={{0,1},{1,0},{2,3},{3,2},{4,5},{5,4},{6,7},{7,6},{8,9},{9,8},{10,11... | collective-permute-start | bytes 393224 | tf_op jit(solution)/shard_map/ppermute | solution.py:101
  37.7 11.9 %collective-permute-start.1 = (bf16[256,512]{1,0:T(8,128)(2,1)S(1)}, bf16[256,512]{1,0:T(8,128)(2,1)S(1)}, u32[]{:S(2)}, u32[]{:S(2)}) collective-permute-start(bf16[256,512]{1,0:T(8,128)(2,1)S(1)} %maximum_select_fusion.1), channel_id=1, source_target_pairs={{0,32},{2,34},{4,36},{6,38},{8,40},{10,42},{12,44},{14,46},{16,48}... | collective-permute-start | bytes 786440 | tf_op jit(solution)/shard_map/ppermute | solution.py:107
  40.0 11.4 %copy-start.3 = (bf16[1,256,512]{2,1,0:T(8,128)(2,1)}, bf16[1,256,512]{2,1,0:T(8,128)(2,1)S(1)}, u32[]{:S(2)}) copy-start(bf16[1,256,512]{2,1,0:T(8,128)(2,1)S(1)} %maximum_select_fusion) | copy-start | bytes 786436
  49.6 1.7 %copy-start.7 = (bf16[256,512]{1,0:T(8,128)(2,1)}, bf16[256,512]{1,0:T(8,128)(2,1)S(1)}, u32[]{:S(2)}) copy-start(bf16[256,512]{1,0:T(8,128)(2,1)S(1)} %collective-permute-done.1) | copy-start | bytes 786436
  51.4 8.2 %copy-start.5 = (bf16[128,256]{1,0:T(8,128)(2,1)S(1)}, bf16[128,256]{1,0:T(8,128)(2,1)}, u32[]{:S(2)}) copy-start(bf16[128,256]{1,0:T(8,128)(2,1)} %param.6) | copy-start | bytes 196612
  51.4 25.0 %all-to-all-start.1 = ((bf16[8,128,512]{2,1,0:T(8,128)(2,1)}), bf16[8,128,512]{2,1,0:T(8,128)(2,1)S(1)}, u32[]{:S(2)}, u32[]{:S(2)}) async-start(bf16[8,128,512]{2,1,0:T(8,128)(2,1)} %bitcast_convert_fusion), calls=%async_computation.1 | async-start | bytes 2097152 | tf_op jit(solution)/shard_map/all_to_all | solution.py:70
  59.5 17.0 %collective-permute-start.2 = (bf16[128,256]{1,0:T(8,128)(2,1)S(1)}, bf16[128,256]{1,0:T(8,128)(2,1)S(1)}, u32[]{:S(2)}, u32[]{:S(2)}) collective-permute-start(bf16[128,256]{1,0:T(8,128)(2,1)S(1)} %copy-done.5), channel_id=1, source_target_pairs={{0,1},{1,0},{2,3},{3,2},{4,5},{5,4},{6,7},{7,6},{8,9},{9,8},{10,11... | collective-permute-start | bytes 196616 | tf_op jit(solution)/shard_map/ppermute | solution.py:108
  76.7 17.2 %collective-permute-start.5 = (f32[128,512]{1,0:T(8,128)S(1)}, f32[128,512]{1,0:T(8,128)S(1)}, u32[]{:S(2)}, u32[]{:S(2)}) collective-permute-start(f32[128,512]{1,0:T(8,128)S(1)} %convert_select_fusion), channel_id=1, source_target_pairs={{1,0},{0,1},{3,64},{64,3},{5,128},{128,5},{7,192},{192,7},{9,256},... | collective-permute-start | bytes 786440 | tf_op jit(solution)/shard_map/ppermute | solution.py:118
  93.9 0.7 copy-start.1
  94.8 29.1 %copy-start.4 = (bf16[1,256,512]{2,1,0:T(8,128)(2,1)S(1)}, bf16[1,256,512]{2,1,0:T(8,128)(2,1)}, u32[]{:S(2)}) copy-start(bf16[1,256,512]{2,1,0:T(8,128)(2,1)} %copy-done.3) | copy-start | bytes 786436
  94.8 29.1 %copy-start.8 = (bf16[256,512]{1,0:T(8,128)(2,1)S(1)}, bf16[256,512]{1,0:T(8,128)(2,1)}, u32[]{:S(2)}) copy-start(bf16[256,512]{1,0:T(8,128)(2,1)} %copy-done.7) | copy-start | bytes 786436
  126.0 31.2 %all-to-all-start.3 = ((bf16[16,128,256]{2,1,0:T(8,128)(2,1)}), bf16[16,128,256]{2,1,0:T(8,128)(2,1)S(1)}, u32[]{:S(2)}, u32[]{:S(2)}) async-start(bf16[16,128,256]{2,1,0:T(8,128)(2,1)} %bitcast.15), calls=%async_computation.3 | async-start | bytes 2097152 | tf_op jit(solution)/shard_map/all_to_all | solution.py:70
  133.9 2.7 %copy-start.2 = (f32[128,512]{1,0:T(8,128)S(1)}, f32[128,512]{1,0:T(8,128)}, u32[]{:S(2)}) copy-start(f32[128,512]{1,0:T(8,128)} %copy-done.1) | copy-start | bytes 786436
  134.7 17.5 %collective-permute-start.9 = (bf16[256,512]{1,0:T(8,128)(2,1)S(1)}, bf16[256,512]{1,0:T(8,128)(2,1)S(1)}, u32[]{:S(2)}, u32[]{:S(2)}) collective-permute-start(bf16[256,512]{1,0:T(8,128)(2,1)S(1)} %fusion.8), channel_id=1, source_target_pairs={{0,32},{2,34},{4,36},{6,38},{8,40},{10,42},{12,44},{14,46},{16,48}... | collective-permute-start | bytes 786440 | tf_op jit(solution)/shard_map/ppermute | solution.py:131
  136.8 18.8 %collective-permute-start.8 = (bf16[128,256]{1,0:T(8,128)(2,1)S(1)}, bf16[128,256]{1,0:T(8,128)(2,1)S(1)}, u32[]{:S(2)}, u32[]{:S(2)}) collective-permute-start(bf16[128,256]{1,0:T(8,128)(2,1)S(1)} %slice.79), channel_id=1, source_target_pairs={{0,1},{1,0},{2,3},{3,2},{4,5},{5,4},{6,7},{7,6},{8,9},{9,8},{10,11... | collective-permute-start | bytes 196616 | tf_op jit(solution)/shard_map/ppermute | solution.py:134
  152.4 4.1 %collective-permute-start.10 = (bf16[256,256]{1,0:T(8,128)(2,1)S(1)}, bf16[256,256]{1,0:T(8,128)(2,1)S(1)}, u32[]{:S(2)}, u32[]{:S(2)}) collective-permute-start(bf16[256,256]{1,0:T(8,128)(2,1)S(1)} %slice_select_fusion.1), channel_id=1, source_target_pairs={{0,1},{1,0},{2,3},{3,2},{4,5},{5,4},{6,7},{7,6},{8,9},{9,8},{10,11... | collective-permute-start | bytes 393224 | tf_op jit(solution)/shard_map/ppermute | solution.py:135
  157.3 7.1 %collective-permute-start.7 = (bf16[128,128]{1,0:T(8,128)(2,1)S(1)}, bf16[128,128]{1,0:T(8,128)(2,1)S(1)}, u32[]{:S(2)}, u32[]{:S(2)}) collective-permute-start(bf16[128,128]{1,0:T(8,128)(2,1)S(1)} %get-tuple-element.20), channel_id=1, source_target_pairs={{0,0},{1,1},{2,2},{3,3},{4,4},{5,5},{6,6},{7,7},{8,8},{9,9},{10,10... | collective-permute-start | bytes 98312 | tf_op jit(solution)/shard_map/ppermute | solution.py:127
  161.4 5.8 %collective-permute-start.6 = (bf16[128,128]{1,0:T(8,128)(2,1)S(1)}, bf16[128,128]{1,0:T(8,128)(2,1)S(1)}, u32[]{:S(2)}, u32[]{:S(2)}) collective-permute-start(bf16[128,128]{1,0:T(8,128)(2,1)S(1)} %get-tuple-element.21), channel_id=1, source_target_pairs={{0,1},{1,0},{2,3},{3,2},{4,5},{5,4},{6,7},{7,6},{8,9},{9,8},{10,11... | collective-permute-start | bytes 98312 | tf_op jit(solution)/shard_map/ppermute | solution.py:128

commit v3 on v2

--- a/solution.py
+++ b/solution.py
@@ -20,11 +20,11 @@
 
 
 def hidden_z(y, xh, token_y):
-    return (column_of(y, xh)[1] + token_y - y) % N
+    return (column_of(y, xh)[1] + token_y - y + N // 2) % N
 
 
 def token_place(y, parity, token_y):
-    return parity, (column_of(y, parity)[1] + token_y - y) % N
+    return parity, (column_of(y, parity)[1] + token_y - y + N // 2) % N
 
 
 WIDE = [
@@ -42,6 +42,9 @@
 PARTNER = [(device(y, xh, xl, z, 0), device(y, 1 - xh, xl, z, 0)) for y, xh, xl, z in CHIPS] + [
     (device(y, xh, xl, z, 1), device(y, xh, 1 - xl, z, 1)) for y, xh, xl, z in CHIPS
 ]
+PARTNER_SWAP = [(device(y, xh, xl, z, 1), device(y, 1 - xh, xl, z, 0)) for y, xh, xl, z in CHIPS] + [
+    (device(y, xh, xl, z, 0), device(y, xh, 1 - xl, z, 1)) for y, xh, xl, z in CHIPS
+]
 
 
 def spread(core):
@@ -58,7 +61,7 @@
 CROSS = [
     move
     for y, xh, xl, z in CHIPS
-    for a in [(z - column_of(y, xh)[1] + y) % N]
+    for a in [(z - column_of(y, xh)[1] + y + N // 2) % N]
     for here, there in [(device(y, xh, xl, z, 1), device(a, xl, *column_of(y, xh), 0))]
     for move in ((here, there), (there, here))
 ]
@@ -98,13 +101,22 @@
     acts = acts.reshape(2, N * acts.shape[1], acts.shape[2])
 
     out_t = out_weight.T
-    weight_in = lax.ppermute(jnp.where(first, fold(out_t), gate_weight), ALL, SWAP)
-    weight = jnp.where(
-        first,
-        jnp.concatenate([gate_weight, weight_in], axis=1),
-        jnp.concatenate([out_t, unfold(weight_in)], axis=0),
+    mine = jnp.where(first, gate_weight, fold(out_t))
+    yours = jnp.where(first, fold(out_t), gate_weight)
+    blocks = [
+        (mine, lax.ppermute(yours, ALL, SWAP)),
+        (lax.ppermute(mine, ALL, PARTNER), lax.ppermute(yours, ALL, PARTNER_SWAP)),
+    ]
+    weight = jnp.stack(
+        [
+            jnp.where(
+                first,
+                jnp.concatenate(pair, axis=1),
+                jnp.concatenate([unfold(block) for block in pair], axis=0),
+            )
+            for pair in blocks
+        ]
     )
-    weight = jnp.stack([weight, lax.ppermute(weight, ALL, PARTNER)])
     mixer_in = lax.ppermute(mixer_out, ALL, SWAP)
     mixer_vals = jnp.concatenate([mixer_out, mixer_in], axis=1).astype(f32)
 
@@ -115,23 +127,25 @@
     gate_sig = jax.nn.sigmoid(gate_pre)
     gate_silu = gate_pre * gate_sig
     gated = (mixer_vals * gate_silu).astype(bf16)
-    crossed = lax.ppermute(jnp.where(first, gated.astype(f32), total), ALL, CROSS)
-    hidden_grad = crossed
+    crossed = lax.ppermute(jnp.where(first, gated, total.astype(bf16)), ALL, CROSS)
+    hidden_grad = crossed.astype(f32)
     mixer_grad = (hidden_grad * gate_silu).astype(bf16)
     pre_grad = (hidden_grad * mixer_vals * gate_sig * (1.0 + gate_pre * (1.0 - gate_sig))).astype(bf16)
-    units = gather(jnp.where(first, pre_grad, crossed.astype(bf16)), NARROW)
+    units = gather(jnp.where(first, pre_grad, crossed), NARROW)
+    mixer_grad_in = lax.ppermute(mixer_grad[:, inner:], ALL, SWAP)
+    units, mixer_grad_in = lax.optimization_barrier((units, mixer_grad_in))
     units = units.reshape(-1, units.shape[2])
+
+    grads = jnp.einsum("kad,an->kdn", acts, units, preferred_element_type=f32)
+    units, grads_out = lax.optimization_barrier((units, grads[1].astype(bf16)))
+    grads_in = lax.ppermute(grads_out, ALL, PARTNER)
 
     layer_part = jnp.einsum("an,kdn->kad", units, weight, preferred_element_type=f32)
     layer_pair = reduce(layer_part.reshape(2 * N, -1, layer_part.shape[2]), WIDE).astype(bf16)
     layer_own = lax.ppermute(layer_pair[:, :width], ALL, BACK_OWN)
     layer_other = lax.ppermute(layer_pair[:, width:], ALL, BACK_OTHER)
 
-    grads = jnp.einsum("kad,an->kdn", acts, units, preferred_element_type=f32)
-    grads_in = lax.ppermute(grads[1].astype(bf16), ALL, PARTNER)
     grads = (grads[0] + grads_in.astype(f32)).astype(bf16)
-
-    mixer_grad_in = lax.ppermute(mixer_grad[:, inner:], ALL, SWAP)
     grads_in = lax.ppermute(jnp.where(first, grads[:, inner:], fold(grads[width:])), ALL, SWAP)
     return (
         jnp.where(first, layer_other, layer_own),

time: 169 us -> 159 us (0.941)
  the two profiles are of different devices: /device:TPU:11 before, /device:TPU:12 now
where the time goes in v3:
time: 159 us; the launch traced here: 158 us
  starting transfers between devices  82.9 us (52%)
  waiting for transfers between devices  61.4 us (39%)
  local copies, waits for them, and re-layouts  6.12 us (4%)
  other arithmetic  3.68 us (2%)
  matrix products  3.17 us (2%)
    all_to_all x4, starting transfers between devices, trade(): lax.all_to_all(blocks, ALL, split_axis=0, concat_axis=0, axis_index_group...  34.2 us
    all_to_all x4, waiting for transfers between devices, trade(): lax.all_to_all(blocks, ALL, split_axis=0, concat_axis=0, axis_index_group...  19.9 us
    ppermute x1, waiting for transfers between devices, local(): grads_in = lax.ppermute(grads_out, ALL, PARTNER)  15.7 us
    ppermute x1, starting transfers between devices, local(): mixer_grad_in = lax.ppermute(mixer_grad[:, inner:], ALL, SWAP)  11.2 us
    ppermute x1, starting transfers between devices, local(): own = lax.ppermute(jnp.where(first, tokens, out_grad), ALL, SPREAD_OWN)  10.8 us
    ppermute x1, waiting for transfers between devices, local(): lax.ppermute(jnp.where(first, gated, total.astype(bf16)), ALL, CROSS)  8.29 us
    ppermute x1, waiting for transfers between devices, local(): lax.ppermute(mine, ALL, PARTNER)  7.94 us
    ppermute x1, waiting for transfers between devices, local(): other = lax.ppermute(jnp.where(first, out_grad, tokens), ALL, SPREAD_OTHER)  5.17 us
  transfers between devices with their start and end apart: 16, of which 9 were waited for; matrix products, arithmetic and copies ran while one was open for 2% of the time, Pallas kernels for 0%

profile of v3, /device:TPU:12, one launch (start us, length us, event | category | flops | bytes accessed | tf_op | source)
XLA Modules:
  0.0 158.3 jit_solution(2466441092814428043)
XLA Ops:
  0.6 0.8 broadcast_select_fusion.4
  1.4 10.8 %collective-permute-start.4 = (bf16[128,128]{1,0:T(8,128)(2,1)S(1)}, bf16[128,128]{1,0:T(8,128)(2,1)S(1)}, u32[]{:S(2)}, u32[]{:S(2)}) collective-permute-start(bf16[128,128]{1,0:T(8,128)(2,1)S(1)} %get-tuple-element.38), channel_id=1, source_target_pairs={{0,8},{1,1},{2,26},{3,3},{4,74},{5,5},{6,92},{7,7},{8,140},{9,9},{... | collective-permute-start | bytes 98312 | tf_op jit(solution)/shard_map/ppermute | solution.py:98
  12.2 1.9 %collective-permute-start.5 = (bf16[128,128]{1,0:T(8,128)(2,1)S(1)}, bf16[128,128]{1,0:T(8,128)(2,1)S(1)}, u32[]{:S(2)}, u32[]{:S(2)}) collective-permute-start(bf16[128,128]{1,0:T(8,128)(2,1)S(1)} %get-tuple-element.39), channel_id=1, source_target_pairs={{1,8},{0,1},{3,26},{2,3},{5,74},{4,5},{7,92},{6,7},{9,140},{8,9},{... | collective-permute-start | bytes 98312 | tf_op jit(solution)/shard_map/ppermute | solution.py:99
  14.2 1.0 copy.11
  15.2 0.0 collective-permute-done.4
  15.2 5.2 %collective-permute-done.5 = bf16[128,128]{1,0:T(8,128)(2,1)S(1)} collective-permute-done((bf16[128,128]{1,0:T(8,128)(2,1)S(1)}, bf16[128,128]{1,0:T(8,128)(2,1)S(1)}, u32[]{:S(2)}, u32[]{:S(2)}) %collective-permute-start.5) | collective-permute-done | bytes 32800 | tf_op jit(solution)/shard_map/ppermute | solution.py:99
  20.4 1.1 broadcast_in_dim.6
  21.4 10.1 %all-to-all-start = ((bf16[16,128,256]{2,1,0:T(8,128)(2,1)}), bf16[16,128,256]{2,1,0:T(8,128)(2,1)S(1)}, u32[]{:S(2)}, u32[]{:S(2)}) async-start(bf16[16,128,256]{2,1,0:T(8,128)(2,1)} %broadcast_in_dim.6), calls=%async_computation | async-start | bytes 2097152 | tf_op jit(solution)/shard_map/all_to_all | solution.py:73
  31.5 0.0 copy-done.6
  31.6 1.9 %collective-permute-start.2 = (bf16[256,256]{1,0:T(8,128)(2,1)S(1)}, bf16[256,256]{1,0:T(8,128)(2,1)S(1)}, u32[]{:S(2)}, u32[]{:S(2)}) collective-permute-start(bf16[256,256]{1,0:T(8,128)(2,1)S(1)} %get-tuple-element.23), channel_id=1, source_target_pairs={{1,32},{3,34},{5,36},{7,38},{9,40},{11,42},{13,44},{15,46},{17,48}... | collective-permute-start | bytes 393224 | tf_op jit(solution)/shard_map/ppermute | solution.py:108
  33.5 2.8 %collective-permute-start = (bf16[256,256]{1,0:T(8,128)(2,1)S(1)}, bf16[256,256]{1,0:T(8,128)(2,1)S(1)}, u32[]{:S(2)}, u32[]{:S(2)}) collective-permute-start(bf16[256,256]{1,0:T(8,128)(2,1)S(1)} %get-tuple-element.23), channel_id=1, source_target_pairs={{0,1},{1,0},{2,3},{3,2},{4,5},{5,4},{6,7},{7,6},{8,9},{9,8},{10,11... | collective-permute-start | bytes 393224 | tf_op jit(solution)/shard_map/ppermute | solution.py:107
  36.3 4.7 %collective-permute-start.1 = (bf16[256,256]{1,0:T(8,128)(2,1)S(1)}, bf16[256,256]{1,0:T(8,128)(2,1)S(1)}, u32[]{:S(2)}, u32[]{:S(2)}) collective-permute-start(bf16[256,256]{1,0:T(8,128)(2,1)S(1)} %get-tuple-element.22), channel_id=1, source_target_pairs={{0,32},{2,34},{4,36},{6,38},{8,40},{10,42},{12,44},{14,46},{16,48}... | collective-permute-start | bytes 393224 | tf_op jit(solution)/shard_map/ppermute | solution.py:108
  41.0 7.9 %collective-permute-done.1 = bf16[256,256]{1,0:T(8,128)(2,1)S(1)} collective-permute-done((bf16[256,256]{1,0:T(8,128)(2,1)S(1)}, bf16[256,256]{1,0:T(8,128)(2,1)S(1)}, u32[]{:S(2)}, u32[]{:S(2)}) %collective-permute-start.1) | collective-permute-done | bytes 131104 | tf_op jit(solution)/shard_map/ppermute | solution.py:108
  49.0 0.0 collective-permute-done.2
  49.0 0.0 collective-permute-done
  49.1 0.1 maximum_select_fusion.1
  49.2 0.0 copy-start.2
  49.2 0.1 maximum_select_fusion
  49.2 0.0 copy-start.4
  49.2 0.0 all-to-all-done
  49.3 1.7 %bitcast_convert_fusion = bf16[8,128,512]{2,1,0:T(8,128)(2,1)} fusion(bf16[8,128,256,2]{2,1,0,3:T(8,128)(2,1)S(1)} %bitcast.48, bf16[1,256,512]{2,1,0:T(8,128)(2,1)S(1)} %maximum_select_fusion.1, bf16[1,256,512]{2,1,0:T(8,128)(2,1)S(1)} %maximum_select_fusion), kind=kOutput, calls=%fused_computation | convolution fusion | flops 537657344 | bytes 2621440 | tf_op jit(solution)/shard_map/kad,kdn->an/dot_general | solution.py:123
  51.0 0.0 copy-done.2
  51.0 0.0 copy-done.4
  51.0 5.1 %all-to-all-start.1 = ((bf16[8,128,512]{2,1,0:T(8,128)(2,1)}), bf16[8,128,512]{2,1,0:T(8,128)(2,1)S(1)}, u32[]{:S(2)}, u32[]{:S(2)}) async-start(bf16[8,128,512]{2,1,0:T(8,128)(2,1)} %bitcast_convert_fusion), calls=%async_computation.1 | async-start | bytes 2097152 | tf_op jit(solution)/shard_map/all_to_all | solution.py:73
  56.1 0.0 copy-done
  56.1 2.8 %collective-permute-start.3 = (bf16[128,256]{1,0:T(8,128)(2,1)S(1)}, bf16[128,256]{1,0:T(8,128)(2,1)S(1)}, u32[]{:S(2)}, u32[]{:S(2)}) collective-permute-start(bf16[128,256]{1,0:T(8,128)(2,1)S(1)} %copy-done), channel_id=1, source_target_pairs={{0,1},{1,0},{2,3},{3,2},{4,5},{5,4},{6,7},{7,6},{8,9},{9,8},{10,11... | collective-permute-start | bytes 196616 | tf_op jit(solution)/shard_map/ppermute | solution.py:120
  58.9 14.6 %all-to-all-done.1 = bf16[8,128,512]{2,1,0:T(8,128)(2,1)S(1)} async-done(((bf16[8,128,512]{2,1,0:T(8,128)(2,1)}), bf16[8,128,512]{2,1,0:T(8,128)(2,1)S(1)}, u32[]{:S(2)}, u32[]{:S(2)}) %all-to-all-start.1) | async-done | bytes 1048608 | tf_op jit(solution)/shard_map/all_to_all | solution.py:73
  73.6 0.1 convert_reduce_fusion
  73.7 0.0 collective-permute-done.3
  73.7 0.1 fusion.13
  73.8 2.9 %collective-permute-start.6 = (bf16[128,512]{1,0:T(8,128)(2,1)S(1)}, bf16[128,512]{1,0:T(8,128)(2,1)S(1)}, u32[]{:S(2)}, u32[]{:S(2)}) collective-permute-start(bf16[128,512]{1,0:T(8,128)(2,1)S(1)} %fusion.13), channel_id=1, source_target_pairs={{1,256},{256,1},{3,320},{320,3},{5,384},{384,5},{7,448},{448,7},{9... | collective-permute-start | bytes 393224 | tf_op jit(solution)/shard_map/ppermute | solution.py:130
  76.7 8.3 %collective-permute-done.6 = bf16[128,512]{1,0:T(8,128)(2,1)S(1)} collective-permute-done((bf16[128,512]{1,0:T(8,128)(2,1)S(1)}, bf16[128,512]{1,0:T(8,128)(2,1)S(1)}, u32[]{:S(2)}, u32[]{:S(2)}) %collective-permute-start.6) | collective-permute-done | bytes 131104 | tf_op jit(solution)/shard_map/ppermute | solution.py:130
  85.0 0.1 fusion.12
  85.1 1.1 broadcast_in_dim.7
  86.2 4.9 %all-to-all-start.2 = ((bf16[8,128,512]{2,1,0:T(8,128)(2,1)}), bf16[8,128,512]{2,1,0:T(8,128)(2,1)S(1)}, u32[]{:S(2)}, u32[]{:S(2)}) async-start(bf16[8,128,512]{2,1,0:T(8,128)(2,1)} %broadcast_in_dim.7), calls=%async_computation.2 | async-start | bytes 2097152 | tf_op jit(solution)/shard_map/all_to_all | solution.py:73
  91.1 0.1 fusion.9
  91.2 11.2 %collective-permute-start.7 = (bf16[128,256]{1,0:T(8,128)(2,1)S(1)}, bf16[128,256]{1,0:T(8,128)(2,1)S(1)}, u32[]{:S(2)}, u32[]{:S(2)}) collective-permute-start(bf16[128,256]{1,0:T(8,128)(2,1)S(1)} %slice.108), channel_id=1, source_target_pairs={{0,1},{1,0},{2,3},{3,2},{4,5},{5,4},{6,7},{7,6},{8,9},{9,8},{10,11... | collective-permute-start | bytes 196616 | tf_op jit(solution)/shard_map/ppermute | solution.py:135
  102.4 0.9 collective-permute-done.7
  103.3 5.3 %all-to-all-done.2 = bf16[8,128,512]{2,1,0:T(8,128)(2,1)S(1)} async-done(((bf16[8,128,512]{2,1,0:T(8,128)(2,1)}), bf16[8,128,512]{2,1,0:T(8,128)(2,1)S(1)}, u32[]{:S(2)}, u32[]{:S(2)}) %all-to-all-start.2) | async-done | bytes 1048608 | tf_op jit(solution)/shard_map/all_to_all | solution.py:73
  108.5 0.0 copy-done.7
  108.5 0.7 fusion.25
  109.3 0.8 fusion.10
  110.0 0.0 copy-done.3
  110.1 0.0 copy-done.5
  110.1 0.7 fusion
  110.8 1.3 copy.14
  112.1 14.1 %all-to-all-start.3 = ((bf16[16,128,256]{2,1,0:T(8,128)(2,1)}), bf16[16,128,256]{2,1,0:T(8,128)(2,1)S(1)}, u32[]{:S(2)}, u32[]{:S(2)}) async-start(bf16[16,128,256]{2,1,0:T(8,128)(2,1)} %bitcast.20), calls=%async_computation.3 | async-start | bytes 2097152 | tf_op jit(solution)/shard_map/all_to_all | solution.py:73
  126.2 0.0 copy-done.1
  126.2 0.0 copy-start.8
  126.3 2.1 %collective-permute-start.10 = (bf16[256,512]{1,0:T(8,128)(2,1)S(1)}, bf16[256,512]{1,0:T(8,128)(2,1)S(1)}, u32[]{:S(2)}, u32[]{:S(2)}) collective-permute-start(bf16[256,512]{1,0:T(8,128)(2,1)S(1)} %copy-done.1), channel_id=1, source_target_pairs={{0,32},{2,34},{4,36},{6,38},{8,40},{10,42},{12,44},{14,46},{16,48}... | collective-permute-start | bytes 786440 | tf_op jit(solution)/shard_map/ppermute | solution.py:141
  128.3 15.7 %collective-permute-done.10 = bf16[256,512]{1,0:T(8,128)(2,1)S(1)} collective-permute-done((bf16[256,512]{1,0:T(8,128)(2,1)S(1)}, bf16[256,512]{1,0:T(8,128)(2,1)S(1)}, u32[]{:S(2)}, u32[]{:S(2)}) %collective-permute-start.10) | collective-permute-done | bytes 262176 | tf_op jit(solution)/shard_map/ppermute | solution.py:141
  144.1 0.1 fusion.3
  144.2 1.9 %collective-permute-start.11 = (bf16[256,256]{1,0:T(8,128)(2,1)S(1)}, bf16[256,256]{1,0:T(8,128)(2,1)S(1)}, u32[]{:S(2)}, u32[]{:S(2)}) collective-permute-start(bf16[256,256]{1,0:T(8,128)(2,1)S(1)} %slice_select_fusion.1), channel_id=1, source_target_pairs={{0,1},{1,0},{2,3},{3,2},{4,5},{5,4},{6,7},{7,6},{8,9},{9,8},{10,11... | collective-permute-start | bytes 393224 | tf_op jit(solution)/shard_map/ppermute | solution.py:149
  146.1 0.6 slice_select_fusion.3
  146.8 0.7 collective-permute-done.11
  147.4 0.7 slice_select_fusion.2
  148.1 0.0 all-to-all-done.3
  148.1 0.1 reduce_sum.22
  148.3 3.6 %collective-permute-start.8 = (bf16[128,128]{1,0:T(8,128)(2,1)S(1)}, bf16[128,128]{1,0:T(8,128)(2,1)S(1)}, u32[]{:S(2)}, u32[]{:S(2)}) collective-permute-start(bf16[128,128]{1,0:T(8,128)(2,1)S(1)} %get-tuple-element.37), channel_id=1, source_target_pairs={{0,1},{1,0},{2,3},{3,2},{4,5},{5,4},{6,7},{7,6},{8,9},{9,8},{10,11... | collective-permute-start | bytes 98312 | tf_op jit(solution)/shard_map/ppermute | solution.py:146
  151.9 2.2 %collective-permute-start.9 = (bf16[128,128]{1,0:T(8,128)(2,1)S(1)}, bf16[128,128]{1,0:T(8,128)(2,1)S(1)}, u32[]{:S(2)}, u32[]{:S(2)}) collective-permute-start(bf16[128,128]{1,0:T(8,128)(2,1)S(1)} %get-tuple-element.36), channel_id=1, source_target_pairs={{0,0},{1,1},{2,2},{3,3},{4,4},{5,5},{6,6},{7,7},{8,8},{9,9},{10,10... | collective-permute-start | bytes 98312 | tf_op jit(solution)/shard_map/ppermute | solution.py:145
  154.1 0.8 copy.15
  154.8 0.0 collective-permute-done.8
  154.8 2.8 %collective-permute-done.9 = bf16[128,128]{1,0:T(8,128)(2,1)S(1)} collective-permute-done((bf16[128,128]{1,0:T(8,128)(2,1)S(1)}, bf16[128,128]{1,0:T(8,128)(2,1)S(1)}, u32[]{:S(2)}, u32[]{:S(2)}) %collective-permute-start.9) | collective-permute-done | bytes 32800 | tf_op jit(solution)/shard_map/ppermute | solution.py:145
  157.7 0.6 broadcast_select_fusion.2
  (24 shorter events, 0.3 us)
Async XLA Ops:
  1.4 13.8 %collective-permute-start.4 = (bf16[128,128]{1,0:T(8,128)(2,1)S(1)}, bf16[128,128]{1,0:T(8,128)(2,1)S(1)}, u32[]{:S(2)}, u32[]{:S(2)}) collective-permute-start(bf16[128,128]{1,0:T(8,128)(2,1)S(1)} %get-tuple-element.38), channel_id=1, source_target_pairs={{0,8},{1,1},{2,26},{3,3},{4,74},{5,5},{6,92},{7,7},{8,140},{9,9},{... | collective-permute-start | bytes 98312 | tf_op jit(solution)/shard_map/ppermute | solution.py:98
  12.2 8.1 %collective-permute-start.5 = (bf16[128,128]{1,0:T(8,128)(2,1)S(1)}, bf16[128,128]{1,0:T(8,128)(2,1)S(1)}, u32[]{:S(2)}, u32[]{:S(2)}) collective-permute-start(bf16[128,128]{1,0:T(8,128)(2,1)S(1)} %get-tuple-element.39), channel_id=1, source_target_pairs={{1,8},{0,1},{3,26},{2,3},{5,74},{4,5},{7,92},{6,7},{9,140},{8,9},{... | collective-permute-start | bytes 98312 | tf_op jit(solution)/shard_map/ppermute | solution.py:99
  21.4 10.1 %copy-start.6 = (bf16[256,256]{1,0:T(8,128)(2,1)S(1)}, bf16[256,256]{1,0:T(8,128)(2,1)}, u32[]{:S(2)}) copy-start(bf16[256,256]{1,0:T(8,128)(2,1)} %param.7) | copy-start | bytes 393220
  21.4 27.8 %all-to-all-start = ((bf16[16,128,256]{2,1,0:T(8,128)(2,1)}), bf16[16,128,256]{2,1,0:T(8,128)(2,1)S(1)}, u32[]{:S(2)}, u32[]{:S(2)}) async-start(bf16[16,128,256]{2,1,0:T(8,128)(2,1)} %broadcast_in_dim.6), calls=%async_computation | async-start | bytes 2097152 | tf_op jit(solution)/shard_map/all_to_all | solution.py:73
  31.6 17.4 %collective-permute-start.2 = (bf16[256,256]{1,0:T(8,128)(2,1)S(1)}, bf16[256,256]{1,0:T(8,128)(2,1)S(1)}, u32[]{:S(2)}, u32[]{:S(2)}) collective-permute-start(bf16[256,256]{1,0:T(8,128)(2,1)S(1)} %get-tuple-element.23), channel_id=1, source_target_pairs={{1,32},{3,34},{5,36},{7,38},{9,40},{11,42},{13,44},{15,46},{17,48}... | collective-permute-start | bytes 393224 | tf_op jit(solution)/shard_map/ppermute | solution.py:108
  33.5 15.5 %collective-permute-start = (bf16[256,256]{1,0:T(8,128)(2,1)S(1)}, bf16[256,256]{1,0:T(8,128)(2,1)S(1)}, u32[]{:S(2)}, u32[]{:S(2)}) collective-permute-start(bf16[256,256]{1,0:T(8,128)(2,1)S(1)} %get-tuple-element.23), channel_id=1, source_target_pairs={{0,1},{1,0},{2,3},{3,2},{4,5},{5,4},{6,7},{7,6},{8,9},{9,8},{10,11... | collective-permute-start | bytes 393224 | tf_op jit(solution)/shard_map/ppermute | solution.py:107
  36.3 12.7 %collective-permute-start.1 = (bf16[256,256]{1,0:T(8,128)(2,1)S(1)}, bf16[256,256]{1,0:T(8,128)(2,1)S(1)}, u32[]{:S(2)}, u32[]{:S(2)}) collective-permute-start(bf16[256,256]{1,0:T(8,128)(2,1)S(1)} %get-tuple-element.22), channel_id=1, source_target_pairs={{0,32},{2,34},{4,36},{6,38},{8,40},{10,42},{12,44},{14,46},{16,48}... | collective-permute-start | bytes 393224 | tf_op jit(solution)/shard_map/ppermute | solution.py:108
  49.2 1.8 %copy-start.2 = (bf16[1,256,512]{2,1,0:T(8,128)(2,1)}, bf16[1,256,512]{2,1,0:T(8,128)(2,1)S(1)}, u32[]{:S(2)}) copy-start(bf16[1,256,512]{2,1,0:T(8,128)(2,1)S(1)} %maximum_select_fusion.1) | copy-start | bytes 786436
  49.2 1.7 %copy-start.4 = (bf16[1,256,512]{2,1,0:T(8,128)(2,1)}, bf16[1,256,512]{2,1,0:T(8,128)(2,1)S(1)}, u32[]{:S(2)}) copy-start(bf16[1,256,512]{2,1,0:T(8,128)(2,1)S(1)} %maximum_select_fusion) | copy-start | bytes 786436
  51.0 5.1 %copy-start = (bf16[128,256]{1,0:T(8,128)(2,1)S(1)}, bf16[128,256]{1,0:T(8,128)(2,1)}, u32[]{:S(2)}) copy-start(bf16[128,256]{1,0:T(8,128)(2,1)} %param.6) | copy-start | bytes 196612
  51.0 22.6 %all-to-all-start.1 = ((bf16[8,128,512]{2,1,0:T(8,128)(2,1)}), bf16[8,128,512]{2,1,0:T(8,128)(2,1)S(1)}, u32[]{:S(2)}, u32[]{:S(2)}) async-start(bf16[8,128,512]{2,1,0:T(8,128)(2,1)} %bitcast_convert_fusion), calls=%async_computation.1 | async-start | bytes 2097152 | tf_op jit(solution)/shard_map/all_to_all | solution.py:73
  56.1 17.6 %collective-permute-start.3 = (bf16[128,256]{1,0:T(8,128)(2,1)S(1)}, bf16[128,256]{1,0:T(8,128)(2,1)S(1)}, u32[]{:S(2)}, u32[]{:S(2)}) collective-permute-start(bf16[128,256]{1,0:T(8,128)(2,1)S(1)} %copy-done), channel_id=1, source_target_pairs={{0,1},{1,0},{2,3},{3,2},{4,5},{5,4},{6,7},{7,6},{8,9},{9,8},{10,11... | collective-permute-start | bytes 196616 | tf_op jit(solution)/shard_map/ppermute | solution.py:120
  73.8 11.2 %collective-permute-start.6 = (bf16[128,512]{1,0:T(8,128)(2,1)S(1)}, bf16[128,512]{1,0:T(8,128)(2,1)S(1)}, u32[]{:S(2)}, u32[]{:S(2)}) collective-permute-start(bf16[128,512]{1,0:T(8,128)(2,1)S(1)} %fusion.13), channel_id=1, source_target_pairs={{1,256},{256,1},{3,320},{320,3},{5,384},{384,5},{7,448},{448,7},{9... | collective-permute-start | bytes 393224 | tf_op jit(solution)/shard_map/ppermute | solution.py:130
  86.2 22.3 %all-to-all-start.2 = ((bf16[8,128,512]{2,1,0:T(8,128)(2,1)}), bf16[8,128,512]{2,1,0:T(8,128)(2,1)S(1)}, u32[]{:S(2)}, u32[]{:S(2)}) async-start(bf16[8,128,512]{2,1,0:T(8,128)(2,1)} %broadcast_in_dim.7), calls=%async_computation.2 | async-start | bytes 2097152 | tf_op jit(solution)/shard_map/all_to_all | solution.py:73
  91.2 12.1 %collective-permute-start.7 = (bf16[128,256]{1,0:T(8,128)(2,1)S(1)}, bf16[128,256]{1,0:T(8,128)(2,1)S(1)}, u32[]{:S(2)}, u32[]{:S(2)}) collective-permute-start(bf16[128,256]{1,0:T(8,128)(2,1)S(1)} %slice.108), channel_id=1, source_target_pairs={{0,1},{1,0},{2,3},{3,2},{4,5},{5,4},{6,7},{7,6},{8,9},{9,8},{10,11... | collective-permute-start | bytes 196616 | tf_op jit(solution)/shard_map/ppermute | solution.py:135
  103.3 5.3 %copy-start.7 = (bf16[128,256]{1,0:T(8,128)(2,1)}, bf16[128,256]{1,0:T(8,128)(2,1)S(1)}, u32[]{:S(2)}) copy-start(bf16[128,256]{1,0:T(8,128)(2,1)S(1)} %collective-permute-done.7) | copy-start | bytes 196612
  108.5 1.5 copy-start.3
  108.5 1.5 copy-start.5
  112.1 14.1 %copy-start.1 = (bf16[256,512]{1,0:T(8,128)(2,1)S(1)}, bf16[256,512]{1,0:T(8,128)(2,1)}, u32[]{:S(2)}) copy-start(bf16[256,512]{1,0:T(8,128)(2,1)} %fusion.10) | copy-start | bytes 786436
  112.1 36.0 %all-to-all-start.3 = ((bf16[16,128,256]{2,1,0:T(8,128)(2,1)}), bf16[16,128,256]{2,1,0:T(8,128)(2,1)S(1)}, u32[]{:S(2)}, u32[]{:S(2)}) async-start(bf16[16,128,256]{2,1,0:T(8,128)(2,1)} %bitcast.20), calls=%async_computation.3 | async-start | bytes 2097152 | tf_op jit(solution)/shard_map/all_to_all | solution.py:73
  126.2 19.9 %copy-start.8 = (bf16[128,256]{1,0:T(8,128)(2,1)S(1)}, bf16[128,256]{1,0:T(8,128)(2,1)}, u32[]{:S(2)}) copy-start(bf16[128,256]{1,0:T(8,128)(2,1)} %copy-done.7) | copy-start | bytes 196612
  126.3 17.8 %collective-permute-start.10 = (bf16[256,512]{1,0:T(8,128)(2,1)S(1)}, bf16[256,512]{1,0:T(8,128)(2,1)S(1)}, u32[]{:S(2)}, u32[]{:S(2)}) collective-permute-start(bf16[256,512]{1,0:T(8,128)(2,1)S(1)} %copy-done.1), channel_id=1, source_target_pairs={{0,32},{2,34},{4,36},{6,38},{8,40},{10,42},{12,44},{14,46},{16,48}... | collective-permute-start | bytes 786440 | tf_op jit(solution)/shard_map/ppermute | solution.py:141
  144.2 3.2 %collective-permute-start.11 = (bf16[256,256]{1,0:T(8,128)(2,1)S(1)}, bf16[256,256]{1,0:T(8,128)(2,1)S(1)}, u32[]{:S(2)}, u32[]{:S(2)}) collective-permute-start(bf16[256,256]{1,0:T(8,128)(2,1)S(1)} %slice_select_fusion.1), channel_id=1, source_target_pairs={{0,1},{1,0},{2,3},{3,2},{4,5},{5,4},{6,7},{7,6},{8,9},{9,8},{10,11... | collective-permute-start | bytes 393224 | tf_op jit(solution)/shard_map/ppermute | solution.py:149
  148.3 6.6 %collective-permute-start.8 = (bf16[128,128]{1,0:T(8,128)(2,1)S(1)}, bf16[128,128]{1,0:T(8,128)(2,1)S(1)}, u32[]{:S(2)}, u32[]{:S(2)}) collective-permute-start(bf16[128,128]{1,0:T(8,128)(2,1)S(1)} %get-tuple-element.37), channel_id=1, source_target_pairs={{0,1},{1,0},{2,3},{3,2},{4,5},{5,4},{6,7},{7,6},{8,9},{9,8},{10,11... | collective-permute-start | bytes 98312 | tf_op jit(solution)/shard_map/ppermute | solution.py:146
  151.9 5.8 %collective-permute-start.9 = (bf16[128,128]{1,0:T(8,128)(2,1)S(1)}, bf16[128,128]{1,0:T(8,128)(2,1)S(1)}, u32[]{:S(2)}, u32[]{:S(2)}) collective-permute-start(bf16[128,128]{1,0:T(8,128)(2,1)S(1)} %get-tuple-element.36), channel_id=1, source_target_pairs={{0,0},{1,1},{2,2},{3,3},{4,4},{5,5},{6,6},{7,7},{8,8},{9,9},{10,10... | collective-permute-start | bytes 98312 | tf_op jit(solution)/shard_map/ppermute | solution.py:145

commit v4 on v3

--- a/solution.py
+++ b/solution.py
@@ -45,6 +45,7 @@
 PARTNER_SWAP = [(device(y, xh, xl, z, 1), device(y, 1 - xh, xl, z, 0)) for y, xh, xl, z in CHIPS] + [
     (device(y, xh, xl, z, 0), device(y, xh, 1 - xl, z, 1)) for y, xh, xl, z in CHIPS
 ]
+SWAP_PARTNER = [(there, here) for here, there in PARTNER_SWAP]
 
 
 def spread(core):
@@ -97,16 +98,15 @@
     inner, width = gate_weight.shape[1], out_grad.shape[1]
     own = lax.ppermute(jnp.where(first, tokens, out_grad), ALL, SPREAD_OWN)
     other = lax.ppermute(jnp.where(first, out_grad, tokens), ALL, SPREAD_OTHER)
-    acts = gather(jnp.concatenate([own, other], axis=1), WIDE)
-    acts = acts.reshape(2, N * acts.shape[1], acts.shape[2])
-
     out_t = out_weight.T
     mine = jnp.where(first, gate_weight, fold(out_t))
     yours = jnp.where(first, fold(out_t), gate_weight)
-    blocks = [
-        (mine, lax.ppermute(yours, ALL, SWAP)),
-        (lax.ppermute(mine, ALL, PARTNER), lax.ppermute(yours, ALL, PARTNER_SWAP)),
-    ]
+    weights_in = [lax.ppermute(yours, ALL, SWAP), lax.ppermute(mine, ALL, PARTNER), lax.ppermute(yours, ALL, PARTNER_SWAP)]
+    acts = gather(jnp.concatenate([own, other], axis=1), WIDE)
+    mixer_in = lax.ppermute(mixer_out, ALL, SWAP)
+    acts, mixer_in = lax.optimization_barrier((acts, mixer_in))
+    acts = acts.reshape(2, N * acts.shape[1], acts.shape[2])
+    blocks = [(mine, weights_in[0]), weights_in[1:]]
     weight = jnp.stack(
         [
             jnp.where(
@@ -117,7 +117,6 @@
             for pair in blocks
         ]
     )
-    mixer_in = lax.ppermute(mixer_out, ALL, SWAP)
     mixer_vals = jnp.concatenate([mixer_out, mixer_in], axis=1).astype(f32)
 
     partial = jnp.einsum("kad,kdn->an", acts, weight, preferred_element_type=f32)
@@ -136,22 +135,23 @@
     units, mixer_grad_in = lax.optimization_barrier((units, mixer_grad_in))
     units = units.reshape(-1, units.shape[2])
 
-    grads = jnp.einsum("kad,an->kdn", acts, units, preferred_element_type=f32)
-    units, grads_out = lax.optimization_barrier((units, grads[1].astype(bf16)))
-    grads_in = lax.ppermute(grads_out, ALL, PARTNER)
-
     layer_part = jnp.einsum("an,kdn->kad", units, weight, preferred_element_type=f32)
     layer_pair = reduce(layer_part.reshape(2 * N, -1, layer_part.shape[2]), WIDE).astype(bf16)
+
+    grads = jnp.einsum("kad,an->kdn", acts, units, preferred_element_type=f32)
+    keep = jnp.where(first, grads[:, :, :inner], jnp.stack([fold(g) for g in grads[:, :width]]))
+    send = jnp.where(first, grads[:, :, inner:], jnp.stack([fold(g) for g in grads[:, width:]]))
+    swap_in = lax.ppermute(send[0], ALL, SWAP)
+    keep_far, send_far = keep[1].astype(bf16), send[1].astype(bf16)
     layer_own = lax.ppermute(layer_pair[:, :width], ALL, BACK_OWN)
     layer_other = lax.ppermute(layer_pair[:, width:], ALL, BACK_OTHER)
-
-    grads = (grads[0] + grads_in.astype(f32)).astype(bf16)
-    grads_in = lax.ppermute(jnp.where(first, grads[:, inner:], fold(grads[width:])), ALL, SWAP)
+    kept = (keep[0] + lax.ppermute(keep_far, ALL, PARTNER).astype(f32)).astype(bf16)
+    sent = (swap_in + lax.ppermute(send_far, ALL, SWAP_PARTNER).astype(f32)).astype(bf16)
     return (
         jnp.where(first, layer_other, layer_own),
         jnp.where(first, mixer_grad[:, :inner], mixer_grad_in),
-        jnp.where(first, grads[:, :inner], grads_in),
-        jnp.where(first, unfold(grads_in), grads[:width]).T,
+        jnp.where(first, kept, sent),
+        unfold(jnp.where(first, sent, kept)).T,
     )
 
 

time: 159 us -> 156 us (0.981)
  the two profiles are of different devices: /device:TPU:12 before, /device:TPU:2 now
where the time goes in v4:
time: 156 us; the launch traced here: 154 us
  starting transfers between devices  69.7 us (45%)
  waiting for transfers between devices  45.9 us (29%)
  blocking collectives  24.1 us (15%)
  local copies, waits for them, and re-layouts  6.49 us (4%)
  other arithmetic  3.83 us (2%)
  matrix products  3.18 us (2%)
    all_to_all x3, starting transfers between devices, trade(): lax.all_to_all(blocks, ALL, split_axis=0, concat_axis=0, axis_index_group...  28.5 us
    all_to_all x1, blocking collectives, trade(): lax.all_to_all(blocks, ALL, split_axis=0, concat_axis=0, axis_index_group...  24.1 us
    all_to_all x3, waiting for transfers between devices, trade(): lax.all_to_all(blocks, ALL, split_axis=0, concat_axis=0, axis_index_group...  15 us
    ppermute x1, starting transfers between devices, local(): own = lax.ppermute(jnp.where(first, tokens, out_grad), ALL, SPREAD_OWN)  7.7 us
    ppermute x1, waiting for transfers between devices, local(): lax.ppermute(jnp.where(first, gated, total.astype(bf16)), ALL, CROSS)  7.15 us
    ppermute x1, waiting for transfers between devices, local(): other = lax.ppermute(jnp.where(first, out_grad, tokens), ALL, SPREAD_OTHER)  5.88 us
    ppermute x1, waiting for transfers between devices, local(): lax.ppermute(send_far, ALL, SWAP_PARTNER).astype(f32)  4.7 us
    ppermute x1, starting transfers between devices, local(): lax.ppermute(mine, ALL, PARTNER)  4.59 us
  transfers between devices with their start and end apart: 16, of which 10 were waited for; matrix products, arithmetic and copies ran while one was open for 3% of the time, Pallas kernels for 0%

profile of v4, /device:TPU:2, one launch (start us, length us, event | category | flops | bytes accessed | tf_op | source)
XLA Modules:
  0.0 154.2 jit_solution(6593704063504705393)
XLA Ops:
  0.6 0.8 broadcast_select_fusion.6
  1.4 7.7 %collective-permute-start.3 = (bf16[128,128]{1,0:T(8,128)(2,1)S(1)}, bf16[128,128]{1,0:T(8,128)(2,1)S(1)}, u32[]{:S(2)}, u32[]{:S(2)}) collective-permute-start(bf16[128,128]{1,0:T(8,128)(2,1)S(1)} %get-tuple-element.52), channel_id=1, source_target_pairs={{0,8},{1,1},{2,26},{3,3},{4,74},{5,5},{6,92},{7,7},{8,140},{9,9},{... | collective-permute-start | bytes 98312 | tf_op jit(solution)/shard_map/ppermute | solution.py:99
  9.1 1.9 %collective-permute-start.4 = (bf16[128,128]{1,0:T(8,128)(2,1)S(1)}, bf16[128,128]{1,0:T(8,128)(2,1)S(1)}, u32[]{:S(2)}, u32[]{:S(2)}) collective-permute-start(bf16[128,128]{1,0:T(8,128)(2,1)S(1)} %get-tuple-element.53), channel_id=1, source_target_pairs={{1,8},{0,1},{3,26},{2,3},{5,74},{4,5},{7,92},{6,7},{9,140},{8,9},{... | collective-permute-start | bytes 98312 | tf_op jit(solution)/shard_map/ppermute | solution.py:100
  11.1 1.0 copy.12
  12.1 0.0 collective-permute-done.3
  12.1 5.9 %collective-permute-done.4 = bf16[128,128]{1,0:T(8,128)(2,1)S(1)} collective-permute-done((bf16[128,128]{1,0:T(8,128)(2,1)S(1)}, bf16[128,128]{1,0:T(8,128)(2,1)S(1)}, u32[]{:S(2)}, u32[]{:S(2)}) %collective-permute-start.4) | collective-permute-done | bytes 32800 | tf_op jit(solution)/shard_map/ppermute | solution.py:100
  18.0 1.1 broadcast_in_dim.6
  19.1 0.0 copy-start.1
  19.1 0.0 copy-start
  19.1 13.5 %all-to-all-start = ((bf16[16,128,256]{2,1,0:T(8,128)(2,1)}), bf16[16,128,256]{2,1,0:T(8,128)(2,1)S(1)}, u32[]{:S(2)}, u32[]{:S(2)}) async-start(bf16[16,128,256]{2,1,0:T(8,128)(2,1)} %broadcast_in_dim.6), calls=%async_computation | async-start | bytes 2097152 | tf_op jit(solution)/shard_map/all_to_all | solution.py:74
  32.6 0.0 copy-done.1
  32.6 1.9 %collective-permute-start.2 = (bf16[256,256]{1,0:T(8,128)(2,1)S(1)}, bf16[256,256]{1,0:T(8,128)(2,1)S(1)}, u32[]{:S(2)}, u32[]{:S(2)}) collective-permute-start(bf16[256,256]{1,0:T(8,128)(2,1)S(1)} %get-tuple-element.37), channel_id=1, source_target_pairs={{1,32},{3,34},{5,36},{7,38},{9,40},{11,42},{13,44},{15,46},{17,48}... | collective-permute-start | bytes 393224 | tf_op jit(solution)/shard_map/ppermute | solution.py:104
  34.5 2.9 %collective-permute-start = (bf16[256,256]{1,0:T(8,128)(2,1)S(1)}, bf16[256,256]{1,0:T(8,128)(2,1)S(1)}, u32[]{:S(2)}, u32[]{:S(2)}) collective-permute-start(bf16[256,256]{1,0:T(8,128)(2,1)S(1)} %get-tuple-element.37), channel_id=1, source_target_pairs={{0,1},{1,0},{2,3},{3,2},{4,5},{5,4},{6,7},{7,6},{8,9},{9,8},{10,11... | collective-permute-start | bytes 393224 | tf_op jit(solution)/shard_map/ppermute | solution.py:104
  37.4 0.0 copy-done
  37.4 1.9 %collective-permute-start.5 = (bf16[128,256]{1,0:T(8,128)(2,1)S(1)}, bf16[128,256]{1,0:T(8,128)(2,1)S(1)}, u32[]{:S(2)}, u32[]{:S(2)}) collective-permute-start(bf16[128,256]{1,0:T(8,128)(2,1)S(1)} %copy-done), channel_id=1, source_target_pairs={{0,1},{1,0},{2,3},{3,2},{4,5},{5,4},{6,7},{7,6},{8,9},{9,8},{10,11... | collective-permute-start | bytes 196616 | tf_op jit(solution)/shard_map/ppermute | solution.py:106
  39.3 4.6 %collective-permute-start.1 = (bf16[256,256]{1,0:T(8,128)(2,1)S(1)}, bf16[256,256]{1,0:T(8,128)(2,1)S(1)}, u32[]{:S(2)}, u32[]{:S(2)}) collective-permute-start(bf16[256,256]{1,0:T(8,128)(2,1)S(1)} %get-tuple-element.36), channel_id=1, source_target_pairs={{0,32},{2,34},{4,36},{6,38},{8,40},{10,42},{12,44},{14,46},{16,48}... | collective-permute-start | bytes 393224 | tf_op jit(solution)/shard_map/ppermute | solution.py:104
  44.0 2.1 %collective-permute-done.2 = bf16[256,256]{1,0:T(8,128)(2,1)S(1)} collective-permute-done((bf16[256,256]{1,0:T(8,128)(2,1)S(1)}, bf16[256,256]{1,0:T(8,128)(2,1)S(1)}, u32[]{:S(2)}, u32[]{:S(2)}) %collective-permute-start.2) | collective-permute-done | bytes 131104 | tf_op jit(solution)/shard_map/ppermute | solution.py:104
  46.1 0.0 collective-permute-done
  46.2 3.2 %collective-permute-done.1 = bf16[256,256]{1,0:T(8,128)(2,1)S(1)} collective-permute-done((bf16[256,256]{1,0:T(8,128)(2,1)S(1)}, bf16[256,256]{1,0:T(8,128)(2,1)S(1)}, u32[]{:S(2)}, u32[]{:S(2)}) %collective-permute-start.1) | collective-permute-done | bytes 131104 | tf_op jit(solution)/shard_map/ppermute | solution.py:104
  49.5 0.1 maximum_select_fusion
  49.6 0.1 maximum_select_fusion.1
  49.6 0.0 collective-permute-done.5
  49.6 0.0 all-to-all-done
  49.6 0.7 bitcast_convert_fusion
  50.4 24.1 %all_to_all.20 = bf16[8,128,512]{2,1,0:T(8,128)(2,1)S(1)} all-to-all(bf16[8,128,512]{2,1,0:T(8,128)(2,1)S(1)} %bitcast_convert_fusion), channel_id=1, replica_groups={{0,64,128,192,256,320,384,448},{2,66,130,194,258,322,386,450},{4,68,132..., dimensions={0} | all-to-all | bytes 2097152 | tf_op jit(solution)/shard_map/all_to_all | solution.py:74
  74.4 0.1 convert_reduce_fusion
  74.6 0.1 fusion.13
  74.7 4.1 %collective-permute-start.6 = (bf16[128,512]{1,0:T(8,128)(2,1)S(1)}, bf16[128,512]{1,0:T(8,128)(2,1)S(1)}, u32[]{:S(2)}, u32[]{:S(2)}) collective-permute-start(bf16[128,512]{1,0:T(8,128)(2,1)S(1)} %fusion.13), channel_id=1, source_target_pairs={{1,256},{256,1},{3,320},{320,3},{5,384},{384,5},{7,448},{448,7},{9... | collective-permute-start | bytes 393224 | tf_op jit(solution)/shard_map/ppermute | solution.py:129
  78.8 7.2 %collective-permute-done.6 = bf16[128,512]{1,0:T(8,128)(2,1)S(1)} collective-permute-done((bf16[128,512]{1,0:T(8,128)(2,1)S(1)}, bf16[128,512]{1,0:T(8,128)(2,1)S(1)}, u32[]{:S(2)}, u32[]{:S(2)}) %collective-permute-start.6) | collective-permute-done | bytes 131104 | tf_op jit(solution)/shard_map/ppermute | solution.py:129
  85.9 0.1 fusion.10
  86.1 1.1 broadcast_in_dim.7
  87.1 5.8 %all-to-all-start.2 = ((bf16[8,128,512]{2,1,0:T(8,128)(2,1)}), bf16[8,128,512]{2,1,0:T(8,128)(2,1)S(1)}, u32[]{:S(2)}, u32[]{:S(2)}) async-start(bf16[8,128,512]{2,1,0:T(8,128)(2,1)} %broadcast_in_dim.7), calls=%async_computation.2 | async-start | bytes 2097152 | tf_op jit(solution)/shard_map/all_to_all | solution.py:74
  92.9 0.1 fusion.6
  93.0 3.0 %collective-permute-start.7 = (bf16[128,256]{1,0:T(8,128)(2,1)S(1)}, bf16[128,256]{1,0:T(8,128)(2,1)S(1)}, u32[]{:S(2)}, u32[]{:S(2)}) collective-permute-start(bf16[128,256]{1,0:T(8,128)(2,1)S(1)} %slice.140), channel_id=1, source_target_pairs={{0,1},{1,0},{2,3},{3,2},{4,5},{5,4},{6,7},{7,6},{8,9},{9,8},{10,11... | collective-permute-start | bytes 196616 | tf_op jit(solution)/shard_map/ppermute | solution.py:134
  96.0 0.9 collective-permute-done.7
  96.9 15.0 %all-to-all-done.2 = bf16[8,128,512]{2,1,0:T(8,128)(2,1)S(1)} async-done(((bf16[8,128,512]{2,1,0:T(8,128)(2,1)}), bf16[8,128,512]{2,1,0:T(8,128)(2,1)S(1)}, u32[]{:S(2)}, u32[]{:S(2)}) %all-to-all-start.2) | async-done | bytes 1048608 | tf_op jit(solution)/shard_map/all_to_all | solution.py:74
  111.9 1.7 %fusion = bf16[2,1024,256]{1,2,0:T(8,128)(2,1)} fusion(bf16[1024,512,1]{1,0,2:T(8,128)(2,1)S(1)} %bitcast.72, bf16[1,256,512]{2,1,0:T(8,128)(2,1)S(1)} %maximum_select_fusion.1, bf16[1,256,512]{2,1,0:T(8,128)(2,1)S(1)} %maximum_select_fusion), kind=kOutput, calls=%fused_computation.3 | convolution fusion | flops 537657344 | bytes 2621440 | tf_op jit(solution)/shard_map/an,kdn->kad/dot_general | solution.py:138
  113.6 0.7 fusion.27
  114.4 2.3 %copy.14 = bf16[2,1024,256]{2,1,0:T(8,128)(2,1)} copy(bf16[2,1024,256]{1,2,0:T(8,128)(2,1)} %fusion) | data formatting | bytes 2097152 | tf_op jit(solution)/shard_map/convert_element_type | solution.py:82
  116.6 9.2 %all-to-all-start.3 = ((bf16[16,128,256]{2,1,0:T(8,128)(2,1)}), bf16[16,128,256]{2,1,0:T(8,128)(2,1)S(1)}, u32[]{:S(2)}, u32[]{:S(2)}) async-start(bf16[16,128,256]{2,1,0:T(8,128)(2,1)} %bitcast.18), calls=%async_computation.3 | async-start | bytes 2097152 | tf_op jit(solution)/shard_map/all_to_all | solution.py:74
  125.9 0.1 slice_bitcast_fusion.5
  126.2 0.2 slice_select_fusion.1
  126.4 2.2 %collective-permute-start.11 = (f32[256,256]{1,0:T(8,128)S(1)}, f32[256,256]{1,0:T(8,128)S(1)}, u32[]{:S(2)}, u32[]{:S(2)}) collective-permute-start(f32[256,256]{1,0:T(8,128)S(1)} %slice_bitcast_fusion), channel_id=1, source_target_pairs={{0,1},{1,0},{2,3},{3,2},{4,5},{5,4},{6,7},{7,6},{8,9},{9,8},{10,11... | collective-permute-start | bytes 786440 | tf_op jit(solution)/shard_map/ppermute | solution.py:144
  128.6 3.4 %collective-permute-start.12 = (bf16[256,256]{1,0:T(8,128)(2,1)S(1)}, bf16[256,256]{1,0:T(8,128)(2,1)S(1)}, u32[]{:S(2)}, u32[]{:S(2)}) collective-permute-start(bf16[256,256]{1,0:T(8,128)(2,1)S(1)} %fusion.12), channel_id=1, source_target_pairs={{32,1},{34,3},{36,5},{38,7},{40,9},{42,11},{44,13},{46,15},{48,17}... | collective-permute-start | bytes 393224 | tf_op jit(solution)/shard_map/ppermute | solution.py:149
  132.0 3.7 %collective-permute-start.10 = (bf16[256,256]{1,0:T(8,128)(2,1)S(1)}, bf16[256,256]{1,0:T(8,128)(2,1)S(1)}, u32[]{:S(2)}, u32[]{:S(2)}) collective-permute-start(bf16[256,256]{1,0:T(8,128)(2,1)S(1)} %fusion.11), channel_id=1, source_target_pairs={{0,32},{2,34},{4,36},{6,38},{8,40},{10,42},{12,44},{14,46},{16,48}... | collective-permute-start | bytes 393224 | tf_op jit(solution)/shard_map/ppermute | solution.py:148
  135.8 0.6 slice_select_fusion.2
  136.4 4.7 %collective-permute-done.12 = bf16[256,256]{1,0:T(8,128)(2,1)S(1)} collective-permute-done((bf16[256,256]{1,0:T(8,128)(2,1)S(1)}, bf16[256,256]{1,0:T(8,128)(2,1)S(1)}, u32[]{:S(2)}, u32[]{:S(2)}) %collective-permute-start.12) | collective-permute-done | bytes 131104 | tf_op jit(solution)/shard_map/ppermute | solution.py:149
  141.1 4.3 %collective-permute-done.10 = bf16[256,256]{1,0:T(8,128)(2,1)S(1)} collective-permute-done((bf16[256,256]{1,0:T(8,128)(2,1)S(1)}, bf16[256,256]{1,0:T(8,128)(2,1)S(1)}, u32[]{:S(2)}, u32[]{:S(2)}) %collective-permute-start.10) | collective-permute-done | bytes 131104 | tf_op jit(solution)/shard_map/ppermute | solution.py:148
  145.5 0.0 collective-permute-done.11
  145.5 0.7 broadcast_select_fusion
  146.2 0.0 all-to-all-done.3
  146.2 0.1 reduce_sum.22
  146.4 1.9 %collective-permute-start.9 = (bf16[128,128]{1,0:T(8,128)(2,1)S(1)}, bf16[128,128]{1,0:T(8,128)(2,1)S(1)}, u32[]{:S(2)}, u32[]{:S(2)}) collective-permute-start(bf16[128,128]{1,0:T(8,128)(2,1)S(1)} %get-tuple-element.50), channel_id=1, source_target_pairs={{0,0},{1,1},{2,2},{3,3},{4,4},{5,5},{6,6},{7,7},{8,8},{9,9},{10,10... | collective-permute-start | bytes 98312 | tf_op jit(solution)/shard_map/ppermute | solution.py:146
  148.3 1.9 %collective-permute-start.8 = (bf16[128,128]{1,0:T(8,128)(2,1)S(1)}, bf16[128,128]{1,0:T(8,128)(2,1)S(1)}, u32[]{:S(2)}, u32[]{:S(2)}) collective-permute-start(bf16[128,128]{1,0:T(8,128)(2,1)S(1)} %get-tuple-element.51), channel_id=1, source_target_pairs={{0,1},{1,0},{2,3},{3,2},{4,5},{5,4},{6,7},{7,6},{8,9},{9,8},{10,11... | collective-permute-start | bytes 98312 | tf_op jit(solution)/shard_map/ppermute | solution.py:147
  150.3 0.8 copy.16
  151.0 1.2 collective-permute-done.9
  152.2 1.4 collective-permute-done.8
  153.6 0.6 broadcast_select_fusion.4
  (24 shorter events, 0.4 us)
Async XLA Ops:
  1.4 10.7 %collective-permute-start.3 = (bf16[128,128]{1,0:T(8,128)(2,1)S(1)}, bf16[128,128]{1,0:T(8,128)(2,1)S(1)}, u32[]{:S(2)}, u32[]{:S(2)}) collective-permute-start(bf16[128,128]{1,0:T(8,128)(2,1)S(1)} %get-tuple-element.52), channel_id=1, source_target_pairs={{0,8},{1,1},{2,26},{3,3},{4,74},{5,5},{6,92},{7,7},{8,140},{9,9},{... | collective-permute-start | bytes 98312 | tf_op jit(solution)/shard_map/ppermute | solution.py:99
  9.1 8.8 %collective-permute-start.4 = (bf16[128,128]{1,0:T(8,128)(2,1)S(1)}, bf16[128,128]{1,0:T(8,128)(2,1)S(1)}, u32[]{:S(2)}, u32[]{:S(2)}) collective-permute-start(bf16[128,128]{1,0:T(8,128)(2,1)S(1)} %get-tuple-element.53), channel_id=1, source_target_pairs={{1,8},{0,1},{3,26},{2,3},{5,74},{4,5},{7,92},{6,7},{9,140},{8,9},{... | collective-permute-start | bytes 98312 | tf_op jit(solution)/shard_map/ppermute | solution.py:100
  19.1 13.5 %copy-start.1 = (bf16[256,256]{1,0:T(8,128)(2,1)S(1)}, bf16[256,256]{1,0:T(8,128)(2,1)}, u32[]{:S(2)}) copy-start(bf16[256,256]{1,0:T(8,128)(2,1)} %param.7) | copy-start | bytes 393220
  19.1 18.4 %copy-start = (bf16[128,256]{1,0:T(8,128)(2,1)S(1)}, bf16[128,256]{1,0:T(8,128)(2,1)}, u32[]{:S(2)}) copy-start(bf16[128,256]{1,0:T(8,128)(2,1)} %param.6) | copy-start | bytes 196612
  19.1 30.6 %all-to-all-start = ((bf16[16,128,256]{2,1,0:T(8,128)(2,1)}), bf16[16,128,256]{2,1,0:T(8,128)(2,1)S(1)}, u32[]{:S(2)}, u32[]{:S(2)}) async-start(bf16[16,128,256]{2,1,0:T(8,128)(2,1)} %broadcast_in_dim.6), calls=%async_computation | async-start | bytes 2097152 | tf_op jit(solution)/shard_map/all_to_all | solution.py:74
  32.6 13.5 %collective-permute-start.2 = (bf16[256,256]{1,0:T(8,128)(2,1)S(1)}, bf16[256,256]{1,0:T(8,128)(2,1)S(1)}, u32[]{:S(2)}, u32[]{:S(2)}) collective-permute-start(bf16[256,256]{1,0:T(8,128)(2,1)S(1)} %get-tuple-element.37), channel_id=1, source_target_pairs={{1,32},{3,34},{5,36},{7,38},{9,40},{11,42},{13,44},{15,46},{17,48}... | collective-permute-start | bytes 393224 | tf_op jit(solution)/shard_map/ppermute | solution.py:104
  34.5 11.6 %collective-permute-start = (bf16[256,256]{1,0:T(8,128)(2,1)S(1)}, bf16[256,256]{1,0:T(8,128)(2,1)S(1)}, u32[]{:S(2)}, u32[]{:S(2)}) collective-permute-start(bf16[256,256]{1,0:T(8,128)(2,1)S(1)} %get-tuple-element.37), channel_id=1, source_target_pairs={{0,1},{1,0},{2,3},{3,2},{4,5},{5,4},{6,7},{7,6},{8,9},{9,8},{10,11... | collective-permute-start | bytes 393224 | tf_op jit(solution)/shard_map/ppermute | solution.py:104
  37.4 12.2 %collective-permute-start.5 = (bf16[128,256]{1,0:T(8,128)(2,1)S(1)}, bf16[128,256]{1,0:T(8,128)(2,1)S(1)}, u32[]{:S(2)}, u32[]{:S(2)}) collective-permute-start(bf16[128,256]{1,0:T(8,128)(2,1)S(1)} %copy-done), channel_id=1, source_target_pairs={{0,1},{1,0},{2,3},{3,2},{4,5},{5,4},{6,7},{7,6},{8,9},{9,8},{10,11... | collective-permute-start | bytes 196616 | tf_op jit(solution)/shard_map/ppermute | solution.py:106
  39.3 10.1 %collective-permute-start.1 = (bf16[256,256]{1,0:T(8,128)(2,1)S(1)}, bf16[256,256]{1,0:T(8,128)(2,1)S(1)}, u32[]{:S(2)}, u32[]{:S(2)}) collective-permute-start(bf16[256,256]{1,0:T(8,128)(2,1)S(1)} %get-tuple-element.36), channel_id=1, source_target_pairs={{0,32},{2,34},{4,36},{6,38},{8,40},{10,42},{12,44},{14,46},{16,48}... | collective-permute-start | bytes 393224 | tf_op jit(solution)/shard_map/ppermute | solution.py:104
  74.7 11.3 %collective-permute-start.6 = (bf16[128,512]{1,0:T(8,128)(2,1)S(1)}, bf16[128,512]{1,0:T(8,128)(2,1)S(1)}, u32[]{:S(2)}, u32[]{:S(2)}) collective-permute-start(bf16[128,512]{1,0:T(8,128)(2,1)S(1)} %fusion.13), channel_id=1, source_target_pairs={{1,256},{256,1},{3,320},{320,3},{5,384},{384,5},{7,448},{448,7},{9... | collective-permute-start | bytes 393224 | tf_op jit(solution)/shard_map/ppermute | solution.py:129
  87.1 24.8 %all-to-all-start.2 = ((bf16[8,128,512]{2,1,0:T(8,128)(2,1)}), bf16[8,128,512]{2,1,0:T(8,128)(2,1)S(1)}, u32[]{:S(2)}, u32[]{:S(2)}) async-start(bf16[8,128,512]{2,1,0:T(8,128)(2,1)} %broadcast_in_dim.7), calls=%async_computation.2 | async-start | bytes 2097152 | tf_op jit(solution)/shard_map/all_to_all | solution.py:74
  93.0 3.9 %collective-permute-start.7 = (bf16[128,256]{1,0:T(8,128)(2,1)S(1)}, bf16[128,256]{1,0:T(8,128)(2,1)S(1)}, u32[]{:S(2)}, u32[]{:S(2)}) collective-permute-start(bf16[128,256]{1,0:T(8,128)(2,1)S(1)} %slice.140), channel_id=1, source_target_pairs={{0,1},{1,0},{2,3},{3,2},{4,5},{5,4},{6,7},{7,6},{8,9},{9,8},{10,11... | collective-permute-start | bytes 196616 | tf_op jit(solution)/shard_map/ppermute | solution.py:134
  116.6 29.6 %all-to-all-start.3 = ((bf16[16,128,256]{2,1,0:T(8,128)(2,1)}), bf16[16,128,256]{2,1,0:T(8,128)(2,1)S(1)}, u32[]{:S(2)}, u32[]{:S(2)}) async-start(bf16[16,128,256]{2,1,0:T(8,128)(2,1)} %bitcast.18), calls=%async_computation.3 | async-start | bytes 2097152 | tf_op jit(solution)/shard_map/all_to_all | solution.py:74
  126.4 19.1 %collective-permute-start.11 = (f32[256,256]{1,0:T(8,128)S(1)}, f32[256,256]{1,0:T(8,128)S(1)}, u32[]{:S(2)}, u32[]{:S(2)}) collective-permute-start(f32[256,256]{1,0:T(8,128)S(1)} %slice_bitcast_fusion), channel_id=1, source_target_pairs={{0,1},{1,0},{2,3},{3,2},{4,5},{5,4},{6,7},{7,6},{8,9},{9,8},{10,11... | collective-permute-start | bytes 786440 | tf_op jit(solution)/shard_map/ppermute | solution.py:144
  128.6 12.5 %collective-permute-start.12 = (bf16[256,256]{1,0:T(8,128)(2,1)S(1)}, bf16[256,256]{1,0:T(8,128)(2,1)S(1)}, u32[]{:S(2)}, u32[]{:S(2)}) collective-permute-start(bf16[256,256]{1,0:T(8,128)(2,1)S(1)} %fusion.12), channel_id=1, source_target_pairs={{32,1},{34,3},{36,5},{38,7},{40,9},{42,11},{44,13},{46,15},{48,17}... | collective-permute-start | bytes 393224 | tf_op jit(solution)/shard_map/ppermute | solution.py:149
  132.0 13.4 %collective-permute-start.10 = (bf16[256,256]{1,0:T(8,128)(2,1)S(1)}, bf16[256,256]{1,0:T(8,128)(2,1)S(1)}, u32[]{:S(2)}, u32[]{:S(2)}) collective-permute-start(bf16[256,256]{1,0:T(8,128)(2,1)S(1)} %fusion.11), channel_id=1, source_target_pairs={{0,32},{2,34},{4,36},{6,38},{8,40},{10,42},{12,44},{14,46},{16,48}... | collective-permute-start | bytes 393224 | tf_op jit(solution)/shard_map/ppermute | solution.py:148
  146.4 5.8 %collective-permute-start.9 = (bf16[128,128]{1,0:T(8,128)(2,1)S(1)}, bf16[128,128]{1,0:T(8,128)(2,1)S(1)}, u32[]{:S(2)}, u32[]{:S(2)}) collective-permute-start(bf16[128,128]{1,0:T(8,128)(2,1)S(1)} %get-tuple-element.50), channel_id=1, source_target_pairs={{0,0},{1,1},{2,2},{3,3},{4,4},{5,5},{6,6},{7,7},{8,8},{9,9},{10,10... | collective-permute-start | bytes 98312 | tf_op jit(solution)/shard_map/ppermute | solution.py:146
  148.3 5.2 %collective-permute-start.8 = (bf16[128,128]{1,0:T(8,128)(2,1)S(1)}, bf16[128,128]{1,0:T(8,128)(2,1)S(1)}, u32[]{:S(2)}, u32[]{:S(2)}) collective-permute-start(bf16[128,128]{1,0:T(8,128)(2,1)S(1)} %get-tuple-element.51), channel_id=1, source_target_pairs={{0,1},{1,0},{2,3},{3,2},{4,5},{5,4},{6,7},{7,6},{8,9},{9,8},{10,11... | collective-permute-start | bytes 98312 | tf_op jit(solution)/shard_map/ppermute | solution.py:147

commit v5 on v4

--- a/solution.py
+++ b/solution.py
@@ -101,22 +101,17 @@
     out_t = out_weight.T
     mine = jnp.where(first, gate_weight, fold(out_t))
     yours = jnp.where(first, fold(out_t), gate_weight)
-    weights_in = [lax.ppermute(yours, ALL, SWAP), lax.ppermute(mine, ALL, PARTNER), lax.ppermute(yours, ALL, PARTNER_SWAP)]
+    own, other, swapped = lax.optimization_barrier((own, other, lax.ppermute(yours, ALL, SWAP)))
     acts = gather(jnp.concatenate([own, other], axis=1), WIDE)
     mixer_in = lax.ppermute(mixer_out, ALL, SWAP)
     acts, mixer_in = lax.optimization_barrier((acts, mixer_in))
     acts = acts.reshape(2, N * acts.shape[1], acts.shape[2])
-    blocks = [(mine, weights_in[0]), weights_in[1:]]
-    weight = jnp.stack(
-        [
-            jnp.where(
-                first,
-                jnp.concatenate(pair, axis=1),
-                jnp.concatenate([unfold(block) for block in pair], axis=0),
-            )
-            for pair in blocks
-        ]
+    weight = jnp.where(
+        first,
+        jnp.concatenate([mine, swapped], axis=1),
+        jnp.concatenate([unfold(mine), unfold(swapped)], axis=0),
     )
+    weight = jnp.stack([weight, lax.ppermute(weight, ALL, PARTNER)])
     mixer_vals = jnp.concatenate([mixer_out, mixer_in], axis=1).astype(f32)
 
     partial = jnp.einsum("kad,kdn->an", acts, weight, preferred_element_type=f32)
@@ -135,7 +130,8 @@
     units, mixer_grad_in = lax.optimization_barrier((units, mixer_grad_in))
     units = units.reshape(-1, units.shape[2])
 
-    layer_part = jnp.einsum("an,kdn->kad", units, weight, preferred_element_type=f32)
+    parts = [lax.dot_general(units, w, (((1,), (1,)), ((), ())), preferred_element_type=f32).astype(bf16) for w in weight]
+    layer_part, units = lax.optimization_barrier((jnp.stack(parts), units))
     layer_pair = reduce(layer_part.reshape(2 * N, -1, layer_part.shape[2]), WIDE).astype(bf16)
 
     grads = jnp.einsum("kad,an->kdn", acts, units, preferred_element_type=f32)

time: 156 us -> 153 us (0.981)
  starting transfers between devices: 69.7 us -> 65.8 us
  waiting for transfers between devices: 45.9 us -> 48.7 us
  local copies, waits for them, and re-layouts: 6.49 us -> 4.2 us
    all_to_all x3, waiting for transfers between devices: 15 us -> 21.9 us  [trade(): lax.all_to_all(blocks, ALL, split_axis=0, concat_axis=0, axis_index_group...]
    ppermute x1, waiting for transfers between devices: 5.88 us -> 0.01 us  [local(): other = lax.ppermute(jnp.where(first, out_grad, tokens), ALL, SPREAD_OTHER)]
    ppermute x2 -> x1, starting transfers between devices: 6.51 us -> 1.92 us  [local(): weight = jnp.stack([weight, lax.ppermute(weight, ALL, PARTNER)])]
    ppermute x1, waiting for transfers between devices: 0.01 us -> 2.78 us  [local(): own = lax.ppermute(jnp.where(first, tokens, out_grad), ALL, SPREAD_OWN)]
    ppermute x2 -> x1, waiting for transfers between devices: 5.38 us -> 3.03 us  [local(): weight = jnp.stack([weight, lax.ppermute(weight, ALL, PARTNER)])]
    convert_element_type x1 -> x0, local copies, waits for them, and re-layouts: 2.27 us -> none  [reduce(): partial.astype(jnp.bfloat16)]
    ppermute x1, starting transfers between devices: 4.09 us -> 1.92 us  [local(): lax.ppermute(jnp.where(first, gated, total.astype(bf16)), ALL, CROSS)]
    ppermute x1, waiting for transfers between devices: 7.15 us -> 9.27 us  [local(): lax.ppermute(jnp.where(first, gated, total.astype(bf16)), ALL, CROSS)]
  transfers between devices with their start and end apart: 16 -> 15, of which waited for: 10 -> 11; matrix products, arithmetic and copies ran while one was open for 3% -> 2% of each run, Pallas kernels for 0% -> 0%
where the time goes in v5:
time: 153 us; the launch traced here: 152 us
  starting transfers between devices  65.8 us (43%)
  waiting for transfers between devices  48.7 us (32%)
  blocking collectives  25.2 us (16%)
  other arithmetic  5.01 us (3%)
  local copies, waits for them, and re-layouts  4.2 us (3%)
  matrix products  2.36 us (2%)
    all_to_all x3, starting transfers between devices, trade(): lax.all_to_all(blocks, ALL, split_axis=0, concat_axis=0, axis_index_group...  30.1 us
    all_to_all x1, blocking collectives, trade(): lax.all_to_all(blocks, ALL, split_axis=0, concat_axis=0, axis_index_group...  25.2 us
    all_to_all x3, waiting for transfers between devices, trade(): lax.all_to_all(blocks, ALL, split_axis=0, concat_axis=0, axis_index_group...  21.9 us
    ppermute x1, waiting for transfers between devices, local(): lax.ppermute(jnp.where(first, gated, total.astype(bf16)), ALL, CROSS)  9.27 us
    ppermute x1, starting transfers between devices, local(): own = lax.ppermute(jnp.where(first, tokens, out_grad), ALL, SPREAD_OWN)  6.61 us
    ppermute x1, starting transfers between devices, local(): mixer_grad_in = lax.ppermute(mixer_grad[:, inner:], ALL, SWAP)  4.45 us
    ppermute x1, starting transfers between devices, local(): lax.ppermute(keep_far, ALL, PARTNER).astype(f32)  4.13 us
    ppermute x1, waiting for transfers between devices, local(): lax.ppermute(send_far, ALL, SWAP_PARTNER).astype(f32)  3.8 us
  transfers between devices with their start and end apart: 15, of which 11 were waited for; matrix products, arithmetic and copies ran while one was open for 2% of the time, Pallas kernels for 0%

profile of v5, /device:TPU:2, one launch (start us, length us, event | category | flops | bytes accessed | tf_op | source)
XLA Modules:
  0.0 152.3 jit_solution(14650611345262888123)
XLA Ops:
  0.6 0.0 copy-start.3
  0.6 0.0 copy-start.4
  0.7 1.0 copy.12
  1.7 1.0 broadcast_select_fusion.2
  2.7 1.9 %collective-permute-start.2 = (bf16[256,256]{1,0:T(8,128)(2,1)S(1)}, bf16[256,256]{1,0:T(8,128)(2,1)S(1)}, u32[]{:S(2)}, u32[]{:S(2)}) collective-permute-start(bf16[256,256]{1,0:T(8,128)(2,1)S(1)} %get-tuple-element.47), channel_id=1, source_target_pairs={{0,1},{1,0},{2,3},{3,2},{4,5},{5,4},{6,7},{7,6},{8,9},{9,8},{10,11... | collective-permute-start | bytes 393224 | tf_op jit(solution)/shard_map/ppermute | solution.py:104
  4.6 0.0 copy-done.3
  4.6 0.0 copy-done.4
  4.6 3.5 %collective-permute-start.1 = (bf16[128,128]{1,0:T(8,128)(2,1)S(1)}, bf16[128,128]{1,0:T(8,128)(2,1)S(1)}, u32[]{:S(2)}, u32[]{:S(2)}) collective-permute-start(bf16[128,128]{1,0:T(8,128)(2,1)S(1)} %get-tuple-element.58), channel_id=1, source_target_pairs={{1,8},{0,1},{3,26},{2,3},{5,74},{4,5},{7,92},{6,7},{9,140},{8,9},{... | collective-permute-start | bytes 98312 | tf_op jit(solution)/shard_map/ppermute | solution.py:100
  8.1 6.6 %collective-permute-start = (bf16[128,128]{1,0:T(8,128)(2,1)S(1)}, bf16[128,128]{1,0:T(8,128)(2,1)S(1)}, u32[]{:S(2)}, u32[]{:S(2)}) collective-permute-start(bf16[128,128]{1,0:T(8,128)(2,1)S(1)} %get-tuple-element.59), channel_id=1, source_target_pairs={{0,8},{1,1},{2,26},{3,3},{4,74},{5,5},{6,92},{7,7},{8,140},{9,9},{... | collective-permute-start | bytes 98312 | tf_op jit(solution)/shard_map/ppermute | solution.py:99
  14.7 0.0 collective-permute-done.1
  14.8 2.8 %collective-permute-done = bf16[128,128]{1,0:T(8,128)(2,1)S(1)} collective-permute-done((bf16[128,128]{1,0:T(8,128)(2,1)S(1)}, bf16[128,128]{1,0:T(8,128)(2,1)S(1)}, u32[]{:S(2)}, u32[]{:S(2)}) %collective-permute-start) | collective-permute-done | bytes 32800 | tf_op jit(solution)/shard_map/ppermute | solution.py:99
  17.5 0.0 collective-permute-done.2
  17.6 1.1 broadcast_in_dim.6
  18.6 15.7 %all-to-all-start = ((bf16[16,128,256]{2,1,0:T(8,128)(2,1)}), bf16[16,128,256]{2,1,0:T(8,128)(2,1)S(1)}, u32[]{:S(2)}, u32[]{:S(2)}) async-start(bf16[16,128,256]{2,1,0:T(8,128)(2,1)} %broadcast_in_dim.6), calls=%async_computation | async-start | bytes 2097152 | tf_op jit(solution)/shard_map/all_to_all | solution.py:74
  34.3 0.0 copy-start
  34.4 0.1 maximum_select_fusion.1
  34.5 1.9 %collective-permute-start.4 = (bf16[256,512]{1,0:T(8,128)(2,1)S(1)}, bf16[256,512]{1,0:T(8,128)(2,1)S(1)}, u32[]{:S(2)}, u32[]{:S(2)}) collective-permute-start(bf16[256,512]{1,0:T(8,128)(2,1)S(1)} %maximum_select_fusion.1), channel_id=1, source_target_pairs={{0,32},{2,34},{4,36},{6,38},{8,40},{10,42},{12,44},{14,46},{16,48}... | collective-permute-start | bytes 786440 | tf_op jit(solution)/shard_map/ppermute | solution.py:114
  36.4 0.0 copy-done
  36.4 1.9 %collective-permute-start.3 = (bf16[128,256]{1,0:T(8,128)(2,1)S(1)}, bf16[128,256]{1,0:T(8,128)(2,1)S(1)}, u32[]{:S(2)}, u32[]{:S(2)}) collective-permute-start(bf16[128,256]{1,0:T(8,128)(2,1)S(1)} %copy-done), channel_id=1, source_target_pairs={{0,1},{1,0},{2,3},{3,2},{4,5},{5,4},{6,7},{7,6},{8,9},{9,8},{10,11... | collective-permute-start | bytes 196616 | tf_op jit(solution)/shard_map/ppermute | solution.py:106
  38.4 0.1 maximum_select_fusion
  38.4 1.1 collective-permute-done.3
  39.5 8.3 %all-to-all-done = bf16[16,128,256]{2,1,0:T(8,128)(2,1)S(1)} async-done(((bf16[16,128,256]{2,1,0:T(8,128)(2,1)}), bf16[16,128,256]{2,1,0:T(8,128)(2,1)S(1)}, u32[]{:S(2)}, u32[]{:S(2)}) %all-to-all-start) | async-done | bytes 1048608 | tf_op jit(solution)/shard_map/all_to_all | solution.py:74
  47.9 3.0 %collective-permute-done.4 = bf16[256,512]{1,0:T(8,128)(2,1)S(1)} collective-permute-done((bf16[256,512]{1,0:T(8,128)(2,1)S(1)}, bf16[256,512]{1,0:T(8,128)(2,1)S(1)}, u32[]{:S(2)}, u32[]{:S(2)}) %collective-permute-start.4) | collective-permute-done | bytes 262176 | tf_op jit(solution)/shard_map/ppermute | solution.py:114
  50.9 0.7 bitcast_convert_fusion
  51.6 25.2 %all_to_all.20 = bf16[8,128,512]{2,1,0:T(8,128)(2,1)S(1)} all-to-all(bf16[8,128,512]{2,1,0:T(8,128)(2,1)S(1)} %bitcast_convert_fusion), channel_id=1, replica_groups={{0,64,128,192,256,320,384,448},{2,66,130,194,258,322,386,450},{4,68,132..., dimensions={0} | all-to-all | bytes 2097152 | tf_op jit(solution)/shard_map/all_to_all | solution.py:74
  76.8 0.1 convert_reduce_fusion
  76.9 0.1 fusion.17
  77.0 1.9 %collective-permute-start.5 = (bf16[128,512]{1,0:T(8,128)(2,1)S(1)}, bf16[128,512]{1,0:T(8,128)(2,1)S(1)}, u32[]{:S(2)}, u32[]{:S(2)}) collective-permute-start(bf16[128,512]{1,0:T(8,128)(2,1)S(1)} %fusion.17), channel_id=1, source_target_pairs={{1,256},{256,1},{3,320},{320,3},{5,384},{384,5},{7,448},{448,7},{9... | collective-permute-start | bytes 393224 | tf_op jit(solution)/shard_map/ppermute | solution.py:124
  79.0 9.3 %collective-permute-done.5 = bf16[128,512]{1,0:T(8,128)(2,1)S(1)} collective-permute-done((bf16[128,512]{1,0:T(8,128)(2,1)S(1)}, bf16[128,512]{1,0:T(8,128)(2,1)S(1)}, u32[]{:S(2)}, u32[]{:S(2)}) %collective-permute-start.5) | collective-permute-done | bytes 131104 | tf_op jit(solution)/shard_map/ppermute | solution.py:124
  88.2 0.1 fusion.14
  88.4 1.1 broadcast_in_dim.7
  89.4 4.2 %all-to-all-start.2 = ((bf16[8,128,512]{2,1,0:T(8,128)(2,1)}), bf16[8,128,512]{2,1,0:T(8,128)(2,1)S(1)}, u32[]{:S(2)}, u32[]{:S(2)}) async-start(bf16[8,128,512]{2,1,0:T(8,128)(2,1)} %broadcast_in_dim.7), calls=%async_computation.2 | async-start | bytes 2097152 | tf_op jit(solution)/shard_map/all_to_all | solution.py:74
  93.7 0.1 fusion.10
  93.8 4.5 %collective-permute-start.6 = (bf16[128,256]{1,0:T(8,128)(2,1)S(1)}, bf16[128,256]{1,0:T(8,128)(2,1)S(1)}, u32[]{:S(2)}, u32[]{:S(2)}) collective-permute-start(bf16[128,256]{1,0:T(8,128)(2,1)S(1)} %slice.118), channel_id=1, source_target_pairs={{0,1},{1,0},{2,3},{3,2},{4,5},{5,4},{6,7},{7,6},{8,9},{9,8},{10,11... | collective-permute-start | bytes 196616 | tf_op jit(solution)/shard_map/ppermute | solution.py:129
  98.3 0.9 collective-permute-done.6
  99.1 0.0 copy-start.1
  99.1 13.5 %all-to-all-done.2 = bf16[8,128,512]{2,1,0:T(8,128)(2,1)S(1)} async-done(((bf16[8,128,512]{2,1,0:T(8,128)(2,1)}), bf16[8,128,512]{2,1,0:T(8,128)(2,1)S(1)}, u32[]{:S(2)}, u32[]{:S(2)}) %all-to-all-start.2) | async-done | bytes 1048608 | tf_op jit(solution)/shard_map/all_to_all | solution.py:74
  112.7 0.5 fusion
  113.1 0.5 fusion.1
  113.6 0.0 copy-done.1
  113.6 1.1 pad_maximum_fusion
  114.7 10.1 %all-to-all-start.3 = ((bf16[16,128,256]{2,1,0:T(8,128)(2,1)}), bf16[16,128,256]{2,1,0:T(8,128)(2,1)S(1)}, u32[]{:S(2)}, u32[]{:S(2)}) async-start(bf16[16,128,256]{2,1,0:T(8,128)(2,1)} %bitcast.15), calls=%async_computation.3 | async-start | bytes 2097152 | tf_op jit(solution)/shard_map/all_to_all | solution.py:74
  124.8 0.7 fusion.2
  125.5 0.1 slice_bitcast_fusion.5
  125.8 0.2 slice_select_fusion.1
  126.0 0.0 copy-start.2
  126.0 1.9 %collective-permute-start.10 = (f32[256,256]{1,0:T(8,128)S(1)}, f32[256,256]{1,0:T(8,128)S(1)}, u32[]{:S(2)}, u32[]{:S(2)}) collective-permute-start(f32[256,256]{1,0:T(8,128)S(1)} %slice_bitcast_fusion), channel_id=1, source_target_pairs={{0,1},{1,0},{2,3},{3,2},{4,5},{5,4},{6,7},{7,6},{8,9},{9,8},{10,11... | collective-permute-start | bytes 786440 | tf_op jit(solution)/shard_map/ppermute | solution.py:140
  128.0 3.3 %collective-permute-start.11 = (bf16[256,256]{1,0:T(8,128)(2,1)S(1)}, bf16[256,256]{1,0:T(8,128)(2,1)S(1)}, u32[]{:S(2)}, u32[]{:S(2)}) collective-permute-start(bf16[256,256]{1,0:T(8,128)(2,1)S(1)} %fusion.16), channel_id=1, source_target_pairs={{32,1},{34,3},{36,5},{38,7},{40,9},{42,11},{44,13},{46,15},{48,17}... | collective-permute-start | bytes 393224 | tf_op jit(solution)/shard_map/ppermute | solution.py:145
  131.3 4.1 %collective-permute-start.9 = (bf16[256,256]{1,0:T(8,128)(2,1)S(1)}, bf16[256,256]{1,0:T(8,128)(2,1)S(1)}, u32[]{:S(2)}, u32[]{:S(2)}) collective-permute-start(bf16[256,256]{1,0:T(8,128)(2,1)S(1)} %fusion.15), channel_id=1, source_target_pairs={{0,32},{2,34},{4,36},{6,38},{8,40},{10,42},{12,44},{14,46},{16,48}... | collective-permute-start | bytes 393224 | tf_op jit(solution)/shard_map/ppermute | solution.py:144
  135.5 0.0 copy-done.2
  135.5 0.6 slice_select_fusion.2
  136.1 3.8 %collective-permute-done.11 = bf16[256,256]{1,0:T(8,128)(2,1)S(1)} collective-permute-done((bf16[256,256]{1,0:T(8,128)(2,1)S(1)}, bf16[256,256]{1,0:T(8,128)(2,1)S(1)}, u32[]{:S(2)}, u32[]{:S(2)}) %collective-permute-start.11) | collective-permute-done | bytes 131104 | tf_op jit(solution)/shard_map/ppermute | solution.py:145
  139.9 3.4 %collective-permute-done.9 = bf16[256,256]{1,0:T(8,128)(2,1)S(1)} collective-permute-done((bf16[256,256]{1,0:T(8,128)(2,1)S(1)}, bf16[256,256]{1,0:T(8,128)(2,1)S(1)}, u32[]{:S(2)}, u32[]{:S(2)}) %collective-permute-start.9) | collective-permute-done | bytes 131104 | tf_op jit(solution)/shard_map/ppermute | solution.py:144
  143.3 0.0 collective-permute-done.10
  143.3 0.7 broadcast_select_fusion
  144.0 0.0 all-to-all-done.3
  144.0 0.1 reduce_sum.22
  144.2 2.2 %collective-permute-start.8 = (bf16[128,128]{1,0:T(8,128)(2,1)S(1)}, bf16[128,128]{1,0:T(8,128)(2,1)S(1)}, u32[]{:S(2)}, u32[]{:S(2)}) collective-permute-start(bf16[128,128]{1,0:T(8,128)(2,1)S(1)} %get-tuple-element.56), channel_id=1, source_target_pairs={{0,0},{1,1},{2,2},{3,3},{4,4},{5,5},{6,6},{7,7},{8,8},{9,9},{10,10... | collective-permute-start | bytes 98312 | tf_op jit(solution)/shard_map/ppermute | solution.py:142
  146.4 1.9 %collective-permute-start.7 = (bf16[128,128]{1,0:T(8,128)(2,1)S(1)}, bf16[128,128]{1,0:T(8,128)(2,1)S(1)}, u32[]{:S(2)}, u32[]{:S(2)}) collective-permute-start(bf16[128,128]{1,0:T(8,128)(2,1)S(1)} %get-tuple-element.57), channel_id=1, source_target_pairs={{0,1},{1,0},{2,3},{3,2},{4,5},{5,4},{6,7},{7,6},{8,9},{9,8},{10,11... | collective-permute-start | bytes 98312 | tf_op jit(solution)/shard_map/ppermute | solution.py:143
  148.3 0.8 copy.15
  149.1 0.9 collective-permute-done.8
  150.0 1.6 %collective-permute-done.7 = bf16[128,128]{1,0:T(8,128)(2,1)S(1)} collective-permute-done((bf16[128,128]{1,0:T(8,128)(2,1)S(1)}, bf16[128,128]{1,0:T(8,128)(2,1)S(1)}, u32[]{:S(2)}, u32[]{:S(2)}) %collective-permute-start.7) | collective-permute-done | bytes 32800 | tf_op jit(solution)/shard_map/ppermute | solution.py:143
  151.6 0.6 broadcast_select_fusion.4
  (21 shorter events, 0.3 us)
Async XLA Ops:
  0.6 4.0 %copy-start.3 = (bf16[128,128]{1,0:T(8,128)(2,1)S(1)}, bf16[128,128]{1,0:T(8,128)(2,1)}, u32[]{:S(2)}) copy-start(bf16[128,128]{1,0:T(8,128)(2,1)} %param.9) | copy-start | bytes 98308
  0.6 4.0 %copy-start.4 = (bf16[128,128]{1,0:T(8,128)(2,1)S(1)}, bf16[128,128]{1,0:T(8,128)(2,1)}, u32[]{:S(2)}) copy-start(bf16[128,128]{1,0:T(8,128)(2,1)} %param.5) | copy-start | bytes 98308
  2.7 14.9 %collective-permute-start.2 = (bf16[256,256]{1,0:T(8,128)(2,1)S(1)}, bf16[256,256]{1,0:T(8,128)(2,1)S(1)}, u32[]{:S(2)}, u32[]{:S(2)}) collective-permute-start(bf16[256,256]{1,0:T(8,128)(2,1)S(1)} %get-tuple-element.47), channel_id=1, source_target_pairs={{0,1},{1,0},{2,3},{3,2},{4,5},{5,4},{6,7},{7,6},{8,9},{9,8},{10,11... | collective-permute-start | bytes 393224 | tf_op jit(solution)/shard_map/ppermute | solution.py:104
  4.6 10.1 %collective-permute-start.1 = (bf16[128,128]{1,0:T(8,128)(2,1)S(1)}, bf16[128,128]{1,0:T(8,128)(2,1)S(1)}, u32[]{:S(2)}, u32[]{:S(2)}) collective-permute-start(bf16[128,128]{1,0:T(8,128)(2,1)S(1)} %get-tuple-element.58), channel_id=1, source_target_pairs={{1,8},{0,1},{3,26},{2,3},{5,74},{4,5},{7,92},{6,7},{9,140},{8,9},{... | collective-permute-start | bytes 98312 | tf_op jit(solution)/shard_map/ppermute | solution.py:100
  8.1 9.4 %collective-permute-start = (bf16[128,128]{1,0:T(8,128)(2,1)S(1)}, bf16[128,128]{1,0:T(8,128)(2,1)S(1)}, u32[]{:S(2)}, u32[]{:S(2)}) collective-permute-start(bf16[128,128]{1,0:T(8,128)(2,1)S(1)} %get-tuple-element.59), channel_id=1, source_target_pairs={{0,8},{1,1},{2,26},{3,3},{4,74},{5,5},{6,92},{7,7},{8,140},{9,9},{... | collective-permute-start | bytes 98312 | tf_op jit(solution)/shard_map/ppermute | solution.py:99
  18.6 29.2 %all-to-all-start = ((bf16[16,128,256]{2,1,0:T(8,128)(2,1)}), bf16[16,128,256]{2,1,0:T(8,128)(2,1)S(1)}, u32[]{:S(2)}, u32[]{:S(2)}) async-start(bf16[16,128,256]{2,1,0:T(8,128)(2,1)} %broadcast_in_dim.6), calls=%async_computation | async-start | bytes 2097152 | tf_op jit(solution)/shard_map/all_to_all | solution.py:74
  34.3 2.0 %copy-start = (bf16[128,256]{1,0:T(8,128)(2,1)S(1)}, bf16[128,256]{1,0:T(8,128)(2,1)}, u32[]{:S(2)}) copy-start(bf16[128,256]{1,0:T(8,128)(2,1)} %param.6) | copy-start | bytes 196612
  34.5 16.4 %collective-permute-start.4 = (bf16[256,512]{1,0:T(8,128)(2,1)S(1)}, bf16[256,512]{1,0:T(8,128)(2,1)S(1)}, u32[]{:S(2)}, u32[]{:S(2)}) collective-permute-start(bf16[256,512]{1,0:T(8,128)(2,1)S(1)} %maximum_select_fusion.1), channel_id=1, source_target_pairs={{0,32},{2,34},{4,36},{6,38},{8,40},{10,42},{12,44},{14,46},{16,48}... | collective-permute-start | bytes 786440 | tf_op jit(solution)/shard_map/ppermute | solution.py:114
  36.4 3.1 %collective-permute-start.3 = (bf16[128,256]{1,0:T(8,128)(2,1)S(1)}, bf16[128,256]{1,0:T(8,128)(2,1)S(1)}, u32[]{:S(2)}, u32[]{:S(2)}) collective-permute-start(bf16[128,256]{1,0:T(8,128)(2,1)S(1)} %copy-done), channel_id=1, source_target_pairs={{0,1},{1,0},{2,3},{3,2},{4,5},{5,4},{6,7},{7,6},{8,9},{9,8},{10,11... | collective-permute-start | bytes 196616 | tf_op jit(solution)/shard_map/ppermute | solution.py:106
  77.0 11.2 %collective-permute-start.5 = (bf16[128,512]{1,0:T(8,128)(2,1)S(1)}, bf16[128,512]{1,0:T(8,128)(2,1)S(1)}, u32[]{:S(2)}, u32[]{:S(2)}) collective-permute-start(bf16[128,512]{1,0:T(8,128)(2,1)S(1)} %fusion.17), channel_id=1, source_target_pairs={{1,256},{256,1},{3,320},{320,3},{5,384},{384,5},{7,448},{448,7},{9... | collective-permute-start | bytes 393224 | tf_op jit(solution)/shard_map/ppermute | solution.py:124
  89.4 23.2 %all-to-all-start.2 = ((bf16[8,128,512]{2,1,0:T(8,128)(2,1)}), bf16[8,128,512]{2,1,0:T(8,128)(2,1)S(1)}, u32[]{:S(2)}, u32[]{:S(2)}) async-start(bf16[8,128,512]{2,1,0:T(8,128)(2,1)} %broadcast_in_dim.7), calls=%async_computation.2 | async-start | bytes 2097152 | tf_op jit(solution)/shard_map/all_to_all | solution.py:74
  93.8 5.3 %collective-permute-start.6 = (bf16[128,256]{1,0:T(8,128)(2,1)S(1)}, bf16[128,256]{1,0:T(8,128)(2,1)S(1)}, u32[]{:S(2)}, u32[]{:S(2)}) collective-permute-start(bf16[128,256]{1,0:T(8,128)(2,1)S(1)} %slice.118), channel_id=1, source_target_pairs={{0,1},{1,0},{2,3},{3,2},{4,5},{5,4},{6,7},{7,6},{8,9},{9,8},{10,11... | collective-permute-start | bytes 196616 | tf_op jit(solution)/shard_map/ppermute | solution.py:129
  99.1 14.4 %copy-start.1 = (bf16[128,256]{1,0:T(8,128)(2,1)}, bf16[128,256]{1,0:T(8,128)(2,1)S(1)}, u32[]{:S(2)}) copy-start(bf16[128,256]{1,0:T(8,128)(2,1)S(1)} %collective-permute-done.6) | copy-start | bytes 196612
  114.7 29.4 %all-to-all-start.3 = ((bf16[16,128,256]{2,1,0:T(8,128)(2,1)}), bf16[16,128,256]{2,1,0:T(8,128)(2,1)S(1)}, u32[]{:S(2)}, u32[]{:S(2)}) async-start(bf16[16,128,256]{2,1,0:T(8,128)(2,1)} %bitcast.15), calls=%async_computation.3 | async-start | bytes 2097152 | tf_op jit(solution)/shard_map/all_to_all | solution.py:74
  126.0 9.5 %copy-start.2 = (bf16[128,256]{1,0:T(8,128)(2,1)S(1)}, bf16[128,256]{1,0:T(8,128)(2,1)}, u32[]{:S(2)}) copy-start(bf16[128,256]{1,0:T(8,128)(2,1)} %copy-done.1) | copy-start | bytes 196612
  126.0 17.3 %collective-permute-start.10 = (f32[256,256]{1,0:T(8,128)S(1)}, f32[256,256]{1,0:T(8,128)S(1)}, u32[]{:S(2)}, u32[]{:S(2)}) collective-permute-start(f32[256,256]{1,0:T(8,128)S(1)} %slice_bitcast_fusion), channel_id=1, source_target_pairs={{0,1},{1,0},{2,3},{3,2},{4,5},{5,4},{6,7},{7,6},{8,9},{9,8},{10,11... | collective-permute-start | bytes 786440 | tf_op jit(solution)/shard_map/ppermute | solution.py:140
  128.0 11.9 %collective-permute-start.11 = (bf16[256,256]{1,0:T(8,128)(2,1)S(1)}, bf16[256,256]{1,0:T(8,128)(2,1)S(1)}, u32[]{:S(2)}, u32[]{:S(2)}) collective-permute-start(bf16[256,256]{1,0:T(8,128)(2,1)S(1)} %fusion.16), channel_id=1, source_target_pairs={{32,1},{34,3},{36,5},{38,7},{40,9},{42,11},{44,13},{46,15},{48,17}... | collective-permute-start | bytes 393224 | tf_op jit(solution)/shard_map/ppermute | solution.py:145
  131.3 12.0 %collective-permute-start.9 = (bf16[256,256]{1,0:T(8,128)(2,1)S(1)}, bf16[256,256]{1,0:T(8,128)(2,1)S(1)}, u32[]{:S(2)}, u32[]{:S(2)}) collective-permute-start(bf16[256,256]{1,0:T(8,128)(2,1)S(1)} %fusion.15), channel_id=1, source_target_pairs={{0,32},{2,34},{4,36},{6,38},{8,40},{10,42},{12,44},{14,46},{16,48}... | collective-permute-start | bytes 393224 | tf_op jit(solution)/shard_map/ppermute | solution.py:144
  144.2 5.8 %collective-permute-start.8 = (bf16[128,128]{1,0:T(8,128)(2,1)S(1)}, bf16[128,128]{1,0:T(8,128)(2,1)S(1)}, u32[]{:S(2)}, u32[]{:S(2)}) collective-permute-start(bf16[128,128]{1,0:T(8,128)(2,1)S(1)} %get-tuple-element.56), channel_id=1, source_target_pairs={{0,0},{1,1},{2,2},{3,3},{4,4},{5,5},{6,6},{7,7},{8,8},{9,9},{10,10... | collective-permute-start | bytes 98312 | tf_op jit(solution)/shard_map/ppermute | solution.py:142
  146.4 5.3 %collective-permute-start.7 = (bf16[128,128]{1,0:T(8,128)(2,1)S(1)}, bf16[128,128]{1,0:T(8,128)(2,1)S(1)}, u32[]{:S(2)}, u32[]{:S(2)}) collective-permute-start(bf16[128,128]{1,0:T(8,128)(2,1)S(1)} %get-tuple-element.57), channel_id=1, source_target_pairs={{0,1},{1,0},{2,3},{3,2},{4,5},{5,4},{6,7},{7,6},{8,9},{9,8},{10,11... | collective-permute-start | bytes 98312 | tf_op jit(solution)/shard_map/ppermute | solution.py:143

commit v6 on v5

--- a/solution.py
+++ b/solution.py
@@ -34,6 +34,12 @@
 ] + [
     [device(a, xl ^ rel, xl, z, 1) for rel in (0, 1) for a in range(N)] for xl in (0, 1) for z in range(N)
 ]
+ROW_GROUPS = [
+    [device(a, xl ^ rel, xl, z, core) for rel in (0, 1) for a in range(N)]
+    for core in (0, 1)
+    for xl in (0, 1)
+    for z in range(N)
+]
 NARROW = [[device(a, xh, xl, z, 0) for a in range(N)] for xh in (0, 1) for xl in (0, 1) for z in range(N)] + [
     [device(y, xh, xl, hidden_z(y, xh, a), 1) for a in range(N)] for y in range(N) for xh in (0, 1) for xl in (0, 1)
 ]
@@ -66,8 +72,7 @@
     for here, there in [(device(y, xh, xl, z, 1), device(a, xl, *column_of(y, xh), 0))]
     for move in ((here, there), (there, here))
 ]
-BACK_OWN = [(device(y, xh, xl, z, core), device(y, xl, xh, z, core)) for y, xh, xl, z in CHIPS for core in (0, 1)]
-BACK_OTHER = [(device(y, xh, xl, z, core), device(y, xl, xh, z, 1 - core)) for y, xh, xl, z in CHIPS for core in (0, 1)]
+BACK = [(device(y, xh, xl, z, core), device(y, xl, xh, z, core)) for y, xh, xl, z in CHIPS for core in (0, 1)]
 
 
 def trade(blocks, groups):
@@ -82,14 +87,24 @@
     return jnp.sum(trade(partial.astype(jnp.bfloat16), groups).astype(jnp.float32), axis=0)
 
 
-def fold(wide):
-    half = wide.shape[1] // 2
-    return jnp.concatenate([wide[:, :half], wide[:, half:]], axis=0)
+def fold(tall):
+    half = tall.shape[0] // 2
+    return jnp.concatenate([tall[:half], tall[half:]], axis=1)
 
 
-def unfold(tall):
-    half = tall.shape[0] // 2
-    return jnp.concatenate([tall[:half], tall[half:]], axis=1)
+def unfold(block):
+    half = block.shape[1] // 2
+    return jnp.concatenate([block[:, :half], block[:, half:]], axis=0)
+
+
+def wide_fold(wide):
+    half = wide.shape[2] // 2
+    return jnp.concatenate([wide[:, :, :half], wide[:, :, half:]], axis=1)
+
+
+def wide_unfold(block):
+    half = block.shape[0] // 2
+    return jnp.concatenate([block[:half], block[half:]], axis=1)
 
 
 def local(tokens, mixer_out, gate_weight, out_weight, out_grad):
@@ -98,10 +113,10 @@
     inner, width = gate_weight.shape[1], out_grad.shape[1]
     own = lax.ppermute(jnp.where(first, tokens, out_grad), ALL, SPREAD_OWN)
     other = lax.ppermute(jnp.where(first, out_grad, tokens), ALL, SPREAD_OTHER)
-    out_t = out_weight.T
-    mine = jnp.where(first, gate_weight, fold(out_t))
-    yours = jnp.where(first, fold(out_t), gate_weight)
-    own, other, swapped = lax.optimization_barrier((own, other, lax.ppermute(yours, ALL, SWAP)))
+    mine = jnp.where(first, gate_weight, fold(out_weight))
+    yours = jnp.where(first, fold(out_weight), gate_weight)
+    swapped = lax.ppermute(yours, ALL, SWAP)
+    own, other, mine, swapped = lax.optimization_barrier((own, other, mine, swapped))
     acts = gather(jnp.concatenate([own, other], axis=1), WIDE)
     mixer_in = lax.ppermute(mixer_out, ALL, SWAP)
     acts, mixer_in = lax.optimization_barrier((acts, mixer_in))
@@ -109,7 +124,7 @@
     weight = jnp.where(
         first,
         jnp.concatenate([mine, swapped], axis=1),
-        jnp.concatenate([unfold(mine), unfold(swapped)], axis=0),
+        jnp.concatenate([unfold(mine), unfold(swapped)], axis=1).T,
     )
     weight = jnp.stack([weight, lax.ppermute(weight, ALL, PARTNER)])
     mixer_vals = jnp.concatenate([mixer_out, mixer_in], axis=1).astype(f32)
@@ -130,24 +145,33 @@
     units, mixer_grad_in = lax.optimization_barrier((units, mixer_grad_in))
     units = units.reshape(-1, units.shape[2])
 
-    parts = [lax.dot_general(units, w, (((1,), (1,)), ((), ())), preferred_element_type=f32).astype(bf16) for w in weight]
-    layer_part, units = lax.optimization_barrier((jnp.stack(parts), units))
-    layer_pair = reduce(layer_part.reshape(2 * N, -1, layer_part.shape[2]), WIDE).astype(bf16)
+    def layer_part(start):
+        return jnp.stack(
+            [
+                lax.dot_general(
+                    units, w[start : start + width], (((1,), (1,)), ((), ())), preferred_element_type=f32
+                ).astype(bf16)
+                for w in weight
+            ]
+        )
+
+    layer_in = lax.ppermute(layer_part(width), ALL, SWAP)
+    layer_blocks = jnp.where(first, layer_in, layer_part(0))
+    layer_own = reduce(layer_blocks.reshape(2 * N, -1, width), ROW_GROUPS).astype(bf16)
 
     grads = jnp.einsum("kad,an->kdn", acts, units, preferred_element_type=f32)
-    keep = jnp.where(first, grads[:, :, :inner], jnp.stack([fold(g) for g in grads[:, :width]]))
-    send = jnp.where(first, grads[:, :, inner:], jnp.stack([fold(g) for g in grads[:, width:]]))
+    keep = jnp.where(first, grads[:, :, :inner], wide_fold(grads[:, :width]))
+    send = jnp.where(first, grads[:, :, inner:], wide_fold(grads[:, width:]))
     swap_in = lax.ppermute(send[0], ALL, SWAP)
     keep_far, send_far = keep[1].astype(bf16), send[1].astype(bf16)
-    layer_own = lax.ppermute(layer_pair[:, :width], ALL, BACK_OWN)
-    layer_other = lax.ppermute(layer_pair[:, width:], ALL, BACK_OTHER)
+    layer_out = lax.ppermute(layer_own, ALL, BACK)
     kept = (keep[0] + lax.ppermute(keep_far, ALL, PARTNER).astype(f32)).astype(bf16)
     sent = (swap_in + lax.ppermute(send_far, ALL, SWAP_PARTNER).astype(f32)).astype(bf16)
     return (
-        jnp.where(first, layer_other, layer_own),
+        layer_out,
         jnp.where(first, mixer_grad[:, :inner], mixer_grad_in),
         jnp.where(first, kept, sent),
-        unfold(jnp.where(first, sent, kept)).T,
+        wide_unfold(jnp.where(first, sent, kept)).T,
     )
 
 

time: 153 us -> 151 us (0.987)
  the two profiles are of different devices: /device:TPU:2 before, /device:TPU:10 now
where the time goes in v6:
time: 151 us; the launch traced here: 150 us
  starting transfers between devices  65.5 us (43%)
  waiting for transfers between devices  47.7 us (32%)
  blocking collectives  23.8 us (16%)
  local copies, waits for them, and re-layouts  5.98 us (4%)
  matrix products  3.17 us (2%)
  other arithmetic  3.08 us (2%)
    all_to_all x3, starting transfers between devices, trade(): lax.all_to_all(blocks, ALL, split_axis=0, concat_axis=0, axis_index_group...  28.1 us
    all_to_all x1, blocking collectives, trade(): lax.all_to_all(blocks, ALL, split_axis=0, concat_axis=0, axis_index_group...  23.8 us
    all_to_all x3, waiting for transfers between devices, trade(): lax.all_to_all(blocks, ALL, split_axis=0, concat_axis=0, axis_index_group...  20.4 us
    ppermute x1, waiting for transfers between devices, local(): lax.ppermute(jnp.where(first, gated, total.astype(bf16)), ALL, CROSS)  11.2 us
    ppermute x1, starting transfers between devices, local(): own = lax.ppermute(jnp.where(first, tokens, out_grad), ALL, SPREAD_OWN)  7.4 us
    ppermute x1, starting transfers between devices, local(): mixer_grad_in = lax.ppermute(mixer_grad[:, inner:], ALL, SWAP)  5.26 us
    ppermute x1, starting transfers between devices, local(): lax.ppermute(keep_far, ALL, PARTNER).astype(f32)  4.88 us
    ppermute x1, waiting for transfers between devices, local(): lax.ppermute(keep_far, ALL, PARTNER).astype(f32)  3.95 us
  transfers between devices with their start and end apart: 15, of which 12 were waited for; matrix products, arithmetic and copies ran while one was open for 3% of the time, Pallas kernels for 0%

profile of v6, /device:TPU:10, one launch (start us, length us, event | category | flops | bytes accessed | tf_op | source)
XLA Modules:
  0.0 150.2 jit_solution(1924963958872331877)
XLA Ops:
  0.6 0.0 copy-start.1
  0.6 0.0 copy-start.2
  0.7 1.0 copy.24
  1.7 0.9 fusion.28
  2.6 0.1 copy.40
  2.7 0.1 copy.41
  2.8 1.9 %collective-permute-start.2 = (bf16[256,256]{0,1:T(8,128)(2,1)S(1)}, bf16[256,256]{0,1:T(8,128)(2,1)S(1)}, u32[]{:S(2)}, u32[]{:S(2)}) collective-permute-start(bf16[256,256]{0,1:T(8,128)(2,1)S(1)} %get-tuple-element.36), channel_id=1, source_target_pairs={{0,1},{1,0},{2,3},{3,2},{4,5},{5,4},{6,7},{7,6},{8,9},{9,8},{10,11... | collective-permute-start | bytes 393224 | tf_op jit(solution)/shard_map/ppermute | solution.py:118
  4.8 0.0 copy-done.1
  4.8 0.0 copy-done.2
  4.8 3.5 %collective-permute-start.1 = (bf16[128,128]{1,0:T(8,128)(2,1)S(1)}, bf16[128,128]{1,0:T(8,128)(2,1)S(1)}, u32[]{:S(2)}, u32[]{:S(2)}) collective-permute-start(bf16[128,128]{1,0:T(8,128)(2,1)S(1)} %get-tuple-element.46), channel_id=1, source_target_pairs={{1,8},{0,1},{3,26},{2,3},{5,74},{4,5},{7,92},{6,7},{9,140},{8,9},{... | collective-permute-start | bytes 98312 | tf_op jit(solution)/shard_map/ppermute | solution.py:115
  8.3 7.4 %collective-permute-start = (bf16[128,128]{1,0:T(8,128)(2,1)S(1)}, bf16[128,128]{1,0:T(8,128)(2,1)S(1)}, u32[]{:S(2)}, u32[]{:S(2)}) collective-permute-start(bf16[128,128]{1,0:T(8,128)(2,1)S(1)} %get-tuple-element.47), channel_id=1, source_target_pairs={{0,8},{1,1},{2,26},{3,3},{4,74},{5,5},{6,92},{7,7},{8,140},{9,9},{... | collective-permute-start | bytes 98312 | tf_op jit(solution)/shard_map/ppermute | solution.py:114
  15.7 0.0 collective-permute-done.1
  15.7 2.2 %collective-permute-done = bf16[128,128]{1,0:T(8,128)(2,1)S(1)} collective-permute-done((bf16[128,128]{1,0:T(8,128)(2,1)S(1)}, bf16[128,128]{1,0:T(8,128)(2,1)S(1)}, u32[]{:S(2)}, u32[]{:S(2)}) %collective-permute-start) | collective-permute-done | bytes 32800 | tf_op jit(solution)/shard_map/ppermute | solution.py:114
  18.0 0.0 collective-permute-done.2
  18.0 1.1 broadcast_in_dim.6
  19.1 14.5 %all-to-all-start = ((bf16[16,128,256]{2,1,0:T(8,128)(2,1)}), bf16[16,128,256]{2,1,0:T(8,128)(2,1)S(1)}, u32[]{:S(2)}, u32[]{:S(2)}) async-start(bf16[16,128,256]{2,1,0:T(8,128)(2,1)} %broadcast_in_dim.6), calls=%async_computation | async-start | bytes 2097152 | tf_op jit(solution)/shard_map/all_to_all | solution.py:79
  33.7 0.0 copy-start
  33.7 0.1 copy.26
  33.9 0.1 fusion.13
  33.9 2.0 %collective-permute-start.4 = (bf16[256,512]{1,0:T(8,128)(2,1)S(1)}, bf16[256,512]{1,0:T(8,128)(2,1)S(1)}, u32[]{:S(2)}, u32[]{:S(2)}) collective-permute-start(bf16[256,512]{1,0:T(8,128)(2,1)S(1)} %fusion.13), channel_id=1, source_target_pairs={{0,32},{2,34},{4,36},{6,38},{8,40},{10,42},{12,44},{14,46},{16,48}... | collective-permute-start | bytes 786440 | tf_op jit(solution)/shard_map/ppermute | solution.py:129
  36.0 1.9 %collective-permute-start.3 = (bf16[128,256]{1,0:T(8,128)(2,1)S(1)}, bf16[128,256]{1,0:T(8,128)(2,1)S(1)}, u32[]{:S(2)}, u32[]{:S(2)}) collective-permute-start(bf16[128,256]{1,0:T(8,128)(2,1)S(1)} %copy-done), channel_id=1, source_target_pairs={{0,1},{1,0},{2,3},{3,2},{4,5},{5,4},{6,7},{7,6},{8,9},{9,8},{10,11... | collective-permute-start | bytes 196616 | tf_op jit(solution)/shard_map/ppermute | solution.py:121
  37.9 1.2 collective-permute-done.3
  39.1 9.0 %all-to-all-done = bf16[16,128,256]{2,1,0:T(8,128)(2,1)S(1)} async-done(((bf16[16,128,256]{2,1,0:T(8,128)(2,1)}), bf16[16,128,256]{2,1,0:T(8,128)(2,1)S(1)}, u32[]{:S(2)}, u32[]{:S(2)}) %all-to-all-start) | async-done | bytes 1048608 | tf_op jit(solution)/shard_map/all_to_all | solution.py:79
  48.1 3.5 %collective-permute-done.4 = bf16[256,512]{1,0:T(8,128)(2,1)S(1)} collective-permute-done((bf16[256,512]{1,0:T(8,128)(2,1)S(1)}, bf16[256,512]{1,0:T(8,128)(2,1)S(1)}, u32[]{:S(2)}, u32[]{:S(2)}) %collective-permute-start.4) | collective-permute-done | bytes 262176 | tf_op jit(solution)/shard_map/ppermute | solution.py:129
  51.7 0.7 bitcast_convert_fusion
  52.4 23.8 %all_to_all.20 = bf16[8,128,512]{2,1,0:T(8,128)(2,1)S(1)} all-to-all(bf16[8,128,512]{2,1,0:T(8,128)(2,1)S(1)} %bitcast_convert_fusion), channel_id=1, replica_groups={{0,64,128,192,256,320,384,448},{2,66,130,194,258,322,386,450},{4,68,132..., dimensions={0} | all-to-all | bytes 2097152 | tf_op jit(solution)/shard_map/all_to_all | solution.py:79
  76.2 0.1 convert_reduce_fusion
  76.3 0.1 fusion.18
  76.4 1.9 %collective-permute-start.5 = (bf16[128,512]{1,0:T(8,128)(2,1)S(1)}, bf16[128,512]{1,0:T(8,128)(2,1)S(1)}, u32[]{:S(2)}, u32[]{:S(2)}) collective-permute-start(bf16[128,512]{1,0:T(8,128)(2,1)S(1)} %fusion.18), channel_id=1, source_target_pairs={{1,256},{256,1},{3,320},{320,3},{5,384},{384,5},{7,448},{448,7},{9... | collective-permute-start | bytes 393224 | tf_op jit(solution)/shard_map/ppermute | solution.py:139
  78.3 11.2 %collective-permute-done.5 = bf16[128,512]{1,0:T(8,128)(2,1)S(1)} collective-permute-done((bf16[128,512]{1,0:T(8,128)(2,1)S(1)}, bf16[128,512]{1,0:T(8,128)(2,1)S(1)}, u32[]{:S(2)}, u32[]{:S(2)}) %collective-permute-start.5) | collective-permute-done | bytes 131104 | tf_op jit(solution)/shard_map/ppermute | solution.py:139
  89.6 0.1 fusion.15
  89.7 1.1 broadcast_in_dim.7
  90.8 3.8 %all-to-all-start.2 = ((bf16[8,128,512]{2,1,0:T(8,128)(2,1)}), bf16[8,128,512]{2,1,0:T(8,128)(2,1)S(1)}, u32[]{:S(2)}, u32[]{:S(2)}) async-start(bf16[8,128,512]{2,1,0:T(8,128)(2,1)} %broadcast_in_dim.7), calls=%async_computation.2 | async-start | bytes 2097152 | tf_op jit(solution)/shard_map/all_to_all | solution.py:79
  94.6 0.1 fusion.10
  94.7 5.3 %collective-permute-start.6 = (bf16[128,256]{1,0:T(8,128)(2,1)S(1)}, bf16[128,256]{1,0:T(8,128)(2,1)S(1)}, u32[]{:S(2)}, u32[]{:S(2)}) collective-permute-start(bf16[128,256]{1,0:T(8,128)(2,1)S(1)} %slice.106), channel_id=1, source_target_pairs={{0,1},{1,0},{2,3},{3,2},{4,5},{5,4},{6,7},{7,6},{8,9},{9,8},{10,11... | collective-permute-start | bytes 196616 | tf_op jit(solution)/shard_map/ppermute | solution.py:144
  100.0 0.9 collective-permute-done.6
  100.8 11.2 %all-to-all-done.2 = bf16[8,128,512]{2,1,0:T(8,128)(2,1)S(1)} async-done(((bf16[8,128,512]{2,1,0:T(8,128)(2,1)}), bf16[8,128,512]{2,1,0:T(8,128)(2,1)S(1)}, u32[]{:S(2)}, u32[]{:S(2)}) %all-to-all-start.2) | async-done | bytes 1048608 | tf_op jit(solution)/shard_map/all_to_all | solution.py:79
  112.0 0.4 fusion.2
  112.5 0.4 fusion
  112.9 0.4 fusion.1
  113.3 0.1 pad_maximum_fusion
  113.4 1.9 %collective-permute-start.7 = (bf16[2,1024,128]{2,1,0:T(8,128)(2,1)S(1)}, bf16[2,1024,128]{2,1,0:T(8,128)(2,1)S(1)}, u32[]{:S(2)}, u32[]{:S(2)}) collective-permute-start(bf16[2,1024,128]{2,1,0:T(8,128)(2,1)S(1)} %pad_maximum_fusion), channel_id=1, source_target_pairs={{0,1},{1,0},{2,3},{3,2},{4,5},{5,4},{6,7},{7,6},{8,9},{9,8},{10,11... | collective-permute-start | bytes 1572872 | tf_op jit(solution)/shard_map/ppermute | solution.py:158
  115.3 0.8 fusion.29
  116.1 0.1 fusion.24
  116.2 0.4 fusion.3
  116.6 0.1 slice_select_fusion.1
  116.8 0.4 collective-permute-done.7
  117.2 0.9 maximum_select_fusion
  118.1 9.8 %all-to-all-start.3 = ((bf16[16,128,128]{2,1,0:T(8,128)(2,1)}), bf16[16,128,128]{2,1,0:T(8,128)(2,1)S(1)}, u32[]{:S(2)}, u32[]{:S(2)}) async-start(bf16[16,128,128]{2,1,0:T(8,128)(2,1)} %bitcast.14), calls=%async_computation.3 | async-start | bytes 1048576 | tf_op jit(solution)/shard_map/all_to_all | solution.py:79
  127.9 1.9 %collective-permute-start.10 = (f32[256,256]{0,1:T(8,128)S(1)}, f32[256,256]{0,1:T(8,128)S(1)}, u32[]{:S(2)}, u32[]{:S(2)}) collective-permute-start(f32[256,256]{0,1:T(8,128)S(1)} %slice_bitcast_fusion), channel_id=1, source_target_pairs={{0,1},{1,0},{2,3},{3,2},{4,5},{5,4},{6,7},{7,6},{8,9},{9,8},{10,11... | collective-permute-start | bytes 786440 | tf_op jit(solution)/shard_map/ppermute | solution.py:165
  129.8 2.6 %collective-permute-start.11 = (bf16[256,256]{0,1:T(8,128)(2,1)S(1)}, bf16[256,256]{0,1:T(8,128)(2,1)S(1)}, u32[]{:S(2)}, u32[]{:S(2)}) collective-permute-start(bf16[256,256]{0,1:T(8,128)(2,1)S(1)} %fusion.17), channel_id=1, source_target_pairs={{32,1},{34,3},{36,5},{38,7},{40,9},{42,11},{44,13},{46,15},{48,17}... | collective-permute-start | bytes 393224 | tf_op jit(solution)/shard_map/ppermute | solution.py:169
  132.4 4.9 %collective-permute-start.9 = (bf16[256,256]{0,1:T(8,128)(2,1)S(1)}, bf16[256,256]{0,1:T(8,128)(2,1)S(1)}, u32[]{:S(2)}, u32[]{:S(2)}) collective-permute-start(bf16[256,256]{0,1:T(8,128)(2,1)S(1)} %fusion.16), channel_id=1, source_target_pairs={{0,32},{2,34},{4,36},{6,38},{8,40},{10,42},{12,44},{14,46},{16,48}... | collective-permute-start | bytes 393224 | tf_op jit(solution)/shard_map/ppermute | solution.py:168
  137.3 0.6 slice_select_fusion.2
  137.9 1.5 collective-permute-done.11
  139.4 4.0 %collective-permute-done.9 = bf16[256,256]{0,1:T(8,128)(2,1)S(1)} collective-permute-done((bf16[256,256]{0,1:T(8,128)(2,1)S(1)}, bf16[256,256]{0,1:T(8,128)(2,1)S(1)}, u32[]{:S(2)}, u32[]{:S(2)}) %collective-permute-start.9) | collective-permute-done | bytes 131104 | tf_op jit(solution)/shard_map/ppermute | solution.py:168
  143.4 0.0 collective-permute-done.10
  143.4 0.1 broadcast_select_fusion
  143.5 0.3 all-to-all-done.3
  143.7 0.1 reduce_sum.22
  143.8 2.1 %collective-permute-start.8 = (bf16[128,128]{1,0:T(8,128)(2,1)S(1)}, bf16[128,128]{1,0:T(8,128)(2,1)S(1)}, u32[]{:S(2)}, u32[]{:S(2)}) collective-permute-start(bf16[128,128]{1,0:T(8,128)(2,1)S(1)} %reduce_sum.22), channel_id=1, source_target_pairs={{0,0},{1,1},{2,2},{3,3},{4,4},{5,5},{6,6},{7,7},{8,8},{9,9},{10,10... | collective-permute-start | bytes 98312 | tf_op jit(solution)/shard_map/ppermute | solution.py:167
  146.0 0.7 maximum_bitcast_fusion.3
  146.6 0.8 copy.35
  147.4 2.2 %collective-permute-done.8 = bf16[128,128]{1,0:T(8,128)(2,1)S(1)} collective-permute-done((bf16[128,128]{1,0:T(8,128)(2,1)S(1)}, bf16[128,128]{1,0:T(8,128)(2,1)S(1)}, u32[]{:S(2)}, u32[]{:S(2)}) %collective-permute-start.8) | collective-permute-done | bytes 32800 | tf_op jit(solution)/shard_map/ppermute | solution.py:167
  149.6 0.6 copy.43
  (11 shorter events, 0.2 us)
Async XLA Ops:
  0.6 4.1 %copy-start.1 = (bf16[128,128]{1,0:T(8,128)(2,1)S(1)}, bf16[128,128]{1,0:T(8,128)(2,1)}, u32[]{:S(2)}) copy-start(bf16[128,128]{1,0:T(8,128)(2,1)} %param.9) | copy-start | bytes 98308
  0.6 4.1 %copy-start.2 = (bf16[128,128]{1,0:T(8,128)(2,1)S(1)}, bf16[128,128]{1,0:T(8,128)(2,1)}, u32[]{:S(2)}) copy-start(bf16[128,128]{1,0:T(8,128)(2,1)} %param.5) | copy-start | bytes 98308
  2.8 15.2 %collective-permute-start.2 = (bf16[256,256]{0,1:T(8,128)(2,1)S(1)}, bf16[256,256]{0,1:T(8,128)(2,1)S(1)}, u32[]{:S(2)}, u32[]{:S(2)}) collective-permute-start(bf16[256,256]{0,1:T(8,128)(2,1)S(1)} %get-tuple-element.36), channel_id=1, source_target_pairs={{0,1},{1,0},{2,3},{3,2},{4,5},{5,4},{6,7},{7,6},{8,9},{9,8},{10,11... | collective-permute-start | bytes 393224 | tf_op jit(solution)/shard_map/ppermute | solution.py:118
  4.8 10.9 %collective-permute-start.1 = (bf16[128,128]{1,0:T(8,128)(2,1)S(1)}, bf16[128,128]{1,0:T(8,128)(2,1)S(1)}, u32[]{:S(2)}, u32[]{:S(2)}) collective-permute-start(bf16[128,128]{1,0:T(8,128)(2,1)S(1)} %get-tuple-element.46), channel_id=1, source_target_pairs={{1,8},{0,1},{3,26},{2,3},{5,74},{4,5},{7,92},{6,7},{9,140},{8,9},{... | collective-permute-start | bytes 98312 | tf_op jit(solution)/shard_map/ppermute | solution.py:115
  8.3 9.7 %collective-permute-start = (bf16[128,128]{1,0:T(8,128)(2,1)S(1)}, bf16[128,128]{1,0:T(8,128)(2,1)S(1)}, u32[]{:S(2)}, u32[]{:S(2)}) collective-permute-start(bf16[128,128]{1,0:T(8,128)(2,1)S(1)} %get-tuple-element.47), channel_id=1, source_target_pairs={{0,8},{1,1},{2,26},{3,3},{4,74},{5,5},{6,92},{7,7},{8,140},{9,9},{... | collective-permute-start | bytes 98312 | tf_op jit(solution)/shard_map/ppermute | solution.py:114
  19.1 29.0 %all-to-all-start = ((bf16[16,128,256]{2,1,0:T(8,128)(2,1)}), bf16[16,128,256]{2,1,0:T(8,128)(2,1)S(1)}, u32[]{:S(2)}, u32[]{:S(2)}) async-start(bf16[16,128,256]{2,1,0:T(8,128)(2,1)} %broadcast_in_dim.6), calls=%async_computation | async-start | bytes 2097152 | tf_op jit(solution)/shard_map/all_to_all | solution.py:79
  33.7 2.3 %copy-start = (bf16[128,256]{1,0:T(8,128)(2,1)S(1)}, bf16[128,256]{1,0:T(8,128)(2,1)}, u32[]{:S(2)}) copy-start(bf16[128,256]{1,0:T(8,128)(2,1)} %param.6) | copy-start | bytes 196612
  33.9 17.7 %collective-permute-start.4 = (bf16[256,512]{1,0:T(8,128)(2,1)S(1)}, bf16[256,512]{1,0:T(8,128)(2,1)S(1)}, u32[]{:S(2)}, u32[]{:S(2)}) collective-permute-start(bf16[256,512]{1,0:T(8,128)(2,1)S(1)} %fusion.13), channel_id=1, source_target_pairs={{0,32},{2,34},{4,36},{6,38},{8,40},{10,42},{12,44},{14,46},{16,48}... | collective-permute-start | bytes 786440 | tf_op jit(solution)/shard_map/ppermute | solution.py:129
  36.0 3.1 %collective-permute-start.3 = (bf16[128,256]{1,0:T(8,128)(2,1)S(1)}, bf16[128,256]{1,0:T(8,128)(2,1)S(1)}, u32[]{:S(2)}, u32[]{:S(2)}) collective-permute-start(bf16[128,256]{1,0:T(8,128)(2,1)S(1)} %copy-done), channel_id=1, source_target_pairs={{0,1},{1,0},{2,3},{3,2},{4,5},{5,4},{6,7},{7,6},{8,9},{9,8},{10,11... | collective-permute-start | bytes 196616 | tf_op jit(solution)/shard_map/ppermute | solution.py:121
  76.4 13.2 %collective-permute-start.5 = (bf16[128,512]{1,0:T(8,128)(2,1)S(1)}, bf16[128,512]{1,0:T(8,128)(2,1)S(1)}, u32[]{:S(2)}, u32[]{:S(2)}) collective-permute-start(bf16[128,512]{1,0:T(8,128)(2,1)S(1)} %fusion.18), channel_id=1, source_target_pairs={{1,256},{256,1},{3,320},{320,3},{5,384},{384,5},{7,448},{448,7},{9... | collective-permute-start | bytes 393224 | tf_op jit(solution)/shard_map/ppermute | solution.py:139
  90.8 21.3 %all-to-all-start.2 = ((bf16[8,128,512]{2,1,0:T(8,128)(2,1)}), bf16[8,128,512]{2,1,0:T(8,128)(2,1)S(1)}, u32[]{:S(2)}, u32[]{:S(2)}) async-start(bf16[8,128,512]{2,1,0:T(8,128)(2,1)} %broadcast_in_dim.7), calls=%async_computation.2 | async-start | bytes 2097152 | tf_op jit(solution)/shard_map/all_to_all | solution.py:79
  94.7 6.2 %collective-permute-start.6 = (bf16[128,256]{1,0:T(8,128)(2,1)S(1)}, bf16[128,256]{1,0:T(8,128)(2,1)S(1)}, u32[]{:S(2)}, u32[]{:S(2)}) collective-permute-start(bf16[128,256]{1,0:T(8,128)(2,1)S(1)} %slice.106), channel_id=1, source_target_pairs={{0,1},{1,0},{2,3},{3,2},{4,5},{5,4},{6,7},{7,6},{8,9},{9,8},{10,11... | collective-permute-start | bytes 196616 | tf_op jit(solution)/shard_map/ppermute | solution.py:144
  113.4 3.8 %collective-permute-start.7 = (bf16[2,1024,128]{2,1,0:T(8,128)(2,1)S(1)}, bf16[2,1024,128]{2,1,0:T(8,128)(2,1)S(1)}, u32[]{:S(2)}, u32[]{:S(2)}) collective-permute-start(bf16[2,1024,128]{2,1,0:T(8,128)(2,1)S(1)} %pad_maximum_fusion), channel_id=1, source_target_pairs={{0,1},{1,0},{2,3},{3,2},{4,5},{5,4},{6,7},{7,6},{8,9},{9,8},{10,11... | collective-permute-start | bytes 1572872 | tf_op jit(solution)/shard_map/ppermute | solution.py:158
  118.1 25.6 %all-to-all-start.3 = ((bf16[16,128,128]{2,1,0:T(8,128)(2,1)}), bf16[16,128,128]{2,1,0:T(8,128)(2,1)S(1)}, u32[]{:S(2)}, u32[]{:S(2)}) async-start(bf16[16,128,128]{2,1,0:T(8,128)(2,1)} %bitcast.14), calls=%async_computation.3 | async-start | bytes 1048576 | tf_op jit(solution)/shard_map/all_to_all | solution.py:79
  127.9 15.5 %collective-permute-start.10 = (f32[256,256]{0,1:T(8,128)S(1)}, f32[256,256]{0,1:T(8,128)S(1)}, u32[]{:S(2)}, u32[]{:S(2)}) collective-permute-start(f32[256,256]{0,1:T(8,128)S(1)} %slice_bitcast_fusion), channel_id=1, source_target_pairs={{0,1},{1,0},{2,3},{3,2},{4,5},{5,4},{6,7},{7,6},{8,9},{9,8},{10,11... | collective-permute-start | bytes 786440 | tf_op jit(solution)/shard_map/ppermute | solution.py:165
  129.8 9.6 %collective-permute-start.11 = (bf16[256,256]{0,1:T(8,128)(2,1)S(1)}, bf16[256,256]{0,1:T(8,128)(2,1)S(1)}, u32[]{:S(2)}, u32[]{:S(2)}) collective-permute-start(bf16[256,256]{0,1:T(8,128)(2,1)S(1)} %fusion.17), channel_id=1, source_target_pairs={{32,1},{34,3},{36,5},{38,7},{40,9},{42,11},{44,13},{46,15},{48,17}... | collective-permute-start | bytes 393224 | tf_op jit(solution)/shard_map/ppermute | solution.py:169
  132.4 11.0 %collective-permute-start.9 = (bf16[256,256]{0,1:T(8,128)(2,1)S(1)}, bf16[256,256]{0,1:T(8,128)(2,1)S(1)}, u32[]{:S(2)}, u32[]{:S(2)}) collective-permute-start(bf16[256,256]{0,1:T(8,128)(2,1)S(1)} %fusion.16), channel_id=1, source_target_pairs={{0,32},{2,34},{4,36},{6,38},{8,40},{10,42},{12,44},{14,46},{16,48}... | collective-permute-start | bytes 393224 | tf_op jit(solution)/shard_map/ppermute | solution.py:168
  143.8 5.8 %collective-permute-start.8 = (bf16[128,128]{1,0:T(8,128)(2,1)S(1)}, bf16[128,128]{1,0:T(8,128)(2,1)S(1)}, u32[]{:S(2)}, u32[]{:S(2)}) collective-permute-start(bf16[128,128]{1,0:T(8,128)(2,1)S(1)} %reduce_sum.22), channel_id=1, source_target_pairs={{0,0},{1,1},{2,2},{3,3},{4,4},{5,5},{6,6},{7,7},{8,8},{9,9},{10,10... | collective-permute-start | bytes 98312 | tf_op jit(solution)/shard_map/ppermute | solution.py:167

commit v7 on v6

--- a/solution.py
+++ b/solution.py
@@ -1,10 +1,12 @@
 import jax
 import jax.numpy as jnp
 from jax import lax
+from jax.experimental.layout import Layout, with_layout_constraint
 from jax.sharding import Mesh, PartitionSpec as P
 
 ROWS, COLS = ("y", "xh"), ("xl", "z", "c")
 ALL = ROWS + COLS
+BY_ROWS = Layout(major_to_minor=(0, 1))
 N = 8
 
 
@@ -64,7 +66,7 @@
     return moves
 
 
-SPREAD_OWN, SPREAD_OTHER = spread(0), spread(1)
+SPREAD = spread(0)
 CROSS = [
     move
     for y, xh, xl, z in CHIPS
@@ -87,14 +89,14 @@
     return jnp.sum(trade(partial.astype(jnp.bfloat16), groups).astype(jnp.float32), axis=0)
 
 
-def fold(tall):
+def fold(block):
+    half = block.shape[1] // 2
+    return jnp.concatenate([block[:, :half], block[:, half:]], axis=0)
+
+
+def unfold(tall):
     half = tall.shape[0] // 2
     return jnp.concatenate([tall[:half], tall[half:]], axis=1)
-
-
-def unfold(block):
-    half = block.shape[1] // 2
-    return jnp.concatenate([block[:, :half], block[:, half:]], axis=0)
 
 
 def wide_fold(wide):
@@ -111,21 +113,22 @@
     f32, bf16 = jnp.float32, jnp.bfloat16
     first = lax.axis_index("c") == 0
     inner, width = gate_weight.shape[1], out_grad.shape[1]
-    own = lax.ppermute(jnp.where(first, tokens, out_grad), ALL, SPREAD_OWN)
-    other = lax.ppermute(jnp.where(first, out_grad, tokens), ALL, SPREAD_OTHER)
-    mine = jnp.where(first, gate_weight, fold(out_weight))
-    yours = jnp.where(first, fold(out_weight), gate_weight)
-    swapped = lax.ppermute(yours, ALL, SWAP)
-    own, other, mine, swapped = lax.optimization_barrier((own, other, mine, swapped))
-    acts = gather(jnp.concatenate([own, other], axis=1), WIDE)
+    mine = jnp.where(first, tokens, out_grad)
+    yours = jnp.where(first, out_grad, tokens)
+    block = jnp.where(first, out_weight, fold(gate_weight))
+    sent = with_layout_constraint(jnp.concatenate([yours, block], axis=0), BY_ROWS)
+    swapped = with_layout_constraint(lax.ppermute(sent, ALL, SWAP), BY_ROWS)
+    pair = lax.ppermute(jnp.concatenate([mine, swapped[: mine.shape[0]]], axis=1), ALL, SPREAD)
+    block = swapped[mine.shape[0] :]
+    weight = jnp.where(
+        first,
+        jnp.concatenate([gate_weight, unfold(block)], axis=1),
+        jnp.concatenate([out_weight, block], axis=1).T,
+    )
+    acts = gather(pair, WIDE)
     mixer_in = lax.ppermute(mixer_out, ALL, SWAP)
     acts, mixer_in = lax.optimization_barrier((acts, mixer_in))
     acts = acts.reshape(2, N * acts.shape[1], acts.shape[2])
-    weight = jnp.where(
-        first,
-        jnp.concatenate([mine, swapped], axis=1),
-        jnp.concatenate([unfold(mine), unfold(swapped)], axis=1).T,
-    )
     weight = jnp.stack([weight, lax.ppermute(weight, ALL, PARTNER)])
     mixer_vals = jnp.concatenate([mixer_out, mixer_in], axis=1).astype(f32)
 

time: 151 us -> 151 us (level)
  the two profiles are of different devices: /device:TPU:10 before, /device:TPU:2 now
where the time goes in v7:
time: 151 us; the launch traced here: 150 us
  starting transfers between devices  69.1 us (46%)
  waiting for transfers between devices  38.7 us (26%)
  blocking collectives  27.8 us (18%)
  local copies, waits for them, and re-layouts  5.44 us (4%)
  other arithmetic  4.78 us (3%)
  matrix products  3.2 us (2%)
    all_to_all x3, starting transfers between devices, trade(): lax.all_to_all(blocks, ALL, split_axis=0, concat_axis=0, axis_index_group...  28.8 us
    all_to_all x1, blocking collectives, trade(): lax.all_to_all(blocks, ALL, split_axis=0, concat_axis=0, axis_index_group...  27.8 us
    all_to_all x3, waiting for transfers between devices, trade(): lax.all_to_all(blocks, ALL, split_axis=0, concat_axis=0, axis_index_group...  15.8 us
    ppermute x1, waiting for transfers between devices, local(): lax.ppermute(jnp.where(first, gated, total.astype(bf16)), ALL, CROSS)  9.26 us
    ppermute x1, starting transfers between devices, local(): mixer_grad_in = lax.ppermute(mixer_grad[:, inner:], ALL, SWAP)  9.21 us
    ppermute x1, starting transfers between devices, local(): lax.ppermute(jnp.concatenate([mine, swapped[:mine.shape[0]]], axis=1), AL...  7.7 us
    ppermute x1, waiting for transfers between devices, local(): lax.ppermute(keep_far, ALL, PARTNER).astype(f32)  5.37 us
    ppermute x1, starting transfers between devices, local(): lax.ppermute(keep_far, ALL, PARTNER).astype(f32)  5.34 us
  transfers between devices with their start and end apart: 14, of which 11 were waited for; matrix products, arithmetic and copies ran while one was open for 3% of the time, Pallas kernels for 0%

profile of v7, /device:TPU:2, one launch (start us, length us, event | category | flops | bytes accessed | tf_op | source)
XLA Modules:
  0.0 150.0 jit_solution(17793965676772731616)
XLA Ops:
  0.6 0.9 fusion.26
  1.5 0.8 broadcast_select_fusion.3
  2.3 0.9 maximum_select_fusion.2
  3.3 1.9 %collective-permute-start = (bf16[640,128]{1,0:T(8,128)(2,1)S(1)}, bf16[640,128]{1,0:T(8,128)(2,1)S(1)}, u32[]{:S(2)}, u32[]{:S(2)}) collective-permute-start(bf16[640,128]{1,0:T(8,128)(2,1)S(1)} %pad_maximum_fusion.1), channel_id=1, source_target_pairs={{0,1},{1,0},{2,3},{3,2},{4,5},{5,4},{6,7},{7,6},{8,9},{9,8},{10,11... | collective-permute-start | bytes 491528 | tf_op jit(solution)/shard_map/ppermute | solution.py:120
  5.2 1.4 collective-permute-done
  6.6 7.7 %collective-permute-start.1 = (bf16[128,256]{1,0:T(8,128)(2,1)S(1)}, bf16[128,256]{1,0:T(8,128)(2,1)S(1)}, u32[]{:S(2)}, u32[]{:S(2)}) collective-permute-start(bf16[128,256]{1,0:T(8,128)(2,1)S(1)} %pad_maximum_fusion.3), channel_id=1, source_target_pairs={{0,8},{1,1},{2,26},{3,3},{4,74},{5,5},{6,92},{7,7},{8,140},{9,9},{... | collective-permute-start | bytes 196616 | tf_op jit(solution)/shard_map/ppermute | solution.py:121
  14.3 2.0 %collective-permute-done.1 = bf16[128,256]{1,0:T(8,128)(2,1)S(1)} collective-permute-done((bf16[128,256]{1,0:T(8,128)(2,1)S(1)}, bf16[128,256]{1,0:T(8,128)(2,1)S(1)}, u32[]{:S(2)}, u32[]{:S(2)}) %collective-permute-start.1) | collective-permute-done | bytes 65568 | tf_op jit(solution)/shard_map/ppermute | solution.py:121
  16.3 1.1 broadcast_in_dim.6
  17.4 0.0 copy-start
  17.4 16.8 %all-to-all-start = ((bf16[16,128,256]{2,1,0:T(8,128)(2,1)}), bf16[16,128,256]{2,1,0:T(8,128)(2,1)S(1)}, u32[]{:S(2)}, u32[]{:S(2)}) async-start(bf16[16,128,256]{2,1,0:T(8,128)(2,1)} %broadcast_in_dim.6), calls=%async_computation | async-start | bytes 2097152 | tf_op jit(solution)/shard_map/all_to_all | solution.py:81
  34.2 0.0 copy-done
  34.2 0.0 copy-start.1
  34.3 0.0 copy-start.2
  34.3 0.1 copy.17
  34.4 0.1 copy.27
  34.5 0.1 copy.28
  34.6 0.5 copy-done.1
  35.2 0.1 maximum_select_fusion.1
  35.2 2.3 %collective-permute-start.3 = (bf16[256,512]{0,1:T(8,128)(2,1)S(1)}, bf16[256,512]{0,1:T(8,128)(2,1)S(1)}, u32[]{:S(2)}, u32[]{:S(2)}) collective-permute-start(bf16[256,512]{0,1:T(8,128)(2,1)S(1)} %maximum_select_fusion.1), channel_id=1, source_target_pairs={{0,32},{2,34},{4,36},{6,38},{8,40},{10,42},{12,44},{14,46},{16,48}... | collective-permute-start | bytes 786440 | tf_op jit(solution)/shard_map/ppermute | solution.py:132
  37.6 0.0 copy-done.2
  37.6 1.9 %collective-permute-start.2 = (bf16[128,256]{1,0:T(8,128)(2,1)S(1)}, bf16[128,256]{1,0:T(8,128)(2,1)S(1)}, u32[]{:S(2)}, u32[]{:S(2)}) collective-permute-start(bf16[128,256]{1,0:T(8,128)(2,1)S(1)} %copy-done.2), channel_id=1, source_target_pairs={{0,1},{1,0},{2,3},{3,2},{4,5},{5,4},{6,7},{7,6},{8,9},{9,8},{10,11... | collective-permute-start | bytes 196616 | tf_op jit(solution)/shard_map/ppermute | solution.py:129
  39.5 1.2 collective-permute-done.2
  40.7 7.1 %all-to-all-done = bf16[16,128,256]{2,1,0:T(8,128)(2,1)S(1)} async-done(((bf16[16,128,256]{2,1,0:T(8,128)(2,1)}), bf16[16,128,256]{2,1,0:T(8,128)(2,1)S(1)}, u32[]{:S(2)}, u32[]{:S(2)}) %all-to-all-start) | async-done | bytes 1048608 | tf_op jit(solution)/shard_map/all_to_all | solution.py:81
  47.8 0.0 collective-permute-done.3
  47.8 0.7 bitcast_convert_fusion
  48.5 27.8 %all_to_all.20 = bf16[8,128,512]{2,1,0:T(8,128)(2,1)S(1)} all-to-all(bf16[8,128,512]{2,1,0:T(8,128)(2,1)S(1)} %bitcast_convert_fusion), channel_id=1, replica_groups={{0,64,128,192,256,320,384,448},{2,66,130,194,258,322,386,450},{4,68,132..., dimensions={0} | all-to-all | bytes 2097152 | tf_op jit(solution)/shard_map/all_to_all | solution.py:81
  76.4 0.1 convert_reduce_fusion
  76.5 0.1 fusion.17
  76.6 1.9 %collective-permute-start.4 = (bf16[128,512]{1,0:T(8,128)(2,1)S(1)}, bf16[128,512]{1,0:T(8,128)(2,1)S(1)}, u32[]{:S(2)}, u32[]{:S(2)}) collective-permute-start(bf16[128,512]{1,0:T(8,128)(2,1)S(1)} %fusion.17), channel_id=1, source_target_pairs={{1,256},{256,1},{3,320},{320,3},{5,384},{384,5},{7,448},{448,7},{9... | collective-permute-start | bytes 393224 | tf_op jit(solution)/shard_map/ppermute | solution.py:142
  78.5 9.3 %collective-permute-done.4 = bf16[128,512]{1,0:T(8,128)(2,1)S(1)} collective-permute-done((bf16[128,512]{1,0:T(8,128)(2,1)S(1)}, bf16[128,512]{1,0:T(8,128)(2,1)S(1)}, u32[]{:S(2)}, u32[]{:S(2)}) %collective-permute-start.4) | collective-permute-done | bytes 131104 | tf_op jit(solution)/shard_map/ppermute | solution.py:142
  87.8 0.1 fusion.14
  87.9 1.1 broadcast_in_dim.7
  89.0 3.8 %all-to-all-start.2 = ((bf16[8,128,512]{2,1,0:T(8,128)(2,1)}), bf16[8,128,512]{2,1,0:T(8,128)(2,1)S(1)}, u32[]{:S(2)}, u32[]{:S(2)}) async-start(bf16[8,128,512]{2,1,0:T(8,128)(2,1)} %broadcast_in_dim.7), calls=%async_computation.2 | async-start | bytes 2097152 | tf_op jit(solution)/shard_map/all_to_all | solution.py:81
  92.8 0.1 fusion.10
  92.9 9.2 %collective-permute-start.5 = (bf16[128,256]{1,0:T(8,128)(2,1)S(1)}, bf16[128,256]{1,0:T(8,128)(2,1)S(1)}, u32[]{:S(2)}, u32[]{:S(2)}) collective-permute-start(bf16[128,256]{1,0:T(8,128)(2,1)S(1)} %slice.110), channel_id=1, source_target_pairs={{0,1},{1,0},{2,3},{3,2},{4,5},{5,4},{6,7},{7,6},{8,9},{9,8},{10,11... | collective-permute-start | bytes 196616 | tf_op jit(solution)/shard_map/ppermute | solution.py:147
  102.1 0.9 collective-permute-done.5
  103.0 8.8 %all-to-all-done.2 = bf16[8,128,512]{2,1,0:T(8,128)(2,1)S(1)} async-done(((bf16[8,128,512]{2,1,0:T(8,128)(2,1)}), bf16[8,128,512]{2,1,0:T(8,128)(2,1)S(1)}, u32[]{:S(2)}, u32[]{:S(2)}) %all-to-all-start.2) | async-done | bytes 1048608 | tf_op jit(solution)/shard_map/all_to_all | solution.py:81
  111.7 0.4 fusion.2
  112.2 0.4 fusion
  112.6 0.4 fusion.1
  113.0 0.1 pad_maximum_fusion
  113.1 2.9 %collective-permute-start.6 = (bf16[2,1024,128]{2,1,0:T(8,128)(2,1)S(1)}, bf16[2,1024,128]{2,1,0:T(8,128)(2,1)S(1)}, u32[]{:S(2)}, u32[]{:S(2)}) collective-permute-start(bf16[2,1024,128]{2,1,0:T(8,128)(2,1)S(1)} %pad_maximum_fusion), channel_id=1, source_target_pairs={{0,1},{1,0},{2,3},{3,2},{4,5},{5,4},{6,7},{7,6},{8,9},{9,8},{10,11... | collective-permute-start | bytes 1572872 | tf_op jit(solution)/shard_map/ppermute | solution.py:161
  116.0 0.7 fusion.27
  116.8 0.1 fusion.23
  116.9 0.4 fusion.3
  117.3 0.1 slice_select_fusion.1
  117.5 0.1 collective-permute-done.6
  117.6 0.9 maximum_select_fusion
  118.4 8.2 %all-to-all-start.3 = ((bf16[16,128,128]{2,1,0:T(8,128)(2,1)}), bf16[16,128,128]{2,1,0:T(8,128)(2,1)S(1)}, u32[]{:S(2)}, u32[]{:S(2)}) async-start(bf16[16,128,128]{2,1,0:T(8,128)(2,1)} %bitcast.13), calls=%async_computation.3 | async-start | bytes 1048576 | tf_op jit(solution)/shard_map/all_to_all | solution.py:81
  126.7 1.9 %collective-permute-start.9 = (f32[256,256]{1,0:T(8,128)S(1)}, f32[256,256]{1,0:T(8,128)S(1)}, u32[]{:S(2)}, u32[]{:S(2)}) collective-permute-start(f32[256,256]{1,0:T(8,128)S(1)} %slice_bitcast_fusion), channel_id=1, source_target_pairs={{0,1},{1,0},{2,3},{3,2},{4,5},{5,4},{6,7},{7,6},{8,9},{9,8},{10,11... | collective-permute-start | bytes 786440 | tf_op jit(solution)/shard_map/ppermute | solution.py:168
  128.6 2.1 %collective-permute-start.10 = (bf16[256,256]{1,0:T(8,128)(2,1)S(1)}, bf16[256,256]{1,0:T(8,128)(2,1)S(1)}, u32[]{:S(2)}, u32[]{:S(2)}) collective-permute-start(bf16[256,256]{1,0:T(8,128)(2,1)S(1)} %fusion.16), channel_id=1, source_target_pairs={{32,1},{34,3},{36,5},{38,7},{40,9},{42,11},{44,13},{46,15},{48,17}... | collective-permute-start | bytes 393224 | tf_op jit(solution)/shard_map/ppermute | solution.py:172
  130.8 5.3 %collective-permute-start.8 = (bf16[256,256]{1,0:T(8,128)(2,1)S(1)}, bf16[256,256]{1,0:T(8,128)(2,1)S(1)}, u32[]{:S(2)}, u32[]{:S(2)}) collective-permute-start(bf16[256,256]{1,0:T(8,128)(2,1)S(1)} %fusion.15), channel_id=1, source_target_pairs={{0,32},{2,34},{4,36},{6,38},{8,40},{10,42},{12,44},{14,46},{16,48}... | collective-permute-start | bytes 393224 | tf_op jit(solution)/shard_map/ppermute | solution.py:171
  136.1 0.6 slice_select_fusion.2
  136.8 0.6 collective-permute-done.10
  137.4 5.4 %collective-permute-done.8 = bf16[256,256]{1,0:T(8,128)(2,1)S(1)} collective-permute-done((bf16[256,256]{1,0:T(8,128)(2,1)S(1)}, bf16[256,256]{1,0:T(8,128)(2,1)S(1)}, u32[]{:S(2)}, u32[]{:S(2)}) %collective-permute-start.8) | collective-permute-done | bytes 131104 | tf_op jit(solution)/shard_map/ppermute | solution.py:171
  142.7 0.0 collective-permute-done.9
  142.7 0.7 broadcast_select_fusion
  143.5 0.0 all-to-all-done.3
  143.5 0.1 reduce_sum.22
  143.6 2.9 %collective-permute-start.7 = (bf16[128,128]{1,0:T(8,128)(2,1)S(1)}, bf16[128,128]{1,0:T(8,128)(2,1)S(1)}, u32[]{:S(2)}, u32[]{:S(2)}) collective-permute-start(bf16[128,128]{1,0:T(8,128)(2,1)S(1)} %reduce_sum.22), channel_id=1, source_target_pairs={{0,0},{1,1},{2,2},{3,3},{4,4},{5,5},{6,6},{7,7},{8,8},{9,9},{10,10... | collective-permute-start | bytes 98312 | tf_op jit(solution)/shard_map/ppermute | solution.py:170
  146.5 0.8 copy.21
  147.3 2.1 %collective-permute-done.7 = bf16[128,128]{1,0:T(8,128)(2,1)S(1)} collective-permute-done((bf16[128,128]{1,0:T(8,128)(2,1)S(1)}, bf16[128,128]{1,0:T(8,128)(2,1)S(1)}, u32[]{:S(2)}, u32[]{:S(2)}) %collective-permute-start.7) | collective-permute-done | bytes 32800 | tf_op jit(solution)/shard_map/ppermute | solution.py:170
  149.4 0.6 copy.30
  (11 shorter events, 0.1 us)
Async XLA Ops:
  3.3 3.3 %collective-permute-start = (bf16[640,128]{1,0:T(8,128)(2,1)S(1)}, bf16[640,128]{1,0:T(8,128)(2,1)S(1)}, u32[]{:S(2)}, u32[]{:S(2)}) collective-permute-start(bf16[640,128]{1,0:T(8,128)(2,1)S(1)} %pad_maximum_fusion.1), channel_id=1, source_target_pairs={{0,1},{1,0},{2,3},{3,2},{4,5},{5,4},{6,7},{7,6},{8,9},{9,8},{10,11... | collective-permute-start | bytes 491528 | tf_op jit(solution)/shard_map/ppermute | solution.py:120
  6.6 9.8 %collective-permute-start.1 = (bf16[128,256]{1,0:T(8,128)(2,1)S(1)}, bf16[128,256]{1,0:T(8,128)(2,1)S(1)}, u32[]{:S(2)}, u32[]{:S(2)}) collective-permute-start(bf16[128,256]{1,0:T(8,128)(2,1)S(1)} %pad_maximum_fusion.3), channel_id=1, source_target_pairs={{0,8},{1,1},{2,26},{3,3},{4,74},{5,5},{6,92},{7,7},{8,140},{9,9},{... | collective-permute-start | bytes 196616 | tf_op jit(solution)/shard_map/ppermute | solution.py:121
  17.4 16.8 %copy-start = (bf16[256,256]{1,0:T(8,128)(2,1)S(1)}, bf16[256,256]{1,0:T(8,128)(2,1)}, u32[]{:S(2)}) copy-start(bf16[256,256]{1,0:T(8,128)(2,1)} %param.7) | copy-start | bytes 393220
  17.4 30.3 %all-to-all-start = ((bf16[16,128,256]{2,1,0:T(8,128)(2,1)}), bf16[16,128,256]{2,1,0:T(8,128)(2,1)S(1)}, u32[]{:S(2)}, u32[]{:S(2)}) async-start(bf16[16,128,256]{2,1,0:T(8,128)(2,1)} %broadcast_in_dim.6), calls=%async_computation | async-start | bytes 2097152 | tf_op jit(solution)/shard_map/all_to_all | solution.py:81
  34.2 0.9 copy-start.1
  34.3 3.3 %copy-start.2 = (bf16[128,256]{1,0:T(8,128)(2,1)S(1)}, bf16[128,256]{1,0:T(8,128)(2,1)}, u32[]{:S(2)}) copy-start(bf16[128,256]{1,0:T(8,128)(2,1)} %param.6) | copy-start | bytes 196612
  35.2 12.6 %collective-permute-start.3 = (bf16[256,512]{0,1:T(8,128)(2,1)S(1)}, bf16[256,512]{0,1:T(8,128)(2,1)S(1)}, u32[]{:S(2)}, u32[]{:S(2)}) collective-permute-start(bf16[256,512]{0,1:T(8,128)(2,1)S(1)} %maximum_select_fusion.1), channel_id=1, source_target_pairs={{0,32},{2,34},{4,36},{6,38},{8,40},{10,42},{12,44},{14,46},{16,48}... | collective-permute-start | bytes 786440 | tf_op jit(solution)/shard_map/ppermute | solution.py:132
  37.6 3.1 %collective-permute-start.2 = (bf16[128,256]{1,0:T(8,128)(2,1)S(1)}, bf16[128,256]{1,0:T(8,128)(2,1)S(1)}, u32[]{:S(2)}, u32[]{:S(2)}) collective-permute-start(bf16[128,256]{1,0:T(8,128)(2,1)S(1)} %copy-done.2), channel_id=1, source_target_pairs={{0,1},{1,0},{2,3},{3,2},{4,5},{5,4},{6,7},{7,6},{8,9},{9,8},{10,11... | collective-permute-start | bytes 196616 | tf_op jit(solution)/shard_map/ppermute | solution.py:129
  76.6 11.2 %collective-permute-start.4 = (bf16[128,512]{1,0:T(8,128)(2,1)S(1)}, bf16[128,512]{1,0:T(8,128)(2,1)S(1)}, u32[]{:S(2)}, u32[]{:S(2)}) collective-permute-start(bf16[128,512]{1,0:T(8,128)(2,1)S(1)} %fusion.17), channel_id=1, source_target_pairs={{1,256},{256,1},{3,320},{320,3},{5,384},{384,5},{7,448},{448,7},{9... | collective-permute-start | bytes 393224 | tf_op jit(solution)/shard_map/ppermute | solution.py:142
  89.0 22.7 %all-to-all-start.2 = ((bf16[8,128,512]{2,1,0:T(8,128)(2,1)}), bf16[8,128,512]{2,1,0:T(8,128)(2,1)S(1)}, u32[]{:S(2)}, u32[]{:S(2)}) async-start(bf16[8,128,512]{2,1,0:T(8,128)(2,1)} %broadcast_in_dim.7), calls=%async_computation.2 | async-start | bytes 2097152 | tf_op jit(solution)/shard_map/all_to_all | solution.py:81
  92.9 10.1 %collective-permute-start.5 = (bf16[128,256]{1,0:T(8,128)(2,1)S(1)}, bf16[128,256]{1,0:T(8,128)(2,1)S(1)}, u32[]{:S(2)}, u32[]{:S(2)}) collective-permute-start(bf16[128,256]{1,0:T(8,128)(2,1)S(1)} %slice.110), channel_id=1, source_target_pairs={{0,1},{1,0},{2,3},{3,2},{4,5},{5,4},{6,7},{7,6},{8,9},{9,8},{10,11... | collective-permute-start | bytes 196616 | tf_op jit(solution)/shard_map/ppermute | solution.py:147
  113.1 4.5 %collective-permute-start.6 = (bf16[2,1024,128]{2,1,0:T(8,128)(2,1)S(1)}, bf16[2,1024,128]{2,1,0:T(8,128)(2,1)S(1)}, u32[]{:S(2)}, u32[]{:S(2)}) collective-permute-start(bf16[2,1024,128]{2,1,0:T(8,128)(2,1)S(1)} %pad_maximum_fusion), channel_id=1, source_target_pairs={{0,1},{1,0},{2,3},{3,2},{4,5},{5,4},{6,7},{7,6},{8,9},{9,8},{10,11... | collective-permute-start | bytes 1572872 | tf_op jit(solution)/shard_map/ppermute | solution.py:161
  118.4 25.0 %all-to-all-start.3 = ((bf16[16,128,128]{2,1,0:T(8,128)(2,1)}), bf16[16,128,128]{2,1,0:T(8,128)(2,1)S(1)}, u32[]{:S(2)}, u32[]{:S(2)}) async-start(bf16[16,128,128]{2,1,0:T(8,128)(2,1)} %bitcast.13), calls=%async_computation.3 | async-start | bytes 1048576 | tf_op jit(solution)/shard_map/all_to_all | solution.py:81
  126.7 16.0 %collective-permute-start.9 = (f32[256,256]{1,0:T(8,128)S(1)}, f32[256,256]{1,0:T(8,128)S(1)}, u32[]{:S(2)}, u32[]{:S(2)}) collective-permute-start(f32[256,256]{1,0:T(8,128)S(1)} %slice_bitcast_fusion), channel_id=1, source_target_pairs={{0,1},{1,0},{2,3},{3,2},{4,5},{5,4},{6,7},{7,6},{8,9},{9,8},{10,11... | collective-permute-start | bytes 786440 | tf_op jit(solution)/shard_map/ppermute | solution.py:168
  128.6 8.7 %collective-permute-start.10 = (bf16[256,256]{1,0:T(8,128)(2,1)S(1)}, bf16[256,256]{1,0:T(8,128)(2,1)S(1)}, u32[]{:S(2)}, u32[]{:S(2)}) collective-permute-start(bf16[256,256]{1,0:T(8,128)(2,1)S(1)} %fusion.16), channel_id=1, source_target_pairs={{32,1},{34,3},{36,5},{38,7},{40,9},{42,11},{44,13},{46,15},{48,17}... | collective-permute-start | bytes 393224 | tf_op jit(solution)/shard_map/ppermute | solution.py:172
  130.8 12.0 %collective-permute-start.8 = (bf16[256,256]{1,0:T(8,128)(2,1)S(1)}, bf16[256,256]{1,0:T(8,128)(2,1)S(1)}, u32[]{:S(2)}, u32[]{:S(2)}) collective-permute-start(bf16[256,256]{1,0:T(8,128)(2,1)S(1)} %fusion.15), channel_id=1, source_target_pairs={{0,32},{2,34},{4,36},{6,38},{8,40},{10,42},{12,44},{14,46},{16,48}... | collective-permute-start | bytes 393224 | tf_op jit(solution)/shard_map/ppermute | solution.py:171
  143.6 5.8 %collective-permute-start.7 = (bf16[128,128]{1,0:T(8,128)(2,1)S(1)}, bf16[128,128]{1,0:T(8,128)(2,1)S(1)}, u32[]{:S(2)}, u32[]{:S(2)}) collective-permute-start(bf16[128,128]{1,0:T(8,128)(2,1)S(1)} %reduce_sum.22), channel_id=1, source_target_pairs={{0,0},{1,1},{2,2},{3,3},{4,4},{5,5},{6,6},{7,7},{8,8},{9,9},{10,10... | collective-permute-start | bytes 98312 | tf_op jit(solution)/shard_map/ppermute | solution.py:170

commit v8 on v7

--- a/solution.py
+++ b/solution.py
@@ -89,11 +89,6 @@
     return jnp.sum(trade(partial.astype(jnp.bfloat16), groups).astype(jnp.float32), axis=0)
 
 
-def fold(block):
-    half = block.shape[1] // 2
-    return jnp.concatenate([block[:, :half], block[:, half:]], axis=0)
-
-
 def unfold(tall):
     half = tall.shape[0] // 2
     return jnp.concatenate([tall[:half], tall[half:]], axis=1)
@@ -113,10 +108,11 @@
     f32, bf16 = jnp.float32, jnp.bfloat16
     first = lax.axis_index("c") == 0
     inner, width = gate_weight.shape[1], out_grad.shape[1]
+    half = gate_weight.shape[1] // 2
+    to_first = jnp.concatenate([tokens, gate_weight[:, :half], gate_weight[:, half:]], axis=0)
+    to_second = jnp.concatenate([out_grad, out_weight], axis=0)
+    sent = with_layout_constraint(jnp.where(first, to_second, to_first), BY_ROWS)
     mine = jnp.where(first, tokens, out_grad)
-    yours = jnp.where(first, out_grad, tokens)
-    block = jnp.where(first, out_weight, fold(gate_weight))
-    sent = with_layout_constraint(jnp.concatenate([yours, block], axis=0), BY_ROWS)
     swapped = with_layout_constraint(lax.ppermute(sent, ALL, SWAP), BY_ROWS)
     pair = lax.ppermute(jnp.concatenate([mine, swapped[: mine.shape[0]]], axis=1), ALL, SPREAD)
     block = swapped[mine.shape[0] :]

time: 151 us -> 150 us (level)
  no operation moved by 1% of the time
where the time goes in v8:
time: 150 us; the launch traced here: 149 us
  starting transfers between devices  69.1 us (46%)
  waiting for transfers between devices  37.9 us (25%)
  blocking collectives  27.8 us (19%)
  local copies, waits for them, and re-layouts  5.46 us (4%)
  other arithmetic  4.78 us (3%)
  matrix products  3.2 us (2%)
    all_to_all x3, starting transfers between devices, trade(): lax.all_to_all(blocks, ALL, split_axis=0, concat_axis=0, axis_index_group...  28.8 us
    all_to_all x1, blocking collectives, trade(): lax.all_to_all(blocks, ALL, split_axis=0, concat_axis=0, axis_index_group...  27.8 us
    all_to_all x3, waiting for transfers between devices, trade(): lax.all_to_all(blocks, ALL, split_axis=0, concat_axis=0, axis_index_group...  15.8 us
    ppermute x1, waiting for transfers between devices, local(): lax.ppermute(jnp.where(first, gated, total.astype(bf16)), ALL, CROSS)  9.27 us
    ppermute x1, starting transfers between devices, local(): mixer_grad_in = lax.ppermute(mixer_grad[:, inner:], ALL, SWAP)  9.21 us
    ppermute x1, starting transfers between devices, local(): lax.ppermute(jnp.concatenate([mine, swapped[:mine.shape[0]]], axis=1), AL...  7.7 us
    ppermute x1, waiting for transfers between devices, local(): lax.ppermute(keep_far, ALL, PARTNER).astype(f32)  5.36 us
    ppermute x1, starting transfers between devices, local(): lax.ppermute(keep_far, ALL, PARTNER).astype(f32)  5.34 us
  transfers between devices with their start and end apart: 14, of which 11 were waited for; matrix products, arithmetic and copies ran while one was open for 3% of the time, Pallas kernels for 0%

profile of v8, /device:TPU:2, one launch (start us, length us, event | category | flops | bytes accessed | tf_op | source)
XLA Modules:
  0.0 149.2 jit_solution(10909933036983401245)
XLA Ops:
  0.6 0.9 fusion.26
  1.5 1.0 maximum_select_fusion.2
  2.5 1.9 %collective-permute-start = (bf16[640,128]{1,0:T(8,128)(2,1)S(1)}, bf16[640,128]{1,0:T(8,128)(2,1)S(1)}, u32[]{:S(2)}, u32[]{:S(2)}) collective-permute-start(bf16[640,128]{1,0:T(8,128)(2,1)S(1)} %maximum_select_fusion.2), channel_id=1, source_target_pairs={{0,1},{1,0},{2,3},{3,2},{4,5},{5,4},{6,7},{7,6},{8,9},{9,8},{10,11... | collective-permute-start | bytes 491528 | tf_op jit(solution)/shard_map/ppermute | solution.py:116
  4.4 0.8 broadcast_select_fusion.2
  5.2 0.6 collective-permute-done
  5.8 7.7 %collective-permute-start.1 = (bf16[128,256]{1,0:T(8,128)(2,1)S(1)}, bf16[128,256]{1,0:T(8,128)(2,1)S(1)}, u32[]{:S(2)}, u32[]{:S(2)}) collective-permute-start(bf16[128,256]{1,0:T(8,128)(2,1)S(1)} %pad_maximum_fusion.2), channel_id=1, source_target_pairs={{0,8},{1,1},{2,26},{3,3},{4,74},{5,5},{6,92},{7,7},{8,140},{9,9},{... | collective-permute-start | bytes 196616 | tf_op jit(solution)/shard_map/ppermute | solution.py:117
  13.5 2.0 %collective-permute-done.1 = bf16[128,256]{1,0:T(8,128)(2,1)S(1)} collective-permute-done((bf16[128,256]{1,0:T(8,128)(2,1)S(1)}, bf16[128,256]{1,0:T(8,128)(2,1)S(1)}, u32[]{:S(2)}, u32[]{:S(2)}) %collective-permute-start.1) | collective-permute-done | bytes 65568 | tf_op jit(solution)/shard_map/ppermute | solution.py:117
  15.6 1.1 broadcast_in_dim.6
  16.7 0.0 copy-start
  16.7 16.8 %all-to-all-start = ((bf16[16,128,256]{2,1,0:T(8,128)(2,1)}), bf16[16,128,256]{2,1,0:T(8,128)(2,1)S(1)}, u32[]{:S(2)}, u32[]{:S(2)}) async-start(bf16[16,128,256]{2,1,0:T(8,128)(2,1)} %broadcast_in_dim.6), calls=%async_computation | async-start | bytes 2097152 | tf_op jit(solution)/shard_map/all_to_all | solution.py:81
  33.5 0.0 copy-done
  33.5 0.0 copy-start.1
  33.5 0.0 copy-start.2
  33.5 0.1 copy.17
  33.6 0.1 copy.27
  33.7 0.1 copy.28
  33.9 0.5 copy-done.1
  34.4 0.1 maximum_select_fusion.1
  34.5 2.3 %collective-permute-start.3 = (bf16[256,512]{0,1:T(8,128)(2,1)S(1)}, bf16[256,512]{0,1:T(8,128)(2,1)S(1)}, u32[]{:S(2)}, u32[]{:S(2)}) collective-permute-start(bf16[256,512]{0,1:T(8,128)(2,1)S(1)} %maximum_select_fusion.1), channel_id=1, source_target_pairs={{0,32},{2,34},{4,36},{6,38},{8,40},{10,42},{12,44},{14,46},{16,48}... | collective-permute-start | bytes 786440 | tf_op jit(solution)/shard_map/ppermute | solution.py:128
  36.8 0.0 copy-done.2
  36.8 1.9 %collective-permute-start.2 = (bf16[128,256]{1,0:T(8,128)(2,1)S(1)}, bf16[128,256]{1,0:T(8,128)(2,1)S(1)}, u32[]{:S(2)}, u32[]{:S(2)}) collective-permute-start(bf16[128,256]{1,0:T(8,128)(2,1)S(1)} %copy-done.2), channel_id=1, source_target_pairs={{0,1},{1,0},{2,3},{3,2},{4,5},{5,4},{6,7},{7,6},{8,9},{9,8},{10,11... | collective-permute-start | bytes 196616 | tf_op jit(solution)/shard_map/ppermute | solution.py:125
  38.7 1.2 collective-permute-done.2
  39.9 7.1 %all-to-all-done = bf16[16,128,256]{2,1,0:T(8,128)(2,1)S(1)} async-done(((bf16[16,128,256]{2,1,0:T(8,128)(2,1)}), bf16[16,128,256]{2,1,0:T(8,128)(2,1)S(1)}, u32[]{:S(2)}, u32[]{:S(2)}) %all-to-all-start) | async-done | bytes 1048608 | tf_op jit(solution)/shard_map/all_to_all | solution.py:81
  47.0 0.0 collective-permute-done.3
  47.0 0.7 bitcast_convert_fusion
  47.8 27.8 %all_to_all.20 = bf16[8,128,512]{2,1,0:T(8,128)(2,1)S(1)} all-to-all(bf16[8,128,512]{2,1,0:T(8,128)(2,1)S(1)} %bitcast_convert_fusion), channel_id=1, replica_groups={{0,64,128,192,256,320,384,448},{2,66,130,194,258,322,386,450},{4,68,132..., dimensions={0} | all-to-all | bytes 2097152 | tf_op jit(solution)/shard_map/all_to_all | solution.py:81
  75.6 0.1 convert_reduce_fusion
  75.7 0.1 fusion.17
  75.8 1.9 %collective-permute-start.4 = (bf16[128,512]{1,0:T(8,128)(2,1)S(1)}, bf16[128,512]{1,0:T(8,128)(2,1)S(1)}, u32[]{:S(2)}, u32[]{:S(2)}) collective-permute-start(bf16[128,512]{1,0:T(8,128)(2,1)S(1)} %fusion.17), channel_id=1, source_target_pairs={{1,256},{256,1},{3,320},{320,3},{5,384},{384,5},{7,448},{448,7},{9... | collective-permute-start | bytes 393224 | tf_op jit(solution)/shard_map/ppermute | solution.py:138
  77.8 9.3 %collective-permute-done.4 = bf16[128,512]{1,0:T(8,128)(2,1)S(1)} collective-permute-done((bf16[128,512]{1,0:T(8,128)(2,1)S(1)}, bf16[128,512]{1,0:T(8,128)(2,1)S(1)}, u32[]{:S(2)}, u32[]{:S(2)}) %collective-permute-start.4) | collective-permute-done | bytes 131104 | tf_op jit(solution)/shard_map/ppermute | solution.py:138
  87.0 0.1 fusion.14
  87.2 1.1 broadcast_in_dim.7
  88.2 3.8 %all-to-all-start.2 = ((bf16[8,128,512]{2,1,0:T(8,128)(2,1)}), bf16[8,128,512]{2,1,0:T(8,128)(2,1)S(1)}, u32[]{:S(2)}, u32[]{:S(2)}) async-start(bf16[8,128,512]{2,1,0:T(8,128)(2,1)} %broadcast_in_dim.7), calls=%async_computation.2 | async-start | bytes 2097152 | tf_op jit(solution)/shard_map/all_to_all | solution.py:81
  92.0 0.1 fusion.10
  92.1 9.2 %collective-permute-start.5 = (bf16[128,256]{1,0:T(8,128)(2,1)S(1)}, bf16[128,256]{1,0:T(8,128)(2,1)S(1)}, u32[]{:S(2)}, u32[]{:S(2)}) collective-permute-start(bf16[128,256]{1,0:T(8,128)(2,1)S(1)} %slice.110), channel_id=1, source_target_pairs={{0,1},{1,0},{2,3},{3,2},{4,5},{5,4},{6,7},{7,6},{8,9},{9,8},{10,11... | collective-permute-start | bytes 196616 | tf_op jit(solution)/shard_map/ppermute | solution.py:143
  101.3 0.9 collective-permute-done.5
  102.2 8.8 %all-to-all-done.2 = bf16[8,128,512]{2,1,0:T(8,128)(2,1)S(1)} async-done(((bf16[8,128,512]{2,1,0:T(8,128)(2,1)}), bf16[8,128,512]{2,1,0:T(8,128)(2,1)S(1)}, u32[]{:S(2)}, u32[]{:S(2)}) %all-to-all-start.2) | async-done | bytes 1048608 | tf_op jit(solution)/shard_map/all_to_all | solution.py:81
  111.0 0.4 fusion.2
  111.4 0.4 fusion
  111.8 0.4 fusion.1
  112.3 0.1 pad_maximum_fusion
  112.3 2.9 %collective-permute-start.6 = (bf16[2,1024,128]{2,1,0:T(8,128)(2,1)S(1)}, bf16[2,1024,128]{2,1,0:T(8,128)(2,1)S(1)}, u32[]{:S(2)}, u32[]{:S(2)}) collective-permute-start(bf16[2,1024,128]{2,1,0:T(8,128)(2,1)S(1)} %pad_maximum_fusion), channel_id=1, source_target_pairs={{0,1},{1,0},{2,3},{3,2},{4,5},{5,4},{6,7},{7,6},{8,9},{9,8},{10,11... | collective-permute-start | bytes 1572872 | tf_op jit(solution)/shard_map/ppermute | solution.py:157
  115.3 0.7 fusion.27
  116.0 0.1 fusion.23
  116.1 0.4 fusion.3
  116.6 0.1 slice_select_fusion.1
  116.7 0.1 collective-permute-done.6
  116.8 0.9 maximum_select_fusion
  117.7 8.3 %all-to-all-start.3 = ((bf16[16,128,128]{2,1,0:T(8,128)(2,1)}), bf16[16,128,128]{2,1,0:T(8,128)(2,1)S(1)}, u32[]{:S(2)}, u32[]{:S(2)}) async-start(bf16[16,128,128]{2,1,0:T(8,128)(2,1)} %bitcast.13), calls=%async_computation.3 | async-start | bytes 1048576 | tf_op jit(solution)/shard_map/all_to_all | solution.py:81
  125.9 1.9 %collective-permute-start.9 = (f32[256,256]{1,0:T(8,128)S(1)}, f32[256,256]{1,0:T(8,128)S(1)}, u32[]{:S(2)}, u32[]{:S(2)}) collective-permute-start(f32[256,256]{1,0:T(8,128)S(1)} %slice_bitcast_fusion), channel_id=1, source_target_pairs={{0,1},{1,0},{2,3},{3,2},{4,5},{5,4},{6,7},{7,6},{8,9},{9,8},{10,11... | collective-permute-start | bytes 786440 | tf_op jit(solution)/shard_map/ppermute | solution.py:164
  127.9 2.1 %collective-permute-start.10 = (bf16[256,256]{1,0:T(8,128)(2,1)S(1)}, bf16[256,256]{1,0:T(8,128)(2,1)S(1)}, u32[]{:S(2)}, u32[]{:S(2)}) collective-permute-start(bf16[256,256]{1,0:T(8,128)(2,1)S(1)} %fusion.16), channel_id=1, source_target_pairs={{32,1},{34,3},{36,5},{38,7},{40,9},{42,11},{44,13},{46,15},{48,17}... | collective-permute-start | bytes 393224 | tf_op jit(solution)/shard_map/ppermute | solution.py:168
  130.0 5.3 %collective-permute-start.8 = (bf16[256,256]{1,0:T(8,128)(2,1)S(1)}, bf16[256,256]{1,0:T(8,128)(2,1)S(1)}, u32[]{:S(2)}, u32[]{:S(2)}) collective-permute-start(bf16[256,256]{1,0:T(8,128)(2,1)S(1)} %fusion.15), channel_id=1, source_target_pairs={{0,32},{2,34},{4,36},{6,38},{8,40},{10,42},{12,44},{14,46},{16,48}... | collective-permute-start | bytes 393224 | tf_op jit(solution)/shard_map/ppermute | solution.py:167
  135.4 0.6 slice_select_fusion.2
  136.0 0.6 collective-permute-done.10
  136.6 5.4 %collective-permute-done.8 = bf16[256,256]{1,0:T(8,128)(2,1)S(1)} collective-permute-done((bf16[256,256]{1,0:T(8,128)(2,1)S(1)}, bf16[256,256]{1,0:T(8,128)(2,1)S(1)}, u32[]{:S(2)}, u32[]{:S(2)}) %collective-permute-start.8) | collective-permute-done | bytes 131104 | tf_op jit(solution)/shard_map/ppermute | solution.py:167
  142.0 0.0 collective-permute-done.9
  142.0 0.7 broadcast_select_fusion
  142.7 0.0 all-to-all-done.3
  142.7 0.1 reduce_sum.22
  142.8 2.9 %collective-permute-start.7 = (bf16[128,128]{1,0:T(8,128)(2,1)S(1)}, bf16[128,128]{1,0:T(8,128)(2,1)S(1)}, u32[]{:S(2)}, u32[]{:S(2)}) collective-permute-start(bf16[128,128]{1,0:T(8,128)(2,1)S(1)} %reduce_sum.22), channel_id=1, source_target_pairs={{0,0},{1,1},{2,2},{3,3},{4,4},{5,5},{6,6},{7,7},{8,8},{9,9},{10,10... | collective-permute-start | bytes 98312 | tf_op jit(solution)/shard_map/ppermute | solution.py:166
  145.7 0.8 copy.21
  146.5 2.1 %collective-permute-done.7 = bf16[128,128]{1,0:T(8,128)(2,1)S(1)} collective-permute-done((bf16[128,128]{1,0:T(8,128)(2,1)S(1)}, bf16[128,128]{1,0:T(8,128)(2,1)S(1)}, u32[]{:S(2)}, u32[]{:S(2)}) %collective-permute-start.7) | collective-permute-done | bytes 32800 | tf_op jit(solution)/shard_map/ppermute | solution.py:166
  148.6 0.6 copy.30
  (10 shorter events, 0.1 us)
Async XLA Ops:
  2.5 3.3 %collective-permute-start = (bf16[640,128]{1,0:T(8,128)(2,1)S(1)}, bf16[640,128]{1,0:T(8,128)(2,1)S(1)}, u32[]{:S(2)}, u32[]{:S(2)}) collective-permute-start(bf16[640,128]{1,0:T(8,128)(2,1)S(1)} %maximum_select_fusion.2), channel_id=1, source_target_pairs={{0,1},{1,0},{2,3},{3,2},{4,5},{5,4},{6,7},{7,6},{8,9},{9,8},{10,11... | collective-permute-start | bytes 491528 | tf_op jit(solution)/shard_map/ppermute | solution.py:116
  5.8 9.8 %collective-permute-start.1 = (bf16[128,256]{1,0:T(8,128)(2,1)S(1)}, bf16[128,256]{1,0:T(8,128)(2,1)S(1)}, u32[]{:S(2)}, u32[]{:S(2)}) collective-permute-start(bf16[128,256]{1,0:T(8,128)(2,1)S(1)} %pad_maximum_fusion.2), channel_id=1, source_target_pairs={{0,8},{1,1},{2,26},{3,3},{4,74},{5,5},{6,92},{7,7},{8,140},{9,9},{... | collective-permute-start | bytes 196616 | tf_op jit(solution)/shard_map/ppermute | solution.py:117
  16.7 16.8 %copy-start = (bf16[256,256]{1,0:T(8,128)(2,1)S(1)}, bf16[256,256]{1,0:T(8,128)(2,1)}, u32[]{:S(2)}) copy-start(bf16[256,256]{1,0:T(8,128)(2,1)} %param.7) | copy-start | bytes 393220
  16.7 30.3 %all-to-all-start = ((bf16[16,128,256]{2,1,0:T(8,128)(2,1)}), bf16[16,128,256]{2,1,0:T(8,128)(2,1)S(1)}, u32[]{:S(2)}, u32[]{:S(2)}) async-start(bf16[16,128,256]{2,1,0:T(8,128)(2,1)} %broadcast_in_dim.6), calls=%async_computation | async-start | bytes 2097152 | tf_op jit(solution)/shard_map/all_to_all | solution.py:81
  33.5 0.9 copy-start.1
  33.5 3.3 %copy-start.2 = (bf16[128,256]{1,0:T(8,128)(2,1)S(1)}, bf16[128,256]{1,0:T(8,128)(2,1)}, u32[]{:S(2)}) copy-start(bf16[128,256]{1,0:T(8,128)(2,1)} %param.6) | copy-start | bytes 196612
  34.5 12.6 %collective-permute-start.3 = (bf16[256,512]{0,1:T(8,128)(2,1)S(1)}, bf16[256,512]{0,1:T(8,128)(2,1)S(1)}, u32[]{:S(2)}, u32[]{:S(2)}) collective-permute-start(bf16[256,512]{0,1:T(8,128)(2,1)S(1)} %maximum_select_fusion.1), channel_id=1, source_target_pairs={{0,32},{2,34},{4,36},{6,38},{8,40},{10,42},{12,44},{14,46},{16,48}... | collective-permute-start | bytes 786440 | tf_op jit(solution)/shard_map/ppermute | solution.py:128
  36.8 3.1 %collective-permute-start.2 = (bf16[128,256]{1,0:T(8,128)(2,1)S(1)}, bf16[128,256]{1,0:T(8,128)(2,1)S(1)}, u32[]{:S(2)}, u32[]{:S(2)}) collective-permute-start(bf16[128,256]{1,0:T(8,128)(2,1)S(1)} %copy-done.2), channel_id=1, source_target_pairs={{0,1},{1,0},{2,3},{3,2},{4,5},{5,4},{6,7},{7,6},{8,9},{9,8},{10,11... | collective-permute-start | bytes 196616 | tf_op jit(solution)/shard_map/ppermute | solution.py:125
  75.8 11.2 %collective-permute-start.4 = (bf16[128,512]{1,0:T(8,128)(2,1)S(1)}, bf16[128,512]{1,0:T(8,128)(2,1)S(1)}, u32[]{:S(2)}, u32[]{:S(2)}) collective-permute-start(bf16[128,512]{1,0:T(8,128)(2,1)S(1)} %fusion.17), channel_id=1, source_target_pairs={{1,256},{256,1},{3,320},{320,3},{5,384},{384,5},{7,448},{448,7},{9... | collective-permute-start | bytes 393224 | tf_op jit(solution)/shard_map/ppermute | solution.py:138
  88.2 22.7 %all-to-all-start.2 = ((bf16[8,128,512]{2,1,0:T(8,128)(2,1)}), bf16[8,128,512]{2,1,0:T(8,128)(2,1)S(1)}, u32[]{:S(2)}, u32[]{:S(2)}) async-start(bf16[8,128,512]{2,1,0:T(8,128)(2,1)} %broadcast_in_dim.7), calls=%async_computation.2 | async-start | bytes 2097152 | tf_op jit(solution)/shard_map/all_to_all | solution.py:81
  92.1 10.1 %collective-permute-start.5 = (bf16[128,256]{1,0:T(8,128)(2,1)S(1)}, bf16[128,256]{1,0:T(8,128)(2,1)S(1)}, u32[]{:S(2)}, u32[]{:S(2)}) collective-permute-start(bf16[128,256]{1,0:T(8,128)(2,1)S(1)} %slice.110), channel_id=1, source_target_pairs={{0,1},{1,0},{2,3},{3,2},{4,5},{5,4},{6,7},{7,6},{8,9},{9,8},{10,11... | collective-permute-start | bytes 196616 | tf_op jit(solution)/shard_map/ppermute | solution.py:143
  112.3 4.5 %collective-permute-start.6 = (bf16[2,1024,128]{2,1,0:T(8,128)(2,1)S(1)}, bf16[2,1024,128]{2,1,0:T(8,128)(2,1)S(1)}, u32[]{:S(2)}, u32[]{:S(2)}) collective-permute-start(bf16[2,1024,128]{2,1,0:T(8,128)(2,1)S(1)} %pad_maximum_fusion), channel_id=1, source_target_pairs={{0,1},{1,0},{2,3},{3,2},{4,5},{5,4},{6,7},{7,6},{8,9},{9,8},{10,11... | collective-permute-start | bytes 1572872 | tf_op jit(solution)/shard_map/ppermute | solution.py:157
  117.7 25.0 %all-to-all-start.3 = ((bf16[16,128,128]{2,1,0:T(8,128)(2,1)}), bf16[16,128,128]{2,1,0:T(8,128)(2,1)S(1)}, u32[]{:S(2)}, u32[]{:S(2)}) async-start(bf16[16,128,128]{2,1,0:T(8,128)(2,1)} %bitcast.13), calls=%async_computation.3 | async-start | bytes 1048576 | tf_op jit(solution)/shard_map/all_to_all | solution.py:81
  125.9 16.0 %collective-permute-start.9 = (f32[256,256]{1,0:T(8,128)S(1)}, f32[256,256]{1,0:T(8,128)S(1)}, u32[]{:S(2)}, u32[]{:S(2)}) collective-permute-start(f32[256,256]{1,0:T(8,128)S(1)} %slice_bitcast_fusion), channel_id=1, source_target_pairs={{0,1},{1,0},{2,3},{3,2},{4,5},{5,4},{6,7},{7,6},{8,9},{9,8},{10,11... | collective-permute-start | bytes 786440 | tf_op jit(solution)/shard_map/ppermute | solution.py:164
  127.9 8.7 %collective-permute-start.10 = (bf16[256,256]{1,0:T(8,128)(2,1)S(1)}, bf16[256,256]{1,0:T(8,128)(2,1)S(1)}, u32[]{:S(2)}, u32[]{:S(2)}) collective-permute-start(bf16[256,256]{1,0:T(8,128)(2,1)S(1)} %fusion.16), channel_id=1, source_target_pairs={{32,1},{34,3},{36,5},{38,7},{40,9},{42,11},{44,13},{46,15},{48,17}... | collective-permute-start | bytes 393224 | tf_op jit(solution)/shard_map/ppermute | solution.py:168
  130.0 11.9 %collective-permute-start.8 = (bf16[256,256]{1,0:T(8,128)(2,1)S(1)}, bf16[256,256]{1,0:T(8,128)(2,1)S(1)}, u32[]{:S(2)}, u32[]{:S(2)}) collective-permute-start(bf16[256,256]{1,0:T(8,128)(2,1)S(1)} %fusion.15), channel_id=1, source_target_pairs={{0,32},{2,34},{4,36},{6,38},{8,40},{10,42},{12,44},{14,46},{16,48}... | collective-permute-start | bytes 393224 | tf_op jit(solution)/shard_map/ppermute | solution.py:167
  142.8 5.8 %collective-permute-start.7 = (bf16[128,128]{1,0:T(8,128)(2,1)S(1)}, bf16[128,128]{1,0:T(8,128)(2,1)S(1)}, u32[]{:S(2)}, u32[]{:S(2)}) collective-permute-start(bf16[128,128]{1,0:T(8,128)(2,1)S(1)} %reduce_sum.22), channel_id=1, source_target_pairs={{0,0},{1,1},{2,2},{3,3},{4,4},{5,5},{6,6},{7,7},{8,8},{9,9},{10,10... | collective-permute-start | bytes 98312 | tf_op jit(solution)/shard_map/ppermute | solution.py:166

commit v9 on v8

--- a/solution.py
+++ b/solution.py
@@ -144,7 +144,7 @@
     units, mixer_grad_in = lax.optimization_barrier((units, mixer_grad_in))
     units = units.reshape(-1, units.shape[2])
 
-    def layer_part(start):
+    def layer_part(units, start):
         return jnp.stack(
             [
                 lax.dot_general(
@@ -154,8 +154,9 @@
             ]
         )
 
-    layer_in = lax.ppermute(layer_part(width), ALL, SWAP)
-    layer_blocks = jnp.where(first, layer_in, layer_part(0))
+    layer_sent, units = lax.optimization_barrier((layer_part(units, width), units))
+    layer_in = lax.ppermute(layer_sent, ALL, SWAP)
+    layer_blocks = jnp.where(first, layer_in, layer_part(units, 0))
     layer_own = reduce(layer_blocks.reshape(2 * N, -1, width), ROW_GROUPS).astype(bf16)
 
     grads = jnp.einsum("kad,an->kdn", acts, units, preferred_element_type=f32)

time: 150 us -> 150 us (level)
  transfers between devices with their start and end apart: 14 -> 14, of which waited for: 11 -> 10; matrix products, arithmetic and copies ran while one was open for 3% -> 4% of each run, Pallas kernels for 0% -> 0%
where the time goes in v9:
time: 150 us; the launch traced here: 149 us
  starting transfers between devices  69.1 us (46%)
  waiting for transfers between devices  37.5 us (25%)
  blocking collectives  27.8 us (19%)
  local copies, waits for them, and re-layouts  5.46 us (4%)
  other arithmetic  4.78 us (3%)
  matrix products  3.2 us (2%)
    all_to_all x3, starting transfers between devices, trade(): lax.all_to_all(blocks, ALL, split_axis=0, concat_axis=0, axis_index_group...  28.8 us
    all_to_all x1, blocking collectives, trade(): lax.all_to_all(blocks, ALL, split_axis=0, concat_axis=0, axis_index_group...  27.8 us
    all_to_all x3, waiting for transfers between devices, trade(): lax.all_to_all(blocks, ALL, split_axis=0, concat_axis=0, axis_index_group...  15.8 us
    ppermute x1, waiting for transfers between devices, local(): lax.ppermute(jnp.where(first, gated, total.astype(bf16)), ALL, CROSS)  9.27 us
    ppermute x1, starting transfers between devices, local(): mixer_grad_in = lax.ppermute(mixer_grad[:, inner:], ALL, SWAP)  9.21 us
    ppermute x1, starting transfers between devices, local(): lax.ppermute(jnp.concatenate([mine, swapped[:mine.shape[0]]], axis=1), AL...  7.7 us
    ppermute x1, starting transfers between devices, local(): lax.ppermute(keep_far, ALL, PARTNER).astype(f32)  5.34 us
    ppermute x1, waiting for transfers between devices, local(): lax.ppermute(keep_far, ALL, PARTNER).astype(f32)  5.31 us
  transfers between devices with their start and end apart: 14, of which 10 were waited for; matrix products, arithmetic and copies ran while one was open for 4% of the time, Pallas kernels for 0%

profile of v9, /device:TPU:2, one launch (start us, length us, event | category | flops | bytes accessed | tf_op | source)
XLA Modules:
  0.0 148.8 jit_solution(16755739435005223560)
XLA Ops:
  0.6 0.9 fusion.28
  1.5 1.0 maximum_select_fusion.2
  2.5 1.9 %collective-permute-start = (bf16[640,128]{1,0:T(8,128)(2,1)S(1)}, bf16[640,128]{1,0:T(8,128)(2,1)S(1)}, u32[]{:S(2)}, u32[]{:S(2)}) collective-permute-start(bf16[640,128]{1,0:T(8,128)(2,1)S(1)} %maximum_select_fusion.2), channel_id=1, source_target_pairs={{0,1},{1,0},{2,3},{3,2},{4,5},{5,4},{6,7},{7,6},{8,9},{9,8},{10,11... | collective-permute-start | bytes 491528 | tf_op jit(solution)/shard_map/ppermute | solution.py:116
  4.4 0.8 broadcast_select_fusion.2
  5.2 0.6 collective-permute-done
  5.8 7.7 %collective-permute-start.1 = (bf16[128,256]{1,0:T(8,128)(2,1)S(1)}, bf16[128,256]{1,0:T(8,128)(2,1)S(1)}, u32[]{:S(2)}, u32[]{:S(2)}) collective-permute-start(bf16[128,256]{1,0:T(8,128)(2,1)S(1)} %pad_maximum_fusion.2), channel_id=1, source_target_pairs={{0,8},{1,1},{2,26},{3,3},{4,74},{5,5},{6,92},{7,7},{8,140},{9,9},{... | collective-permute-start | bytes 196616 | tf_op jit(solution)/shard_map/ppermute | solution.py:117
  13.5 2.0 %collective-permute-done.1 = bf16[128,256]{1,0:T(8,128)(2,1)S(1)} collective-permute-done((bf16[128,256]{1,0:T(8,128)(2,1)S(1)}, bf16[128,256]{1,0:T(8,128)(2,1)S(1)}, u32[]{:S(2)}, u32[]{:S(2)}) %collective-permute-start.1) | collective-permute-done | bytes 65568 | tf_op jit(solution)/shard_map/ppermute | solution.py:117
  15.6 1.1 broadcast_in_dim.6
  16.7 0.0 copy-start
  16.7 16.8 %all-to-all-start = ((bf16[16,128,256]{2,1,0:T(8,128)(2,1)}), bf16[16,128,256]{2,1,0:T(8,128)(2,1)S(1)}, u32[]{:S(2)}, u32[]{:S(2)}) async-start(bf16[16,128,256]{2,1,0:T(8,128)(2,1)} %broadcast_in_dim.6), calls=%async_computation | async-start | bytes 2097152 | tf_op jit(solution)/shard_map/all_to_all | solution.py:81
  33.5 0.0 copy-done
  33.5 0.0 copy-start.1
  33.5 0.0 copy-start.2
  33.5 0.1 copy.17
  33.6 0.1 copy.28
  33.7 0.1 copy.27
  33.9 0.5 copy-done.1
  34.4 0.1 maximum_select_fusion.1
  34.5 2.3 %collective-permute-start.3 = (bf16[256,512]{0,1:T(8,128)(2,1)S(1)}, bf16[256,512]{0,1:T(8,128)(2,1)S(1)}, u32[]{:S(2)}, u32[]{:S(2)}) collective-permute-start(bf16[256,512]{0,1:T(8,128)(2,1)S(1)} %maximum_select_fusion.1), channel_id=1, source_target_pairs={{0,32},{2,34},{4,36},{6,38},{8,40},{10,42},{12,44},{14,46},{16,48}... | collective-permute-start | bytes 786440 | tf_op jit(solution)/shard_map/ppermute | solution.py:128
  36.8 0.0 copy-done.2
  36.8 1.9 %collective-permute-start.2 = (bf16[128,256]{1,0:T(8,128)(2,1)S(1)}, bf16[128,256]{1,0:T(8,128)(2,1)S(1)}, u32[]{:S(2)}, u32[]{:S(2)}) collective-permute-start(bf16[128,256]{1,0:T(8,128)(2,1)S(1)} %copy-done.2), channel_id=1, source_target_pairs={{0,1},{1,0},{2,3},{3,2},{4,5},{5,4},{6,7},{7,6},{8,9},{9,8},{10,11... | collective-permute-start | bytes 196616 | tf_op jit(solution)/shard_map/ppermute | solution.py:125
  38.7 1.2 collective-permute-done.2
  39.9 7.1 %all-to-all-done = bf16[16,128,256]{2,1,0:T(8,128)(2,1)S(1)} async-done(((bf16[16,128,256]{2,1,0:T(8,128)(2,1)}), bf16[16,128,256]{2,1,0:T(8,128)(2,1)S(1)}, u32[]{:S(2)}, u32[]{:S(2)}) %all-to-all-start) | async-done | bytes 1048608 | tf_op jit(solution)/shard_map/all_to_all | solution.py:81
  47.0 0.0 collective-permute-done.3
  47.0 0.7 bitcast_convert_fusion
  47.8 27.8 %all_to_all.20 = bf16[8,128,512]{2,1,0:T(8,128)(2,1)S(1)} all-to-all(bf16[8,128,512]{2,1,0:T(8,128)(2,1)S(1)} %bitcast_convert_fusion), channel_id=1, replica_groups={{0,64,128,192,256,320,384,448},{2,66,130,194,258,322,386,450},{4,68,132..., dimensions={0} | all-to-all | bytes 2097152 | tf_op jit(solution)/shard_map/all_to_all | solution.py:81
  75.6 0.1 convert_reduce_fusion
  75.7 0.1 fusion.19
  75.8 1.9 %collective-permute-start.4 = (bf16[128,512]{1,0:T(8,128)(2,1)S(1)}, bf16[128,512]{1,0:T(8,128)(2,1)S(1)}, u32[]{:S(2)}, u32[]{:S(2)}) collective-permute-start(bf16[128,512]{1,0:T(8,128)(2,1)S(1)} %fusion.19), channel_id=1, source_target_pairs={{1,256},{256,1},{3,320},{320,3},{5,384},{384,5},{7,448},{448,7},{9... | collective-permute-start | bytes 393224 | tf_op jit(solution)/shard_map/ppermute | solution.py:138
  77.8 9.3 %collective-permute-done.4 = bf16[128,512]{1,0:T(8,128)(2,1)S(1)} collective-permute-done((bf16[128,512]{1,0:T(8,128)(2,1)S(1)}, bf16[128,512]{1,0:T(8,128)(2,1)S(1)}, u32[]{:S(2)}, u32[]{:S(2)}) %collective-permute-start.4) | collective-permute-done | bytes 131104 | tf_op jit(solution)/shard_map/ppermute | solution.py:138
  87.0 0.1 fusion.16
  87.2 1.1 broadcast_in_dim.7
  88.2 3.8 %all-to-all-start.2 = ((bf16[8,128,512]{2,1,0:T(8,128)(2,1)}), bf16[8,128,512]{2,1,0:T(8,128)(2,1)S(1)}, u32[]{:S(2)}, u32[]{:S(2)}) async-start(bf16[8,128,512]{2,1,0:T(8,128)(2,1)} %broadcast_in_dim.7), calls=%async_computation.2 | async-start | bytes 2097152 | tf_op jit(solution)/shard_map/all_to_all | solution.py:81
  92.0 0.1 fusion.12
  92.1 9.2 %collective-permute-start.5 = (bf16[128,256]{1,0:T(8,128)(2,1)S(1)}, bf16[128,256]{1,0:T(8,128)(2,1)S(1)}, u32[]{:S(2)}, u32[]{:S(2)}) collective-permute-start(bf16[128,256]{1,0:T(8,128)(2,1)S(1)} %slice.110), channel_id=1, source_target_pairs={{0,1},{1,0},{2,3},{3,2},{4,5},{5,4},{6,7},{7,6},{8,9},{9,8},{10,11... | collective-permute-start | bytes 196616 | tf_op jit(solution)/shard_map/ppermute | solution.py:143
  101.3 0.9 collective-permute-done.5
  102.2 8.8 %all-to-all-done.2 = bf16[8,128,512]{2,1,0:T(8,128)(2,1)S(1)} async-done(((bf16[8,128,512]{2,1,0:T(8,128)(2,1)}), bf16[8,128,512]{2,1,0:T(8,128)(2,1)S(1)}, u32[]{:S(2)}, u32[]{:S(2)}) %all-to-all-start.2) | async-done | bytes 1048608 | tf_op jit(solution)/shard_map/all_to_all | solution.py:81
  111.0 0.4 fusion
  111.4 0.4 fusion.1
  111.8 0.1 pad_maximum_fusion
  111.9 2.9 %collective-permute-start.6 = (bf16[2,1024,128]{2,1,0:T(8,128)(2,1)S(1)}, bf16[2,1024,128]{2,1,0:T(8,128)(2,1)S(1)}, u32[]{:S(2)}, u32[]{:S(2)}) collective-permute-start(bf16[2,1024,128]{2,1,0:T(8,128)(2,1)S(1)} %pad_maximum_fusion), channel_id=1, source_target_pairs={{0,1},{1,0},{2,3},{3,2},{4,5},{5,4},{6,7},{7,6},{8,9},{9,8},{10,11... | collective-permute-start | bytes 1572872 | tf_op jit(solution)/shard_map/ppermute | solution.py:158
  114.8 0.4 fusion.2
  115.3 0.7 fusion.4
  116.0 0.1 fusion.25
  116.1 0.4 fusion.3
  116.5 0.1 slice_select_fusion.1
  116.7 0.0 collective-permute-done.6
  116.7 0.9 maximum_select_fusion
  117.6 8.3 %all-to-all-start.3 = ((bf16[16,128,128]{2,1,0:T(8,128)(2,1)}), bf16[16,128,128]{2,1,0:T(8,128)(2,1)S(1)}, u32[]{:S(2)}, u32[]{:S(2)}) async-start(bf16[16,128,128]{2,1,0:T(8,128)(2,1)} %bitcast.13), calls=%async_computation.3 | async-start | bytes 1048576 | tf_op jit(solution)/shard_map/all_to_all | solution.py:81
  125.9 1.9 %collective-permute-start.9 = (f32[256,256]{1,0:T(8,128)S(1)}, f32[256,256]{1,0:T(8,128)S(1)}, u32[]{:S(2)}, u32[]{:S(2)}) collective-permute-start(f32[256,256]{1,0:T(8,128)S(1)} %slice_bitcast_fusion), channel_id=1, source_target_pairs={{0,1},{1,0},{2,3},{3,2},{4,5},{5,4},{6,7},{7,6},{8,9},{9,8},{10,11... | collective-permute-start | bytes 786440 | tf_op jit(solution)/shard_map/ppermute | solution.py:165
  127.8 2.1 %collective-permute-start.10 = (bf16[256,256]{1,0:T(8,128)(2,1)S(1)}, bf16[256,256]{1,0:T(8,128)(2,1)S(1)}, u32[]{:S(2)}, u32[]{:S(2)}) collective-permute-start(bf16[256,256]{1,0:T(8,128)(2,1)S(1)} %fusion.18), channel_id=1, source_target_pairs={{32,1},{34,3},{36,5},{38,7},{40,9},{42,11},{44,13},{46,15},{48,17}... | collective-permute-start | bytes 393224 | tf_op jit(solution)/shard_map/ppermute | solution.py:169
  129.9 5.3 %collective-permute-start.8 = (bf16[256,256]{1,0:T(8,128)(2,1)S(1)}, bf16[256,256]{1,0:T(8,128)(2,1)S(1)}, u32[]{:S(2)}, u32[]{:S(2)}) collective-permute-start(bf16[256,256]{1,0:T(8,128)(2,1)S(1)} %fusion.17), channel_id=1, source_target_pairs={{0,32},{2,34},{4,36},{6,38},{8,40},{10,42},{12,44},{14,46},{16,48}... | collective-permute-start | bytes 393224 | tf_op jit(solution)/shard_map/ppermute | solution.py:168
  135.3 0.6 slice_select_fusion.2
  135.9 0.3 collective-permute-done.10
  136.3 5.3 %collective-permute-done.8 = bf16[256,256]{1,0:T(8,128)(2,1)S(1)} collective-permute-done((bf16[256,256]{1,0:T(8,128)(2,1)S(1)}, bf16[256,256]{1,0:T(8,128)(2,1)S(1)}, u32[]{:S(2)}, u32[]{:S(2)}) %collective-permute-start.8) | collective-permute-done | bytes 131104 | tf_op jit(solution)/shard_map/ppermute | solution.py:168
  141.6 0.0 collective-permute-done.9
  141.6 0.7 broadcast_select_fusion
  142.3 0.0 all-to-all-done.3
  142.3 0.1 reduce_sum.22
  142.4 3.0 %collective-permute-start.7 = (bf16[128,128]{1,0:T(8,128)(2,1)S(1)}, bf16[128,128]{1,0:T(8,128)(2,1)S(1)}, u32[]{:S(2)}, u32[]{:S(2)}) collective-permute-start(bf16[128,128]{1,0:T(8,128)(2,1)S(1)} %reduce_sum.22), channel_id=1, source_target_pairs={{0,0},{1,1},{2,2},{3,3},{4,4},{5,5},{6,6},{7,7},{8,8},{9,9},{10,10... | collective-permute-start | bytes 98312 | tf_op jit(solution)/shard_map/ppermute | solution.py:167
  145.4 0.8 copy.21
  146.1 2.1 %collective-permute-done.7 = bf16[128,128]{1,0:T(8,128)(2,1)S(1)} collective-permute-done((bf16[128,128]{1,0:T(8,128)(2,1)S(1)}, bf16[128,128]{1,0:T(8,128)(2,1)S(1)}, u32[]{:S(2)}, u32[]{:S(2)}) %collective-permute-start.7) | collective-permute-done | bytes 32800 | tf_op jit(solution)/shard_map/ppermute | solution.py:167
  148.2 0.6 copy.30
  (10 shorter events, 0.1 us)
Async XLA Ops:
  2.5 3.3 %collective-permute-start = (bf16[640,128]{1,0:T(8,128)(2,1)S(1)}, bf16[640,128]{1,0:T(8,128)(2,1)S(1)}, u32[]{:S(2)}, u32[]{:S(2)}) collective-permute-start(bf16[640,128]{1,0:T(8,128)(2,1)S(1)} %maximum_select_fusion.2), channel_id=1, source_target_pairs={{0,1},{1,0},{2,3},{3,2},{4,5},{5,4},{6,7},{7,6},{8,9},{9,8},{10,11... | collective-permute-start | bytes 491528 | tf_op jit(solution)/shard_map/ppermute | solution.py:116
  5.8 9.8 %collective-permute-start.1 = (bf16[128,256]{1,0:T(8,128)(2,1)S(1)}, bf16[128,256]{1,0:T(8,128)(2,1)S(1)}, u32[]{:S(2)}, u32[]{:S(2)}) collective-permute-start(bf16[128,256]{1,0:T(8,128)(2,1)S(1)} %pad_maximum_fusion.2), channel_id=1, source_target_pairs={{0,8},{1,1},{2,26},{3,3},{4,74},{5,5},{6,92},{7,7},{8,140},{9,9},{... | collective-permute-start | bytes 196616 | tf_op jit(solution)/shard_map/ppermute | solution.py:117
  16.7 16.8 %copy-start = (bf16[256,256]{1,0:T(8,128)(2,1)S(1)}, bf16[256,256]{1,0:T(8,128)(2,1)}, u32[]{:S(2)}) copy-start(bf16[256,256]{1,0:T(8,128)(2,1)} %param.7) | copy-start | bytes 393220
  16.7 30.3 %all-to-all-start = ((bf16[16,128,256]{2,1,0:T(8,128)(2,1)}), bf16[16,128,256]{2,1,0:T(8,128)(2,1)S(1)}, u32[]{:S(2)}, u32[]{:S(2)}) async-start(bf16[16,128,256]{2,1,0:T(8,128)(2,1)} %broadcast_in_dim.6), calls=%async_computation | async-start | bytes 2097152 | tf_op jit(solution)/shard_map/all_to_all | solution.py:81
  33.5 0.9 copy-start.1
  33.5 3.3 %copy-start.2 = (bf16[128,256]{1,0:T(8,128)(2,1)S(1)}, bf16[128,256]{1,0:T(8,128)(2,1)}, u32[]{:S(2)}) copy-start(bf16[128,256]{1,0:T(8,128)(2,1)} %param.6) | copy-start | bytes 196612
  34.5 12.6 %collective-permute-start.3 = (bf16[256,512]{0,1:T(8,128)(2,1)S(1)}, bf16[256,512]{0,1:T(8,128)(2,1)S(1)}, u32[]{:S(2)}, u32[]{:S(2)}) collective-permute-start(bf16[256,512]{0,1:T(8,128)(2,1)S(1)} %maximum_select_fusion.1), channel_id=1, source_target_pairs={{0,32},{2,34},{4,36},{6,38},{8,40},{10,42},{12,44},{14,46},{16,48}... | collective-permute-start | bytes 786440 | tf_op jit(solution)/shard_map/ppermute | solution.py:128
  36.8 3.1 %collective-permute-start.2 = (bf16[128,256]{1,0:T(8,128)(2,1)S(1)}, bf16[128,256]{1,0:T(8,128)(2,1)S(1)}, u32[]{:S(2)}, u32[]{:S(2)}) collective-permute-start(bf16[128,256]{1,0:T(8,128)(2,1)S(1)} %copy-done.2), channel_id=1, source_target_pairs={{0,1},{1,0},{2,3},{3,2},{4,5},{5,4},{6,7},{7,6},{8,9},{9,8},{10,11... | collective-permute-start | bytes 196616 | tf_op jit(solution)/shard_map/ppermute | solution.py:125
  75.8 11.2 %collective-permute-start.4 = (bf16[128,512]{1,0:T(8,128)(2,1)S(1)}, bf16[128,512]{1,0:T(8,128)(2,1)S(1)}, u32[]{:S(2)}, u32[]{:S(2)}) collective-permute-start(bf16[128,512]{1,0:T(8,128)(2,1)S(1)} %fusion.19), channel_id=1, source_target_pairs={{1,256},{256,1},{3,320},{320,3},{5,384},{384,5},{7,448},{448,7},{9... | collective-permute-start | bytes 393224 | tf_op jit(solution)/shard_map/ppermute | solution.py:138
  88.2 22.7 %all-to-all-start.2 = ((bf16[8,128,512]{2,1,0:T(8,128)(2,1)}), bf16[8,128,512]{2,1,0:T(8,128)(2,1)S(1)}, u32[]{:S(2)}, u32[]{:S(2)}) async-start(bf16[8,128,512]{2,1,0:T(8,128)(2,1)} %broadcast_in_dim.7), calls=%async_computation.2 | async-start | bytes 2097152 | tf_op jit(solution)/shard_map/all_to_all | solution.py:81
  92.1 10.1 %collective-permute-start.5 = (bf16[128,256]{1,0:T(8,128)(2,1)S(1)}, bf16[128,256]{1,0:T(8,128)(2,1)S(1)}, u32[]{:S(2)}, u32[]{:S(2)}) collective-permute-start(bf16[128,256]{1,0:T(8,128)(2,1)S(1)} %slice.110), channel_id=1, source_target_pairs={{0,1},{1,0},{2,3},{3,2},{4,5},{5,4},{6,7},{7,6},{8,9},{9,8},{10,11... | collective-permute-start | bytes 196616 | tf_op jit(solution)/shard_map/ppermute | solution.py:143
  111.9 4.8 %collective-permute-start.6 = (bf16[2,1024,128]{2,1,0:T(8,128)(2,1)S(1)}, bf16[2,1024,128]{2,1,0:T(8,128)(2,1)S(1)}, u32[]{:S(2)}, u32[]{:S(2)}) collective-permute-start(bf16[2,1024,128]{2,1,0:T(8,128)(2,1)S(1)} %pad_maximum_fusion), channel_id=1, source_target_pairs={{0,1},{1,0},{2,3},{3,2},{4,5},{5,4},{6,7},{7,6},{8,9},{9,8},{10,11... | collective-permute-start | bytes 1572872 | tf_op jit(solution)/shard_map/ppermute | solution.py:158
  117.6 24.7 %all-to-all-start.3 = ((bf16[16,128,128]{2,1,0:T(8,128)(2,1)}), bf16[16,128,128]{2,1,0:T(8,128)(2,1)S(1)}, u32[]{:S(2)}, u32[]{:S(2)}) async-start(bf16[16,128,128]{2,1,0:T(8,128)(2,1)} %bitcast.13), calls=%async_computation.3 | async-start | bytes 1048576 | tf_op jit(solution)/shard_map/all_to_all | solution.py:81
  125.9 15.7 %collective-permute-start.9 = (f32[256,256]{1,0:T(8,128)S(1)}, f32[256,256]{1,0:T(8,128)S(1)}, u32[]{:S(2)}, u32[]{:S(2)}) collective-permute-start(f32[256,256]{1,0:T(8,128)S(1)} %slice_bitcast_fusion), channel_id=1, source_target_pairs={{0,1},{1,0},{2,3},{3,2},{4,5},{5,4},{6,7},{7,6},{8,9},{9,8},{10,11... | collective-permute-start | bytes 786440 | tf_op jit(solution)/shard_map/ppermute | solution.py:165
  127.8 8.5 %collective-permute-start.10 = (bf16[256,256]{1,0:T(8,128)(2,1)S(1)}, bf16[256,256]{1,0:T(8,128)(2,1)S(1)}, u32[]{:S(2)}, u32[]{:S(2)}) collective-permute-start(bf16[256,256]{1,0:T(8,128)(2,1)S(1)} %fusion.18), channel_id=1, source_target_pairs={{32,1},{34,3},{36,5},{38,7},{40,9},{42,11},{44,13},{46,15},{48,17}... | collective-permute-start | bytes 393224 | tf_op jit(solution)/shard_map/ppermute | solution.py:169
  129.9 11.6 %collective-permute-start.8 = (bf16[256,256]{1,0:T(8,128)(2,1)S(1)}, bf16[256,256]{1,0:T(8,128)(2,1)S(1)}, u32[]{:S(2)}, u32[]{:S(2)}) collective-permute-start(bf16[256,256]{1,0:T(8,128)(2,1)S(1)} %fusion.17), channel_id=1, source_target_pairs={{0,32},{2,34},{4,36},{6,38},{8,40},{10,42},{12,44},{14,46},{16,48}... | collective-permute-start | bytes 393224 | tf_op jit(solution)/shard_map/ppermute | solution.py:168
  142.4 5.8 %collective-permute-start.7 = (bf16[128,128]{1,0:T(8,128)(2,1)S(1)}, bf16[128,128]{1,0:T(8,128)(2,1)S(1)}, u32[]{:S(2)}, u32[]{:S(2)}) collective-permute-start(bf16[128,128]{1,0:T(8,128)(2,1)S(1)} %reduce_sum.22), channel_id=1, source_target_pairs={{0,0},{1,1},{2,2},{3,3},{4,4},{5,5},{6,6},{7,7},{8,8},{9,9},{10,10... | collective-permute-start | bytes 98312 | tf_op jit(solution)/shard_map/ppermute | solution.py:167
